TPU v7x, 32 devices: a whole 2x2x4 slice. The times are simulated.
32 devices in a mesh: cell: 8 (over z, x), net: 4 (over y, core).
Axes of the slice: x: 2, y: 2, z: 4, core: 2. Of those that a mesh axis runs over, the one named last changes fastest.
Arguments:
- cell_feat: bfloat16 [4096, 256], P('cell'), may hold values from -6 to 6
- out_grad: bfloat16 [4096, 256], P('cell'), may hold values from -6 to 6
- w_in: bfloat16 [256, 1024], replicated, may hold values from -0.25 to 0.25
- w_net: bfloat16 [256, 1024], replicated, may hold values from -0.25 to 0.25
- bias: float32 [1024], replicated, may hold values from -3 to 3
- w_out: bfloat16 [1024, 256], replicated, may hold values from -0.1875 to 0.1875
- send_idx: int32 [8, 8, 16], P('cell'), may hold values from 0 to 511
- pin_net: int32 [8, 4, 2, 512], P('cell', 'net'), may hold values from 0 to 127
- pin_ref: int32 [8, 4, 2, 512], P('cell', 'net'), may hold values from 0 to 639
- block_count: int32 [8, 4], P('cell', 'net'), may hold values from 1 to 2, as said below
Outputs:
- updated: bfloat16 [4096, 256], P(('cell', 'net'))
- cell_grad: bfloat16 [4096, 256], P(('cell', 'net'))
- grad_in: float32 [256, 1024], replicated
- grad_net: float32 [256, 1024], replicated
- grad_bias: float32 [1024], replicated
- grad_out: float32 [1024, 256], replicated
Inputs may be any that keep to these rules, and one draw needn't show every extreme that they name: `block_count`: in each partition exactly one device of the net axis holds 2 live blocks; the others hold exactly 1.
All inputs are finite; a program needn't handle non-finite values.
Results may differ from a plain program's by a relative error of at most 0.0034.
Values may be sent and summed in bfloat16 or wider, within the bound.
No kernel may reach another device: no remote copies, remote signals or barrier semaphores. Data moves between devices by JAX's collectives and lax.ppermute only.
A program may use at most 64 MiB of HBM per device.

v0:
```python
import jax
import jax.numpy as jnp
from jax import lax
from jax.sharding import PartitionSpec as P

NETS_BLK = 128


def block_pass(table_x, table_g, net_ids, refs, w_in, w_net, bias, w_out):
    pin_feat = table_x[refs]
    pin_grad = table_g[refs]
    onehot = (net_ids[:, None] == jnp.arange(NETS_BLK, dtype=jnp.int32)[None, :]).astype(
        jnp.bfloat16
    )
    counts = jnp.sum(onehot.astype(jnp.float32), axis=0)
    inverse = 1.0 / jnp.maximum(counts, 1.0)
    net_sum = lax.dot_general(
        onehot, pin_feat, (((0,), (0,)), ((), ())), preferred_element_type=jnp.float32
    )
    net_feat = (net_sum * inverse[:, None]).astype(jnp.bfloat16)
    net_pre = jnp.dot(net_feat, w_net, preferred_element_type=jnp.float32).astype(jnp.bfloat16)
    pre_act = (
        jnp.dot(pin_feat, w_in, preferred_element_type=jnp.float32)
        + jnp.dot(onehot, net_pre, preferred_element_type=jnp.float32)
        + bias
    )
    hidden_full, gelu_back = jax.vjp(jax.nn.gelu, pre_act)
    hidden = hidden_full.astype(jnp.bfloat16)
    message = jnp.dot(hidden, w_out, preferred_element_type=jnp.float32)
    pulled = lax.dot_general(
        pin_grad, w_out, (((1,), (1,)), ((), ())), preferred_element_type=jnp.float32
    )
    pre_grad = gelu_back(pulled)[0].astype(jnp.bfloat16)
    grad_out = lax.dot_general(
        hidden, pin_grad, (((0,), (0,)), ((), ())), preferred_element_type=jnp.float32
    )
    grad_in = lax.dot_general(
        pin_feat, pre_grad, (((0,), (0,)), ((), ())), preferred_element_type=jnp.float32
    )
    grad_bias = jnp.sum(pre_grad.astype(jnp.float32), axis=0)
    net_grad = lax.dot_general(
        onehot, pre_grad, (((0,), (0,)), ((), ())), preferred_element_type=jnp.float32
    ).astype(jnp.bfloat16)
    grad_net = lax.dot_general(
        net_feat, net_grad, (((0,), (0,)), ((), ())), preferred_element_type=jnp.float32
    )
    feat_grad = (
        lax.dot_general(
            net_grad, w_net, (((1,), (1,)), ((), ())), preferred_element_type=jnp.float32
        )
        * inverse[:, None]
    ).astype(jnp.bfloat16)
    pin_back = lax.dot_general(
        pre_grad, w_in, (((1,), (1,)), ((), ())), preferred_element_type=jnp.float32
    ) + jnp.dot(onehot, feat_grad, preferred_element_type=jnp.float32)
    return (message, pin_back, (grad_in, grad_net, grad_bias, grad_out))


def local(cell_feat, out_grad, w_in, w_net, bias, w_out, send_idx, pin_net, pin_ref, block_count):
    part_count = lax.axis_size("cell")
    group_size = lax.axis_size("net")
    net_rank = lax.axis_index("net")
    local_rows = cell_feat.shape[0]
    feat_dim = cell_feat.shape[1]
    hidden_dim = w_in.shape[1]
    slot_count = send_idx.shape[2]
    chosen = send_idx[0]
    incoming_x, incoming_g = (
        lax.all_to_all(cell_feat[chosen], "cell", split_axis=0, concat_axis=0, tiled=True),
        lax.all_to_all(out_grad[chosen], "cell", split_axis=0, concat_axis=0, tiled=True),
    )
    table_x = jnp.concatenate([cell_feat, incoming_x.reshape(-1, feat_dim)], axis=0)
    table_g = jnp.concatenate([out_grad, incoming_g.reshape(-1, feat_dim)], axis=0)
    table_len = table_x.shape[0]
    grads_zero = (
        jnp.zeros((feat_dim, hidden_dim), jnp.float32),
        jnp.zeros((feat_dim, hidden_dim), jnp.float32),
        jnp.zeros((hidden_dim,), jnp.float32),
        jnp.zeros((hidden_dim, feat_dim), jnp.float32),
    )
    initial = (
        jnp.zeros((table_len, feat_dim), jnp.float32),
        jnp.zeros((table_len, feat_dim), jnp.float32),
        grads_zero,
    )

    def accumulate(running, net_ids, refs):
        acc_y, acc_x, gradients = running
        message, pin_back, terms = block_pass(
            table_x, table_g, net_ids, refs, w_in, w_net, bias, w_out
        )
        return (
            acc_y.at[refs].add(message),
            acc_x.at[refs].add(pin_back),
            jax.tree.map(jnp.add, gradients, terms),
        )

    def own_block(block_no, running):
        return accumulate(running, pin_net[0, 0, block_no], pin_ref[0, 0, block_no])

    acc_y, acc_x, gradients = lax.fori_loop(0, block_count[0, 0], own_block, initial)
    own_y = acc_y[:local_rows]
    own_x = acc_x[:local_rows]
    halo_y = acc_y[local_rows:].reshape(part_count, slot_count, feat_dim)
    halo_x = acc_x[local_rows:].reshape(part_count, slot_count, feat_dim)
    back_y, back_x = (
        lax.all_to_all(halo_y, "cell", split_axis=0, concat_axis=0, tiled=True),
        lax.all_to_all(halo_x, "cell", split_axis=0, concat_axis=0, tiled=True),
    )
    flat_targets = chosen.reshape(-1)
    own_y = own_y.at[flat_targets].add(back_y.reshape(-1, feat_dim))
    own_x = own_x.at[flat_targets].add(back_x.reshape(-1, feat_dim))
    summed_y, summed_x = (
        lax.psum_scatter(own_y, "net", scatter_dimension=0, tiled=True),
        lax.psum_scatter(own_x, "net", scatter_dimension=0, tiled=True),
    )
    share_rows = local_rows // group_size
    base_feat = lax.dynamic_slice_in_dim(cell_feat, net_rank * share_rows, share_rows, 0)
    base_grad = lax.dynamic_slice_in_dim(out_grad, net_rank * share_rows, share_rows, 0)
    updated = (base_feat.astype(jnp.float32) + summed_y).astype(jnp.bfloat16)
    cell_grad = (base_grad.astype(jnp.float32) + summed_x).astype(jnp.bfloat16)
    grad_in, grad_net, grad_bias, grad_out = lax.psum(
        (gradients[0], gradients[1], gradients[2], gradients[3]), ("cell", "net")
    )
    return (updated, cell_grad, grad_in, grad_net, grad_bias, grad_out)


def solution(mesh):
    placed = (
        P("cell", None),
        P("cell", None),
        P(),
        P(),
        P(),
        P(),
        P("cell", None, None),
        P("cell", "net", None, None),
        P("cell", "net", None, None),
        P("cell", "net"),
    )
    return jax.shard_map(
        local,
        mesh=mesh,
        in_specs=placed,
        out_specs=(P(("cell", "net"), None), P(("cell", "net"), None), P(), P(), P(), P()),
        check_vma=False,
    )
```

profile of v0, /device:TPU:0, one launch (start us, length us, event | category | flops | bytes accessed | tf_op | source)
XLA Modules:
  0.0 295.6 jit_solution(850603817054095432)
XLA Ops:
  8.0 0.7 compare_select_fusion.1
  8.8 2.4 gather_fusion.2
  11.2 7.3 %all-to-all-start = ((bf16[8,16,256]{2,1,0:T(8,128)(2,1)}), bf16[8,16,256]{2,1,0:T(8,128)(2,1)S(1)}, u32[]{:S(2)}, u32[]{:S(2)}) async-start(bf16[8,16,256]{2,1,0:T(8,128)(2,1)} %bitcast.5), calls=%async_computation | async-start | bytes 131072 | tf_op jit(solution)/shard_map/all_to_all | solution.py:69
  18.5 2.4 gather_fusion.3
  20.8 4.5 %all-to-all-done = bf16[8,16,256]{2,1,0:T(8,128)(2,1)S(1)} async-done(((bf16[8,16,256]{2,1,0:T(8,128)(2,1)}), bf16[8,16,256]{2,1,0:T(8,128)(2,1)S(1)}, u32[]{:S(2)}, u32[]{:S(2)}) %all-to-all-start) | async-done | bytes 65568 | tf_op jit(solution)/shard_map/all_to_all | solution.py:69
  25.4 3.4 %all-to-all-start.1 = ((bf16[8,16,256]{2,1,0:T(8,128)(2,1)}), bf16[8,16,256]{2,1,0:T(8,128)(2,1)S(1)}, u32[]{:S(2)}, u32[]{:S(2)}) async-start(bf16[8,16,256]{2,1,0:T(8,128)(2,1)} %bitcast.7), calls=%async_computation.1 | async-start | bytes 131072 | tf_op jit(solution)/shard_map/all_to_all | solution.py:70
  28.7 1.0 pad_maximum_fusion
  29.7 5.9 %all-to-all-done.1 = bf16[8,16,256]{2,1,0:T(8,128)(2,1)S(1)} async-done(((bf16[8,16,256]{2,1,0:T(8,128)(2,1)}), bf16[8,16,256]{2,1,0:T(8,128)(2,1)S(1)}, u32[]{:S(2)}, u32[]{:S(2)}) %all-to-all-start.1) | async-done | bytes 65568 | tf_op jit(solution)/shard_map/all_to_all | solution.py:70
  35.7 1.1 broadcast.125.clone
  36.8 1.0 broadcast_in_dim.5
  37.9 1.1 broadcast.125
  39.0 75.5 %while.22 = (s32[]{:T(128)}, f32[640,256]{1,0:T(8,128)S(1)}, f32[640,256]{1,0:T(8,128)S(1)}, f32[256,1024]{1,0:T(8,128)}, f32[256,1024]{1,0:T(8,128)}, /*index=5...) while((s32[]{:T(128)}, f32[640,256]{1,0:T(8,128)S(1)}, ...), condition=%wide.region_5.0_spmd, body=%wide.region_0.0_spmd.sunk | while | flops 2171603456 | bytes 61596680 | solution.py:101
  39.6 0.7 constant_dynamic-slice_fusion.2
  40.5 0.7 compare_select_fusion.4
  41.2 2.0 gather_fusion
  43.6 2.6 gather_fusion.1
  46.1 2.0 fusion.78
  48.1 2.1 add_add_fusion.2
  50.2 1.3 copy-done
  51.5 0.8 fusion.79
  52.4 3.6 %scatter_fusion = f32[640,256]{1,0:T(8,128)S(1)} fusion(f32[640,256]{1,0:T(8,128)S(1)} %get-tuple-element.376, s32[512]{0:T(512)S(1)} %bitcast.85, f32[512,256]{1,0:T(8,128)S(1)} %fusion.79), kind=kCustom, calls=%fused_computation.4.clone.1 | custom fusion | flops 131072 | bytes 1574912 | tf_op jit(solution)/shard_map/while/body/scatter-add | solution.py:93
  56.0 3.8 %convolution_add_fusion.11 = f32[1024,256]{1,0:T(8,128)} fusion(f32[1024,256]{1,0:T(8,128)} %get-tuple-element.381, bf16[512,256]{1,0:T(8,128)(2,1)S(1)} %copy-done.10, f32[512,1024]{1,0:T(8,128)} %copy-done), kind=kOutput, calls=%fused_computation.20.clone.1 | convolution fusion | flops 273416192 | bytes 4456448 | tf_op jit(solution)/shard_map/while/body/dot_general | solution.py:34
  59.8 1.7 convert_reduce_fusion.5
  61.5 0.5 convolution_convert_fusion.3
  62.0 2.5 fusion.80
  64.5 2.5 convolution_add_fusion.8
  67.0 2.7 convolution_add_fusion.9
  69.6 4.1 %scatter_fusion.1 = f32[640,256]{1,0:T(8,128)S(1)} fusion(f32[640,256]{1,0:T(8,128)S(1)} %get-tuple-element.377, s32[512]{0:T(512)S(1)} %bitcast.86, f32[512,256]{1,0:T(8,128)} %convolution_add_fusion.8), kind=kCustom, calls=%fused_computation.5.clone.1 | custom fusion | flops 131072 | bytes 1574912 | tf_op jit(solution)/shard_map/while/body/scatter-add | solution.py:94
  73.7 2.6 convolution_add_fusion.10
  77.0 0.7 constant_dynamic-slice_fusion.2
  77.9 0.7 compare_select_fusion.4
  78.6 2.0 gather_fusion
  80.9 2.6 gather_fusion.1
  83.5 1.9 fusion.78
  85.4 2.1 add_add_fusion.2
  87.5 1.3 copy-done
  88.9 0.8 fusion.79
  89.7 3.6 %scatter_fusion = f32[640,256]{1,0:T(8,128)S(1)} fusion(f32[640,256]{1,0:T(8,128)S(1)} %get-tuple-element.376, s32[512]{0:T(512)S(1)} %bitcast.85, f32[512,256]{1,0:T(8,128)S(1)} %fusion.79), kind=kCustom, calls=%fused_computation.4.clone.1 | custom fusion | flops 131072 | bytes 1574912 | tf_op jit(solution)/shard_map/while/body/scatter-add | solution.py:93
  93.3 3.8 %convolution_add_fusion.11 = f32[1024,256]{1,0:T(8,128)} fusion(f32[1024,256]{1,0:T(8,128)} %get-tuple-element.381, bf16[512,256]{1,0:T(8,128)(2,1)S(1)} %copy-done.10, f32[512,1024]{1,0:T(8,128)} %copy-done), kind=kOutput, calls=%fused_computation.20.clone.1 | convolution fusion | flops 273416192 | bytes 4456448 | tf_op jit(solution)/shard_map/while/body/dot_general | solution.py:34
  97.2 1.7 convert_reduce_fusion.5
  99.4 2.5 fusion.80
  101.8 2.5 convolution_add_fusion.8
  104.3 2.7 convolution_add_fusion.9
  106.9 4.1 %scatter_fusion.1 = f32[640,256]{1,0:T(8,128)S(1)} fusion(f32[640,256]{1,0:T(8,128)S(1)} %get-tuple-element.377, s32[512]{0:T(512)S(1)} %bitcast.86, f32[512,256]{1,0:T(8,128)} %convolution_add_fusion.8), kind=kCustom, calls=%fused_computation.5.clone.1 | custom fusion | flops 131072 | bytes 1574912 | tf_op jit(solution)/shard_map/while/body/scatter-add | solution.py:94
  111.1 2.6 convolution_add_fusion.10
  114.5 0.7 slice.13
  115.2 3.4 %all-to-all-start.2 = ((f32[8,16,256]{2,1,0:T(8,128)}), f32[8,16,256]{2,1,0:T(8,128)S(1)}, u32[]{:S(2)}, u32[]{:S(2)}) async-start(f32[8,16,256]{2,1,0:T(8,128)} %bitcast.10), calls=%async_computation.2 | async-start | bytes 262144 | tf_op jit(solution)/shard_map/all_to_all | solution.py:107
  118.6 0.8 reshape_squeeze.3
  119.4 6.4 %all-to-all-done.2 = f32[8,16,256]{2,1,0:T(8,128)S(1)} async-done(((f32[8,16,256]{2,1,0:T(8,128)}), f32[8,16,256]{2,1,0:T(8,128)S(1)}, u32[]{:S(2)}, u32[]{:S(2)}) %all-to-all-start.2) | async-done | bytes 131104 | tf_op jit(solution)/shard_map/all_to_all | solution.py:107
  125.8 1.5 scatter_fusion.2
  127.3 0.8 copy-done.7
  128.1 0.7 slice.15
  128.8 3.4 %all-to-all-start.3 = ((f32[8,16,256]{2,1,0:T(8,128)}), f32[8,16,256]{2,1,0:T(8,128)S(1)}, u32[]{:S(2)}, u32[]{:S(2)}) async-start(f32[8,16,256]{2,1,0:T(8,128)} %bitcast.12), calls=%async_computation.4 | async-start | bytes 262144 | tf_op jit(solution)/shard_map/all_to_all | solution.py:108
  132.2 7.2 %all-to-all-done.3 = f32[8,16,256]{2,1,0:T(8,128)S(1)} async-done(((f32[8,16,256]{2,1,0:T(8,128)}), f32[8,16,256]{2,1,0:T(8,128)S(1)}, u32[]{:S(2)}, u32[]{:S(2)}) %all-to-all-start.3) | async-done | bytes 131104 | tf_op jit(solution)/shard_map/all_to_all | solution.py:108
  139.4 1.5 scatter_fusion.3
  140.9 0.8 copy-done.6
  141.8 0.5 all-reduce.3.cloned.1.call-update
  142.3 37.9 %psum.30 = f32[1024]{0:T(1024)} all-reduce(f32[1024]{0:T(1024)S(1)} %get-tuple-element.452), channel_id=1, replica_groups=mesh['cell'=8,'net'=4] {'cell','net'}, use_global_device_ids=true, to_apply=%region_12.0 | all-reduce | flops 1024 | bytes 8192 | tf_op jit(solution)/shard_map/psum | solution.py:122
  180.2 1.6 add_convert_fusion.1
  181.8 1.5 add_convert_fusion
  183.4 100.4 %all-reduce.3.cloned.1.call-done = (f32[256,1024]{1,0:T(8,128)}, f32[256,1024]{1,0:T(8,128)}, f32[1024,256]{1,0:T(8,128)}) async-done(((f32[256,1024]{1,0:T(8,128)}, f32[256,1024]{1,0:T(8,128)}, f32[1024,256]{1,0:T(8,128)}), (f32[256,1024]{1,0:T(8,128)}, f32[256,1024]{1,0:T(8,128)}, f32[1024,256]{1,0:T(8,128)})) %all-reduce.3.cloned.1.call-update) | async-done | bytes 3145744 | tf_op jit(solution)/shard_map/psum | solution.py:122
  283.8 2.5 copy.44
  286.2 1.0 copy.45
  287.2 1.0 copy.46
  (79 shorter events, 2.1 us)
Async XLA Ops:
  8.0 27.6 %copy-start.11 = (bf16[512,256]{1,0:T(8,128)(2,1)S(1)}, bf16[512,256]{1,0:T(8,128)(2,1)}, u32[]{:S(2)}) copy-start(bf16[512,256]{1,0:T(8,128)(2,1)} %param.13) | copy-start | bytes 786436
  11.2 14.2 %all-to-all-start = ((bf16[8,16,256]{2,1,0:T(8,128)(2,1)}), bf16[8,16,256]{2,1,0:T(8,128)(2,1)S(1)}, u32[]{:S(2)}, u32[]{:S(2)}) async-start(bf16[8,16,256]{2,1,0:T(8,128)(2,1)} %bitcast.5), calls=%async_computation | async-start | bytes 131072 | tf_op jit(solution)/shard_map/all_to_all | solution.py:69
  25.4 10.2 %all-to-all-start.1 = ((bf16[8,16,256]{2,1,0:T(8,128)(2,1)}), bf16[8,16,256]{2,1,0:T(8,128)(2,1)S(1)}, u32[]{:S(2)}, u32[]{:S(2)}) async-start(bf16[8,16,256]{2,1,0:T(8,128)(2,1)} %bitcast.7), calls=%async_computation.1 | async-start | bytes 131072 | tf_op jit(solution)/shard_map/all_to_all | solution.py:70
  35.6 3.4 %copy-start.2 = (bf16[256,1024]{1,0:T(8,128)(2,1)S(1)}, bf16[256,1024]{1,0:T(8,128)(2,1)}, u32[]{:S(2)}) copy-start(bf16[256,1024]{1,0:T(8,128)(2,1)} %param.15) | copy-start | bytes 1572868
  35.6 3.4 %copy-start.4 = (bf16[256,1024]{1,0:T(8,128)(2,1)S(1)}, bf16[256,1024]{1,0:T(8,128)(2,1)}, u32[]{:S(2)}) copy-start(bf16[256,1024]{1,0:T(8,128)(2,1)} %param.14) | copy-start | bytes 1572868
  35.6 3.3 %copy-start.14 = (f32[1024]{0:T(1024)S(1)}, f32[1024]{0:T(1024)}, u32[]{:S(2)}) copy-start(f32[1024]{0:T(1024)} %param.16) | copy-start | bytes 12292
  40.5 5.6 %copy-start.15 = (f32[128]{0:T(128)}, f32[128]{0:T(128)S(1)}, u32[]{:S(2)}) copy-start(f32[128]{0:T(128)S(1)} %maximum_divide_fusion.2) | copy-start | bytes 1540 | tf_op jit(solution)/shard_map/while
  43.6 4.5 %copy-start.8 = (bf16[128,256]{1,0:T(8,128)(2,1)}, bf16[128,256]{1,0:T(8,128)(2,1)S(1)}, u32[]{:S(2)}) copy-start(bf16[128,256]{1,0:T(8,128)(2,1)S(1)} %fusion.77) | copy-start | bytes 196612 | tf_op jit(solution)/shard_map/while
  48.1 3.4 %copy-start.16 = (bf16[1024,256]{1,0:T(8,128)(2,1)S(1)}, bf16[1024,256]{1,0:T(8,128)(2,1)}, u32[]{:S(2)}) copy-start(bf16[1024,256]{1,0:T(8,128)(2,1)} %get-tuple-element.408) | copy-start | bytes 1572868 | tf_op jit(solution)/shard_map/while
  50.2 1.3 copy-start
  52.3 3.6 %copy-start.10 = (bf16[512,256]{1,0:T(8,128)(2,1)S(1)}, bf16[512,256]{1,0:T(8,128)(2,1)}, u32[]{:S(2)}) copy-start(bf16[512,256]{1,0:T(8,128)(2,1)} %gather_fusion.1) | copy-start | bytes 786436 | tf_op jit(solution)/shard_map/while
  56.0 3.9 %copy-start.1 = (f32[512,1024]{1,0:T(8,128)S(1)}, f32[512,1024]{1,0:T(8,128)}, u32[]{:S(2)}) copy-start(f32[512,1024]{1,0:T(8,128)} %copy-done) | copy-start | bytes 6291460 | tf_op jit(solution)/shard_map/while
  56.0 3.9 %copy-start.17 = (bf16[1024,256]{1,0:T(8,128)(2,1)S(1)}, bf16[1024,256]{1,0:T(8,128)(2,1)}, u32[]{:S(2)}) copy-start(bf16[1024,256]{1,0:T(8,128)(2,1)} %get-tuple-element.408) | copy-start | bytes 1572868 | tf_op jit(solution)/shard_map/while
  69.6 4.1 %copy-start.9 = (bf16[128,256]{1,0:T(8,128)(2,1)S(1)}, bf16[128,256]{1,0:T(8,128)(2,1)}, u32[]{:S(2)}) copy-start(bf16[128,256]{1,0:T(8,128)(2,1)} %copy-done.8) | copy-start | bytes 196612 | tf_op jit(solution)/shard_map/while
  73.7 2.6 copy-start.3
  73.7 2.6 copy-start.5
  77.8 5.6 %copy-start.15 = (f32[128]{0:T(128)}, f32[128]{0:T(128)S(1)}, u32[]{:S(2)}) copy-start(f32[128]{0:T(128)S(1)} %maximum_divide_fusion.2) | copy-start | bytes 1540 | tf_op jit(solution)/shard_map/while
  80.9 4.5 %copy-start.8 = (bf16[128,256]{1,0:T(8,128)(2,1)}, bf16[128,256]{1,0:T(8,128)(2,1)S(1)}, u32[]{:S(2)}) copy-start(bf16[128,256]{1,0:T(8,128)(2,1)S(1)} %fusion.77) | copy-start | bytes 196612 | tf_op jit(solution)/shard_map/while
  85.4 3.4 %copy-start.16 = (bf16[1024,256]{1,0:T(8,128)(2,1)S(1)}, bf16[1024,256]{1,0:T(8,128)(2,1)}, u32[]{:S(2)}) copy-start(bf16[1024,256]{1,0:T(8,128)(2,1)} %get-tuple-element.408) | copy-start | bytes 1572868 | tf_op jit(solution)/shard_map/while
  87.5 1.3 copy-start
  89.7 3.6 %copy-start.10 = (bf16[512,256]{1,0:T(8,128)(2,1)S(1)}, bf16[512,256]{1,0:T(8,128)(2,1)}, u32[]{:S(2)}) copy-start(bf16[512,256]{1,0:T(8,128)(2,1)} %gather_fusion.1) | copy-start | bytes 786436 | tf_op jit(solution)/shard_map/while
  93.3 3.9 %copy-start.1 = (f32[512,1024]{1,0:T(8,128)S(1)}, f32[512,1024]{1,0:T(8,128)}, u32[]{:S(2)}) copy-start(f32[512,1024]{1,0:T(8,128)} %copy-done) | copy-start | bytes 6291460 | tf_op jit(solution)/shard_map/while
  93.3 3.9 %copy-start.17 = (bf16[1024,256]{1,0:T(8,128)(2,1)S(1)}, bf16[1024,256]{1,0:T(8,128)(2,1)}, u32[]{:S(2)}) copy-start(bf16[1024,256]{1,0:T(8,128)(2,1)} %get-tuple-element.408) | copy-start | bytes 1572868 | tf_op jit(solution)/shard_map/while
  106.9 4.1 %copy-start.9 = (bf16[128,256]{1,0:T(8,128)(2,1)S(1)}, bf16[128,256]{1,0:T(8,128)(2,1)}, u32[]{:S(2)}) copy-start(bf16[128,256]{1,0:T(8,128)(2,1)} %copy-done.8) | copy-start | bytes 196612 | tf_op jit(solution)/shard_map/while
  111.0 2.6 copy-start.3
  111.0 2.6 copy-start.5
  115.2 10.7 %all-to-all-start.2 = ((f32[8,16,256]{2,1,0:T(8,128)}), f32[8,16,256]{2,1,0:T(8,128)S(1)}, u32[]{:S(2)}, u32[]{:S(2)}) async-start(f32[8,16,256]{2,1,0:T(8,128)} %bitcast.10), calls=%async_computation.2 | async-start | bytes 262144 | tf_op jit(solution)/shard_map/all_to_all | solution.py:107
  118.5 61.7 %reduce-scatter.3.cloned.1.call-start = ((), (), s32[]{:S(2)}) async-start(), calls=%async_computation.6 | async-start | bytes 655360 | tf_op jit(solution)/shard_map/reduce_scatter | solution.py:114
  127.3 0.8 copy-start.7
  128.8 10.7 %all-to-all-start.3 = ((f32[8,16,256]{2,1,0:T(8,128)}), f32[8,16,256]{2,1,0:T(8,128)S(1)}, u32[]{:S(2)}, u32[]{:S(2)}) async-start(f32[8,16,256]{2,1,0:T(8,128)} %bitcast.12), calls=%async_computation.4 | async-start | bytes 262144 | tf_op jit(solution)/shard_map/all_to_all | solution.py:108
  132.2 49.7 %reduce-scatter.5.cloned.1.call-start = ((), (), s32[]{:S(2)}) async-start(), calls=%async_computation.7 | async-start | bytes 655360 | tf_op jit(solution)/shard_map/reduce_scatter | solution.py:115
  140.9 0.8 copy-start.6
  141.7 142.0 %all-reduce.3.cloned.1.call-start = ((), (), s32[]{:S(2)}) async-start(), calls=%async_computation.8 | async-start | bytes 6291456 | tf_op jit(solution)/shard_map/psum | solution.py:122
  283.8 2.5 copy-start.13
  283.8 3.4 %copy-start.12 = (f32[1024,256]{1,0:T(8,128)S(1)}, f32[1024,256]{1,0:T(8,128)}, u32[]{:S(2)}) copy-start(f32[1024,256]{1,0:T(8,128)} %get-tuple-element.418) | copy-start | bytes 3145732
Sparse Core Ops, SparseCore 0:
  128.2 18.4 reduce-scatter.2
  149.4 22.0 reduce-scatter.4
Sparse Core Ops, SparseCore 1:
  148.6 135.1 all-reduce.2
where the time goes:
time: 297 us; the launch traced here: 296 us
  waiting for transfers between devices  125 us (42%)
  matrix products  42.8 us (14%)
  blocking collectives  37.9 us (13%)
  local copies, waits for them, and re-layouts  29.5 us (10%)
  other arithmetic  24.8 us (8%)
  starting transfers between devices  17.5 us (6%)
  between operations  15.6 us (5%)
    psum x1, waiting for transfers between devices, local(): lax.psum((gradients[0], gradients[1], gradients[2], gradients[3]), ('cell...  100 us
    psum x1, blocking collectives, local(): lax.psum((gradients[0], gradients[1], gradients[2], gradients[3]), ('cell...  37.9 us
    scatter-add x2, other arithmetic, accumulate(): acc_x.at[refs].add(pin_back)  8.12 us
    dot_general x2, matrix products, block_pass(): lax.dot_general(hidden, pin_grad, (((0,), (0,)), ((), ())), preferred_ele...  7.7 us
    all_to_all x1, starting transfers between devices, local(): lax.all_to_all(cell_feat[chosen], 'cell', split_axis=0, concat_axis=0, ti...  7.25 us
    all_to_all x1, waiting for transfers between devices, local(): lax.all_to_all(halo_x, 'cell', split_axis=0, concat_axis=0, tiled=True)  7.19 us
    scatter-add x2, other arithmetic, accumulate(): acc_y.at[refs].add(message)  7.17 us
    all_to_all x1, waiting for transfers between devices, local(): lax.all_to_all(halo_y, 'cell', split_axis=0, concat_axis=0, tiled=True)  6.42 us
  transfers between devices with their start and end apart: 7, of which 5 were waited for; matrix products, arithmetic and copies ran while one was open for 3% of the time, Pallas kernels for 0%

commit v1 on v0

v1 whole, which is shorter than its diff:
```python
import functools

import jax
import jax.numpy as jnp
from jax import lax
from jax.experimental import pallas as pl
from jax.experimental.pallas import tpu as pltpu
from jax.sharding import PartitionSpec as P

NETS_BLK = 128
BF16 = jnp.bfloat16
F32 = jnp.float32
VMEM_LIMIT = 48 * 1024 * 1024


def dot_nn(a, b):
    return jnp.dot(a, b, preferred_element_type=F32)


def dot_nt(a, b):
    return lax.dot_general(a, b, (((1,), (1,)), ((), ())), preferred_element_type=F32)


def dot_tn(a, b):
    return lax.dot_general(a, b, (((0,), (0,)), ((), ())), preferred_element_type=F32)


def slot_onehot(idx, cells):
    parts, slots = idx.shape
    lanes = parts * slots
    lane = lax.broadcasted_iota(jnp.int32, (slots, lanes), 1)
    spread = ((lane & (slots - 1)) == lax.broadcasted_iota(jnp.int32, (slots, lanes), 0)).astype(BF16)
    high = dot_nn((idx >> 6).astype(F32).astype(BF16), spread)
    low = dot_nn((idx & 63).astype(F32).astype(BF16), spread)
    wide = high * 64.0 + low
    lane = lax.broadcasted_iota(jnp.int32, (parts, lanes), 1)
    mine = (lane // slots) == lax.broadcasted_iota(jnp.int32, (parts, lanes), 0)
    row = jnp.sum(jnp.where(mine, wide, 0.0), axis=0, keepdims=True).astype(jnp.int32)
    return (lax.broadcasted_iota(jnp.int32, (cells, lanes), 0) == row).astype(BF16)


def gather_kernel(count_ref, idx_ref, x_ref, g_ref, net_ref, ref_ref, out_ref, ints_ref):
    part_count, slots = idx_ref.shape[1:]
    cells, feat = x_ref.shape
    group = 128 // slots
    for first in range(0, part_count, group):
        onehot = slot_onehot(idx_ref[0, first : first + group], cells)
        rows = pl.ds(first * slots, 128)
        out_ref[rows, :feat] = dot_tn(onehot, x_ref[...]).astype(BF16)
        out_ref[rows, feat:] = dot_tn(onehot, g_ref[...]).astype(BF16)
    slot_max = net_ref.shape[2]
    ints_ref[...] = jnp.full(ints_ref.shape, count_ref[0, 0], jnp.int32)
    ints_ref[:slot_max, :] = net_ref[0, 0]
    ints_ref[slot_max : 2 * slot_max, :] = ref_ref[0, 0]


def layer_kernel(
    split, pos_ref, x_ref, g_ref, halo_ref, ints_ref, w_in_ref, w_net_ref, bias_ref, w_out_ref, own_ref, *rest
):
    (*outs, table, win_t, wnet_t, wout_t, bias_t, nets, refs, acc, acc_in, acc_net, acc_out, acc_bias) = rest
    cells, feat = x_ref.shape
    hid = w_in_ref.shape[1]
    group_size, _, pins = ints_ref.shape
    part_count, slots = halo_ref.shape[:2]
    table_len = acc.shape[0]

    extra_net = jnp.zeros((1, pins), jnp.int32)
    extra_ref = jnp.zeros((1, pins), jnp.int32)
    for src in range(group_size):
        nets[src : src + 1, :] = ints_ref[src, 0:1, :]
        refs[src : src + 1, :] = ints_ref[src, 2:3, :]
        second = ints_ref[src, 4:5, :] > 1
        extra_net += jnp.where(second, ints_ref[src, 1:2, :] + 1, 0)
        extra_ref += jnp.where(second, ints_ref[src, 3:4, :] + 1, 0)
    nets[group_size : group_size + 1, :] = extra_net - 1
    refs[group_size : group_size + 1, :] = extra_ref - 1

    table[:feat, :cells] = x_ref[...].T
    table[feat:, :cells] = g_ref[...].T
    halo = halo_ref[...].reshape(part_count * slots, 2 * feat)
    table[:feat, cells:] = halo[:, :feat].T
    table[feat:, cells:] = halo[:, feat:].T
    win_t[...] = w_in_ref[...].T
    wnet_t[...] = w_net_ref[...].T
    wout_t[...] = w_out_ref[...].T
    bias_t[...] = jnp.broadcast_to(bias_ref[...], (128, hid)).T
    acc[...] = jnp.zeros_like(acc)
    acc_in[...] = jnp.zeros_like(acc_in)
    acc_net[...] = jnp.zeros_like(acc_net)
    acc_out[...] = jnp.zeros_like(acc_out)
    acc_bias[...] = jnp.zeros_like(acc_bias)
    ones = jnp.ones((8, pins), BF16)

    def block(b, carry):
        in_net = lax.broadcasted_iota(jnp.int32, (NETS_BLK, pins), 0) == nets[pl.ds(b, 1), :]
        in_net = in_net.astype(BF16)
        at_row = lax.broadcasted_iota(jnp.int32, (table_len, pins), 0) == refs[pl.ds(b, 1), :]
        at_row = at_row.astype(BF16)
        inverse = 1.0 / jnp.maximum(dot_nt(ones, in_net)[0:1], 1.0)
        taken = dot_nn(table[...], at_row).astype(BF16)
        feat_t, grad_t = taken[:feat], taken[feat:]
        net_feat = (dot_nt(feat_t, in_net) * inverse).astype(BF16)
        net_pre = dot_nn(wnet_t[...], net_feat).astype(BF16)
        bias_col = jnp.concatenate([bias_t[...]] * (pins // 128), axis=1)
        pre = dot_nn(win_t[...], feat_t) + dot_nn(net_pre, in_net) + bias_col
        pulled = dot_nn(w_out_ref[...], grad_t)
        square = pre * pre
        scale = 0.7978845608028654
        bend = jnp.tanh(pre * (scale + (scale * 0.044715) * square))
        half = 0.5 * bend + 0.5
        hidden = (pre * half).astype(BF16)
        slope = half + (0.5 * pre) * (1.0 - bend * bend) * (scale + (3 * scale * 0.044715) * square)
        pre_grad = (pulled * slope).astype(BF16)
        acc_out[...] += dot_nt(hidden, grad_t)
        acc_in[...] += dot_nt(feat_t, pre_grad)
        acc_bias[...] += dot_nt(ones, pre_grad)
        net_grad = dot_nt(pre_grad, in_net).astype(BF16)
        acc_net[...] += dot_nt(net_feat, net_grad)
        feat_grad = (dot_nn(w_net_ref[...], net_grad) * inverse).astype(BF16)
        message = dot_nn(wout_t[...], hidden).astype(BF16)
        back = (dot_nn(w_in_ref[...], pre_grad) + dot_nn(feat_grad, in_net)).astype(BF16)
        acc[...] += dot_nt(at_row, jnp.concatenate([message, back], axis=0))
        return carry

    lax.fori_loop(0, group_size + 1, block, 0)

    own_ref[...] = acc[:cells, :]
    if split:
        (send_ref,) = outs
        base = 3 * (feat // part_count)
    else:
        send_ref, grads_ref = outs
        base = 0
        grads_ref[:feat, :] = acc_in[...]
        grads_ref[feat : 2 * feat, :] = acc_net[...]
        grads_ref[2 * feat : 2 * feat + hid, :] = acc_out[...]
        grads_ref[2 * feat + hid :, :] = acc_bias[...]
    for part in range(part_count):
        if split:
            share = feat // part_count
            rows = slice(part * share, (part + 1) * share)
            send_ref[part, :share, :] = acc_in[rows, :].astype(BF16)
            send_ref[part, share : 2 * share, :] = acc_net[rows, :].astype(BF16)
            send_ref[part, 2 * share : 3 * share, :] = acc_out[rows, :].astype(BF16)
            bias_at = base + 2 * slots
            send_ref[part, bias_at : bias_at + 16, :] = jnp.broadcast_to(acc_bias[0:1, :], (16, hid)).astype(BF16)
        rows = slice(cells + part * slots, cells + (part + 1) * slots)
        send_ref[part, base : base + slots, :] = acc[rows, :feat].astype(BF16)
        send_ref[part, base + slots : base + 2 * slots, :] = acc[rows, feat:].astype(BF16)


def combine_kernel(split, pos_ref, idx_ref, got_ref, own_ref, *outs):
    part_count, slots = idx_ref.shape[1:]
    cells, wide = own_ref.shape
    feat = wide // 2
    base = 3 * (feat // part_count) if split else 0
    group = 128 // slots
    rows_y = own_ref[:, :feat]
    rows_x = own_ref[:, feat:]
    for first in range(0, part_count, group):
        onehot = slot_onehot(idx_ref[0, first : first + group], cells)
        y = got_ref[first : first + group, base : base + slots, :].reshape(128, feat)
        x = got_ref[first : first + group, base + slots : base + 2 * slots, :].reshape(128, feat)
        rows_y += dot_nn(onehot, y)
        rows_x += dot_nn(onehot, x)
    scratch = outs[-1]
    scratch[:, :feat] = rows_y
    scratch[:, feat:] = rows_x
    if split:
        piece_ref, *shares, _ = outs
        piece_ref[...] = jnp.sum(got_ref[:, :base, :].astype(F32), axis=0).astype(BF16)
        bias_at = base + 2 * slots
        bias = jnp.sum(got_ref[:, bias_at : bias_at + 16, :].astype(F32), axis=0)
    else:
        *shares, _ = outs
    group_size = len(shares)
    share = cells // group_size
    net = pos_ref[1]
    for k, share_ref in enumerate(shares):
        at = pl.multiple_of((net ^ k) * share, share)
        share_ref[:share, :] = scratch[pl.ds(at, share), :].astype(share_ref.dtype)
        if split:
            share_ref[share:, :feat] = bias.astype(share_ref.dtype)
            share_ref[share:, feat:] = jnp.zeros((16, feat), share_ref.dtype)


def rows_kernel(split, pos_ref, x_ref, g_ref, own_ref, *rest):
    updated_ref, back_ref = rest[-3:-1] if split else rest[-2:]
    others = rest[:-3] if split else rest[:-2]
    share, feat = x_ref.shape
    total = own_ref[:share, :]
    for other in others:
        total += other[:share, :].astype(F32)
    updated_ref[...] = (x_ref[...].astype(F32) + total[:, :feat]).astype(BF16)
    back_ref[...] = (g_ref[...].astype(F32) + total[:, feat:]).astype(BF16)
    if split:
        bias_ref = rest[-1]
        for k, part in enumerate((own_ref,) + tuple(others)):
            at = pl.multiple_of((pos_ref[1] ^ k) * feat, feat)
            bias_ref[:, pl.ds(at, feat)] = part[share : share + 1, :feat].astype(F32)


def place_kernel(tags, pos_ref, *refs):
    ins, (in_ref, net_ref, out_ref) = refs[:-3], refs[-3:]
    for ref, tag in zip(ins, tags):
        share = ref.shape[1] // 3
        hid = ref.shape[2]
        for at, (cell_bits, net_bits) in enumerate(tag):
            row = pl.multiple_of((pos_ref[0] ^ cell_bits) * share, share)
            first = pl.multiple_of((pos_ref[1] ^ net_bits) * hid, hid)
            in_ref[pl.ds(row, share), pl.ds(first, hid)] = ref[at, :share, :].astype(F32)
            net_ref[pl.ds(row, share), pl.ds(first, hid)] = ref[at, share : 2 * share, :].astype(F32)
            out_ref[pl.ds(pl.multiple_of(first + row, share), share), :] = ref[at, 2 * share :, :].astype(F32)


def whole(*shapes_and_specs):
    return [pl.BlockSpec(memory_space=pltpu.VMEM) for _ in range(shapes_and_specs[0])]


SMEM = pl.BlockSpec(memory_space=pltpu.SMEM)
PARAMS = dict(compiler_params=pltpu.CompilerParams(vmem_limit_bytes=VMEM_LIMIT))


def flip(x, axis, bits):
    size = lax.axis_size(axis)
    return lax.ppermute(x, axis, [(i, i ^ bits) for i in range(size)])


def gather_pieces(piece):
    near = [piece[None]] + [flip(piece, "cell", 2 * k)[None] for k in (1, 2, 3)]
    first = jnp.concatenate(near[:2])
    second = jnp.concatenate(near[2:])
    first = jnp.concatenate([first, flip(first, "cell", 1)])
    second = jnp.concatenate([second, flip(second, "net", 2)])
    first_tag = [(0, 0), (2, 0), (1, 0), (3, 0)]
    second_tag = [(4, 0), (6, 0), (4, 2), (6, 2)]
    all_of = jnp.concatenate([first, flip(first, "net", 2), second, flip(second, "cell", 1)])
    tag = (
        first_tag
        + [(a, b ^ 2) for a, b in first_tag]
        + second_tag
        + [(a ^ 1, b) for a, b in second_tag]
    )
    return [all_of, flip(all_of, "net", 1)], [tag, [(a, b ^ 1) for a, b in tag]]


def local(cell_feat, out_grad, w_in, w_net, bias, w_out, send_idx, pin_net, pin_ref, block_count):
    part_count = lax.axis_size("cell")
    group_size = lax.axis_size("net")
    cells, feat = cell_feat.shape
    hidden_dim = w_in.shape[1]
    hid = hidden_dim // group_size
    slots = send_idx.shape[2]
    pins = pin_net.shape[3]
    table_len = cells + part_count * slots
    split = part_count == 8 and group_size == 4
    pos = jnp.stack([lax.axis_index("cell"), lax.axis_index("net")]).astype(jnp.int32)

    sent, ints = pl.pallas_call(
        gather_kernel,
        in_specs=[SMEM] + whole(5),
        out_specs=whole(2),
        out_shape=[
            jax.ShapeDtypeStruct((part_count * slots, 2 * feat), BF16),
            jax.ShapeDtypeStruct((8, pins), jnp.int32),
        ],
        name="take_boundary",
        **PARAMS,
    )(block_count, send_idx, cell_feat, out_grad, pin_net, pin_ref)
    halo = lax.all_to_all(
        sent.reshape(part_count, slots, 2 * feat), "cell", split_axis=0, concat_axis=0, tiled=True
    )
    all_ints = lax.all_gather(ints, "net")

    base = 3 * (feat // part_count) if split else 0
    send_rows = base + 2 * slots + (16 if split else 0)
    out_shape = [
        jax.ShapeDtypeStruct((cells, 2 * feat), F32),
        jax.ShapeDtypeStruct((part_count, send_rows, feat), BF16),
    ]
    if not split:
        out_shape.append(jax.ShapeDtypeStruct((2 * feat + hid + 8, hid), F32))

    def full(*shape):
        return pl.BlockSpec(shape, lambda i, pos: (0,) * len(shape))

    own, send, *grads = pl.pallas_call(
        functools.partial(layer_kernel, split),
        grid_spec=pltpu.PrefetchScalarGridSpec(
            num_scalar_prefetch=1,
            grid=(1,),
            in_specs=[
                full(cells, feat),
                full(cells, feat),
                full(part_count, slots, 2 * feat),
                full(group_size, 8, pins),
                pl.BlockSpec((feat, hid), lambda i, pos: (0, pos[1])),
                pl.BlockSpec((feat, hid), lambda i, pos: (0, pos[1])),
                pl.BlockSpec((1, hid), lambda i, pos: (0, pos[1])),
                pl.BlockSpec((hid, feat), lambda i, pos: (pos[1], 0)),
            ],
            out_specs=[full(*s.shape) for s in out_shape],
            scratch_shapes=[
                pltpu.VMEM((2 * feat, table_len), BF16),
                pltpu.VMEM((hid, feat), BF16),
                pltpu.VMEM((hid, feat), BF16),
                pltpu.VMEM((feat, hid), BF16),
                pltpu.VMEM((hid, 128), F32),
                pltpu.VMEM((8 * (-(-(group_size + 1) // 8)), pins), jnp.int32),
                pltpu.VMEM((8 * (-(-(group_size + 1) // 8)), pins), jnp.int32),
                pltpu.VMEM((table_len, 2 * feat), F32),
                pltpu.VMEM((feat, hid), F32),
                pltpu.VMEM((feat, hid), F32),
                pltpu.VMEM((hid, feat), F32),
                pltpu.VMEM((8, hid), F32),
            ],
        ),
        out_shape=out_shape,
        name="layer",
        **PARAMS,
    )(pos, cell_feat, out_grad, halo, all_ints, w_in, w_net, bias.reshape(1, hidden_dim), w_out)

    got = lax.all_to_all(send, "cell", split_axis=0, concat_axis=0, tiled=True)
    share = cells // group_size
    share_rows = share + (16 if split else 0)
    out_shape = [jax.ShapeDtypeStruct((share_rows, 2 * feat), F32 if k == 0 else BF16) for k in range(group_size)]
    if split:
        out_shape = [jax.ShapeDtypeStruct((base, feat), BF16)] + out_shape
    outs = pl.pallas_call(
        functools.partial(combine_kernel, split),
        in_specs=[SMEM] + whole(3),
        out_specs=whole(len(out_shape)),
        out_shape=out_shape,
        scratch_shapes=[pltpu.VMEM((cells, 2 * feat), F32)],
        name="combine",
        **PARAMS,
    )(pos, send_idx, got, own)
    shares = outs[1:] if split else outs
    received = [flip(shares[k], "net", k) for k in range(1, group_size)]

    def mine(i, pos):
        return (pos[1], 0)

    out_shape = [jax.ShapeDtypeStruct((share, feat), BF16)] * 2
    if split:
        out_shape.append(jax.ShapeDtypeStruct((1, hidden_dim), F32))
    rows = pl.pallas_call(
        functools.partial(rows_kernel, split),
        grid_spec=pltpu.PrefetchScalarGridSpec(
            num_scalar_prefetch=1,
            grid=(1,),
            in_specs=[pl.BlockSpec((share, feat), mine)] * 2 + [full(share_rows, 2 * feat)] * group_size,
            out_specs=[full(*s.shape) for s in out_shape],
        ),
        out_shape=out_shape,
        name="own_rows",
        **PARAMS,
    )(pos, cell_feat, out_grad, shares[0], *received)
    if split:
        pieces, tags = gather_pieces(outs[0])
        grad_in, grad_net, grad_out = pl.pallas_call(
            functools.partial(place_kernel, tags),
            in_specs=[SMEM] + whole(len(pieces)),
            out_specs=whole(3),
            out_shape=[
                jax.ShapeDtypeStruct((feat, hidden_dim), F32),
                jax.ShapeDtypeStruct((feat, hidden_dim), F32),
                jax.ShapeDtypeStruct((hidden_dim, feat), F32),
            ],
            name="place",
            **PARAMS,
        )(pos, *pieces)
        return (rows[0], rows[1], grad_in, grad_net, rows[2].reshape(hidden_dim), grad_out)
    summed = lax.all_gather(lax.psum(grads[0], "cell"), "net")
    grad_in = jnp.moveaxis(summed[:, :feat], 0, 1).reshape(feat, hidden_dim)
    grad_net = jnp.moveaxis(summed[:, feat : 2 * feat], 0, 1).reshape(feat, hidden_dim)
    grad_out = summed[:, 2 * feat : 2 * feat + hid].reshape(hidden_dim, feat)
    grad_bias = summed[:, 2 * feat + hid].reshape(hidden_dim)
    return (rows[0], rows[1], grad_in, grad_net, grad_bias, grad_out)


def solution(mesh):
    placed = (
        P("cell", None),
        P("cell", None),
        P(),
        P(),
        P(),
        P(),
        P("cell", None, None),
        P("cell", "net", None, None),
        P("cell", "net", None, None),
        P("cell", "net"),
    )
    return jax.shard_map(
        local,
        mesh=mesh,
        in_specs=placed,
        out_specs=(P(("cell", "net"), None), P(("cell", "net"), None), P(), P(), P(), P()),
        check_vma=False,
    )
```

time: 297 us -> 94.4 us (0.32)
  waiting for transfers between devices: 125 us -> 20.8 us
  matrix products: 42.8 us -> 0 us
  other arithmetic: 24.8 us -> 0.14 us
  local copies, waits for them, and re-layouts: 29.5 us -> 7.15 us
  Pallas kernels: 0 us -> 20 us
  between operations: 15.6 us -> 1.42 us
  blocking collectives: 37.9 us -> 26.6 us
    psum x1 -> x0, waiting for transfers between devices: 100 us -> none  [local(): lax.psum((gradients[0], gradients[1], gradients[2], gradients[3]), ('cell...]
    dot_general x22 -> x0, matrix products: 42.8 us -> none  [the longest x2 7.7 us: block_pass(): lax.dot_general(hidden, pin_grad, (((0,), (0,)), ((), ())), preferred_ele...]
    psum x1 -> x0, blocking collectives: 37.9 us -> none  [local(): lax.psum((gradients[0], gradients[1], gradients[2], gradients[3]), ('cell...]
    all_to_all x4 -> x1, waiting for transfers between devices: 24 us -> 2.04 us  [local(): lax.all_to_all(sent.reshape(part_count, slots, 2 * feat), 'cell', split_a...]
    all_to_all x0 -> x1, blocking collectives: none -> 21.4 us  [local(): got = lax.all_to_all(send, 'cell', split_axis=0, concat_axis=0, tiled=True)]
    pallas_call x0 -> x5, Pallas kernels: none -> 20 us  [the longest x1 14.3 us: local(): pl.pallas_call(functools.partial(layer_kernel, split), grid_spec=pltpu.Pr...]
    ppermute x0 -> x11, waiting for transfers between devices: none -> 18.8 us  [flip(): return lax.ppermute(x, axis, [(i, i ^ bits) for i in range(size)])]
    scatter-add x6 -> x0, other arithmetic: 18.3 us -> none  [the longest x2 8.12 us: accumulate(): acc_x.at[refs].add(pin_back)]
  transfers between devices with their start and end apart: 7 -> 12, of which waited for: 5 -> 8; matrix products, arithmetic and copies ran while one was open for 3% -> 0% of each run, Pallas kernels for 0% -> 1%
where the time goes in v1:
time: 94.4 us; the launch traced here: 93.8 us
  blocking collectives  26.6 us (28%)
  waiting for transfers between devices  20.8 us (22%)
  Pallas kernels  20 us (21%)
  starting transfers between devices  17.6 us (19%)
  local copies, waits for them, and re-layouts  7.15 us (8%)
  between operations  1.42 us (2%)
    all_to_all x1, blocking collectives, local(): got = lax.all_to_all(send, 'cell', split_axis=0, concat_axis=0, tiled=True)  21.4 us
    ppermute x11, waiting for transfers between devices, flip(): return lax.ppermute(x, axis, [(i, i ^ bits) for i in range(size)])  18.8 us
    pallas_call x1, Pallas kernels, local(): pl.pallas_call(functools.partial(layer_kernel, split), grid_spec=pltpu.Pr...  14.3 us
    ppermute x11, starting transfers between devices, flip(): return lax.ppermute(x, axis, [(i, i ^ bits) for i in range(size)])  10.2 us
    all_to_all x1, starting transfers between devices, local(): lax.all_to_all(sent.reshape(part_count, slots, 2 * feat), 'cell', split_a...  7.38 us
    unnamed x31, local copies, waits for them, and re-layouts  7.14 us
    all_gather x1, blocking collectives, local(): all_ints = lax.all_gather(ints, 'net')  5.23 us
    pallas_call x1, Pallas kernels, local(): pl.pallas_call(functools.partial(place_kernel, tags), in_specs=[SMEM] + w...  2.41 us
  transfers between devices with their start and end apart: 12, of which 8 were waited for; matrix products, arithmetic and copies ran while one was open for 0% of the time, Pallas kernels for 1%

profile of v1, /device:TPU:0, one launch (start us, length us, event | category | flops | bytes accessed | tf_op | source)
XLA Modules:
  0.0 93.8 jit_solution(2377235537418343103)
XLA Ops:
  1.3 0.0 copy-start
  1.3 0.9 %copy-done = bf16[512,256]{1,0:T(8,128)(2,1)S(1)} copy-done((bf16[512,256]{1,0:T(8,128)(2,1)S(1)}, bf16[512,256]{1,0:T(8,128)(2,1)}, u32[]{:S(2)}) %copy-start) | copy-done | bytes 262168
  2.2 0.0 copy-start.2
  2.2 0.9 %copy-done.2 = bf16[512,256]{1,0:T(8,128)(2,1)S(1)} copy-done((bf16[512,256]{1,0:T(8,128)(2,1)S(1)}, bf16[512,256]{1,0:T(8,128)(2,1)}, u32[]{:S(2)}) %copy-start.2) | copy-done | bytes 262168
  3.2 0.0 copy-start.7
  3.2 0.7 copy-done.7
  3.9 0.0 copy-start.9
  3.9 0.7 copy-done.9
  4.6 0.0 copy-start.10
  4.6 0.7 copy-done.10
  5.2 0.0 copy-start.3
  5.2 1.0 %take_boundary.1 = (bf16[128,512]{1,0:T(8,128)(2,1)}, s32[8,512]{1,0:T(8,128)S(1)}) custom-call(s32[1,1]{1,0:T(1,128)S(6)} %copy.23.count_ref, s32[1,8,16]{2,1,0:T(8,128)S(1)} %copy-done.7, bf16[512,256]{1,0:T(8,128)(2,1)S(1)} %copy-done, bf16[512,256]{1,0:T(8,128)(2,1)S(1)} %copy-done.2, s32[1,1,2,512]{3,2,1,0:T(2,128)S(1)} %copy-done.9, ...), custom_call_target="tpu_custom_call" | custom-call | tf_op jit(solution)/shard_map/take_boundary/pallas_call | solution.py:259
  6.3 0.0 copy-start.1
  6.3 7.4 %all-to-all-start = ((bf16[8,16,512]{2,1,0:T(8,128)(2,1)}), bf16[8,16,512]{2,1,0:T(8,128)(2,1)S(1)}, u32[]{:S(2)}, u32[]{:S(2)}) async-start(bf16[8,16,512]{2,1,0:T(8,128)(2,1)} %bitcast.2), calls=%async_computation | async-start | bytes 262144 | tf_op jit(solution)/shard_map/all_to_all | solution.py:270
  13.7 5.2 %all-gather = s32[32,512]{1,0:T(8,128)S(1)} all-gather(s32[8,512]{1,0:T(8,128)S(1)} %get-tuple-element.22), channel_id=2, replica_groups=mesh['cell'=8,'net'=4] {'net'}, dimensions={0}, use_global_device_ids=true | all-gather | bytes 81920 | tf_op jit(solution)/shard_map/all_gather | solution.py:273
  18.9 0.0 copy-start.11
  18.9 0.1 pad_add_fusion.pos_ref
  19.0 2.0 %all-to-all-done.halo_ref = bf16[8,16,512]{2,1,0:T(8,128)(2,1)S(1)} async-done(((bf16[8,16,512]{2,1,0:T(8,128)(2,1)}), bf16[8,16,512]{2,1,0:T(8,128)(2,1)S(1)}, u32[]{:S(2)}, u32[]{:S(2)}) %all-to-all-start) | async-done | bytes 131104 | tf_op jit(solution)/shard_map/all_to_all | solution.py:270
  21.0 0.0 copy-done.3
  21.0 0.0 copy-done.1
  21.0 0.0 copy-done.11
  21.0 0.0 copy-start.4
  21.0 1.0 %copy-done.4 = bf16[256,1024]{1,0:T(8,128)(2,1)S(1)} copy-done((bf16[256,1024]{1,0:T(8,128)(2,1)S(1)}, bf16[256,1024]{1,0:T(8,128)(2,1)}, u32[]{:S(2)}) %copy-start.4) | copy-done | bytes 524312
  22.1 0.0 copy-start.5
  22.1 1.0 %copy-done.5 = bf16[256,1024]{1,0:T(8,128)(2,1)S(1)} copy-done((bf16[256,1024]{1,0:T(8,128)(2,1)S(1)}, bf16[256,1024]{1,0:T(8,128)(2,1)}, u32[]{:S(2)}) %copy-start.5) | copy-done | bytes 524312
  23.1 0.0 copy-start.6
  23.1 1.0 %copy-done.6 = bf16[1024,256]{1,0:T(8,128)(2,1)S(1)} copy-done((bf16[1024,256]{1,0:T(8,128)(2,1)S(1)}, bf16[1024,256]{1,0:T(8,128)(2,1)}, u32[]{:S(2)}) %copy-start.6) | copy-done | bytes 524312
  24.2 14.3 %layer.1 = (f32[512,512]{1,0:T(8,128)S(1)}, bf16[8,144,256]{2,1,0:T(8,128)(2,1)S(1)}) custom-call(s32[2]{0:T(128)S(1)} %pad_add_fusion.pos_ref, bf16[512,256]{1,0:T(8,128)(2,1)S(1)} %copy-done.1, bf16[512,256]{1,0:T(8,128)(2,1)S(1)} %copy-done.3, bf16[8,16,512]{2,1,0:T(8,128)(2,1)S(1)} %all-to-all-done.halo_ref, s32[4,8,512]{2,1,0:T(8,128)S(1)} %bitcast.16, ...), custom_call_target="tpu_custom_call" | custom-call | tf_op jit(solution)/shard_map/layer/pallas_call | solution.py:287
  38.5 0.0 copy-start.8
  38.5 21.4 %all_to_all.10.got_ref = bf16[8,144,256]{2,1,0:T(8,128)(2,1)S(1)} all-to-all(bf16[8,144,256]{2,1,0:T(8,128)(2,1)S(1)} %get-tuple-element.23), channel_id=1, replica_groups=mesh['cell'=8,'net'=4] {'cell'}, dimensions={0} | all-to-all | bytes 1179648 | tf_op jit(solution)/shard_map/all_to_all | solution.py:323
  59.9 0.0 copy-done.8
  59.9 1.0 %combine.1 = (bf16[96,256]{1,0:T(8,128)(2,1)S(1)}, f32[144,512]{1,0:T(8,128)S(1)}, bf16[144,512]{1,0:T(8,128)(2,1)S(1)}, bf16[144,512]{1,0:T(8,128)(2,1)S(1)}, bf16[144,512]{1,0:T(8,128)(2,1)S(1)}) custom-call(s32[2]{0:T(128)S(1)} %pad_add_fusion.pos_ref, s32[1,8,16]{2,1,0:T(8,128)S(1)} %copy-done.8, bf16[8,144,256]{2,1,0:T(8,128)(2,1)S(1)} %all_to_all.10.got_ref, ...), custom_call_target="tpu_custom_call" | custom-call | tf_op jit(solution)/shard_map/combine/pallas_call | solution.py:329
  60.9 1.5 %collective-permute-start.7 = (bf16[96,256]{1,0:T(8,128)(2,1)S(1)}, bf16[96,256]{1,0:T(8,128)(2,1)S(1)}, u32[]{:S(2)}, u32[]{:S(2)}) collective-permute-start(bf16[96,256]{1,0:T(8,128)(2,1)S(1)} %get-tuple-element.31), channel_id=1, source_target_pairs={{0,24},{4,28},{8,16},{12,20},{16,8},{20,12},{24,0},{28,4},{1,25},{... | collective-permute-start | bytes 147464 | tf_op jit(solution)/shard_map/ppermute | solution.py:226
  62.4 0.8 collective-permute-start.6
  63.2 2.2 %collective-permute-start.3 = (bf16[96,256]{1,0:T(8,128)(2,1)S(1)}, bf16[96,256]{1,0:T(8,128)(2,1)S(1)}, u32[]{:S(2)}, u32[]{:S(2)}) collective-permute-start(bf16[96,256]{1,0:T(8,128)(2,1)S(1)} %get-tuple-element.31), channel_id=1, source_target_pairs={{0,8},{4,12},{8,0},{12,4},{16,24},{20,28},{24,16},{28,20},{1,9},{5... | collective-permute-start | bytes 147464 | tf_op jit(solution)/shard_map/ppermute | solution.py:226
  65.4 2.0 %collective-permute-done.7 = bf16[96,256]{1,0:T(8,128)(2,1)S(1)} collective-permute-done((bf16[96,256]{1,0:T(8,128)(2,1)S(1)}, bf16[96,256]{1,0:T(8,128)(2,1)S(1)}, u32[]{:S(2)}, u32[]{:S(2)}) %collective-permute-start.7) | collective-permute-done | bytes 49184 | tf_op jit(solution)/shard_map/ppermute | solution.py:226
  67.4 0.8 collective-permute-done.6
  68.2 1.6 %collective-permute-start.8 = (bf16[2,96,256]{2,1,0:T(8,128)(2,1)S(1)}, bf16[2,96,256]{2,1,0:T(8,128)(2,1)S(1)}, u32[]{:S(2)}, u32[]{:S(2)}) collective-permute-start(bf16[2,96,256]{2,1,0:T(8,128)(2,1)S(1)} %pad_maximum_fusion.3), channel_id=1, source_target_pairs={{0,2},{1,3},{2,0},{3,1},{4,6},{5,7},{6,4},{7,5},{8,10},{9,11},{10,... | collective-permute-start | bytes 294920 | tf_op jit(solution)/shard_map/ppermute | solution.py:226
  69.8 0.0 collective-permute-done.3
  69.8 0.8 collective-permute-start.4
  70.6 4.4 %collective-permute-done.4 = bf16[2,96,256]{2,1,0:T(8,128)(2,1)S(1)} collective-permute-done((bf16[2,96,256]{2,1,0:T(8,128)(2,1)S(1)}, bf16[2,96,256]{2,1,0:T(8,128)(2,1)S(1)}, u32[]{:S(2)}, u32[]{:S(2)}) %collective-permute-start.4) | collective-permute-done | bytes 98336 | tf_op jit(solution)/shard_map/ppermute | solution.py:226
  75.0 0.1 collective-permute-start.5
  75.1 0.0 collective-permute-done.8
  75.1 0.8 collective-permute-start.9
  75.9 4.8 %collective-permute-done.5 = bf16[4,96,256]{2,1,0:T(8,128)(2,1)S(1)} collective-permute-done((bf16[4,96,256]{2,1,0:T(8,128)(2,1)S(1)}, bf16[4,96,256]{2,1,0:T(8,128)(2,1)S(1)}, u32[]{:S(2)}, u32[]{:S(2)}) %collective-permute-start.5) | collective-permute-done | bytes 196640 | tf_op jit(solution)/shard_map/ppermute | solution.py:226
  80.8 0.1 collective-permute-done.9
  80.9 0.1 collective-permute-start.10
  81.0 0.5 collective-permute-start
  81.5 2.0 %collective-permute-start.1 = (bf16[144,512]{1,0:T(8,128)(2,1)S(1)}, bf16[144,512]{1,0:T(8,128)(2,1)S(1)}, u32[]{:S(2)}, u32[]{:S(2)}) collective-permute-start(bf16[144,512]{1,0:T(8,128)(2,1)S(1)} %get-tuple-element.27), channel_id=1, source_target_pairs={{0,2},{1,3},{2,0},{3,1},{4,6},{5,7},{6,4},{7,5},{8,10},{9,11},{10,... | collective-permute-start | bytes 442376 | tf_op jit(solution)/shard_map/ppermute | solution.py:226
  83.5 0.0 collective-permute-start.2
  83.5 0.0 collective-permute-done.rest_0_
  83.5 4.7 %collective-permute-done.1.rest_1_ = bf16[144,512]{1,0:T(8,128)(2,1)S(1)} collective-permute-done((bf16[144,512]{1,0:T(8,128)(2,1)S(1)}, bf16[144,512]{1,0:T(8,128)(2,1)S(1)}, u32[]{:S(2)}, u32[]{:S(2)}) %collective-permute-start.1) | collective-permute-done | bytes 147488 | tf_op jit(solution)/shard_map/ppermute | solution.py:226
  88.1 2.0 %collective-permute-done.2.rest_2_ = bf16[144,512]{1,0:T(8,128)(2,1)S(1)} collective-permute-done((bf16[144,512]{1,0:T(8,128)(2,1)S(1)}, bf16[144,512]{1,0:T(8,128)(2,1)S(1)}, u32[]{:S(2)}, u32[]{:S(2)}) %collective-permute-start.2) | collective-permute-done | bytes 147488 | tf_op jit(solution)/shard_map/ppermute | solution.py:226
  90.1 1.3 %own_rows.1 = (bf16[128,256]{1,0:T(8,128)(2,1)}, bf16[128,256]{1,0:T(8,128)(2,1)}, f32[1,1024]{1,0:T(1,128)}) custom-call(s32[2]{0:T(128)S(1)} %pad_add_fusion.pos_ref, bf16[512,256]{1,0:T(8,128)(2,1)S(1)} %copy-done.1, bf16[512,256]{1,0:T(8,128)(2,1)S(1)} %copy-done.3, f32[144,512]{1,0:T(8,128)S(1)} %get-tuple-element.25.own_ref, ...), custom_call_target="tpu_custom_call" | custom-call | tf_op jit(solution)/shard_map/own_rows/pallas_call | solution.py:347
  91.4 0.0 collective-permute-done.10.refs_1_
  91.4 2.4 %place.1 = (f32[256,1024]{1,0:T(8,128)}, f32[256,1024]{1,0:T(8,128)}, f32[1024,256]{1,0:T(8,128)}) custom-call(s32[2]{0:T(128)S(1)} %pad_add_fusion.pos_ref, bf16[16,96,256]{2,1,0:T(8,128)(2,1)S(1)} %constant_dynamic-update-slice_fusion.refs_0_, bf16[16,96,256]{2,1,0:T(8,128)(2,1)S(1)} %collective-permute-done.10.refs_1_), custom_call_target="tpu_custom_call" | custom-call | tf_op jit(solution)/shard_map/place/pallas_call | solution.py:361
  (12 shorter events, 0.1 us)
Async XLA Ops:
  1.3 1.0 %copy-start = (bf16[512,256]{1,0:T(8,128)(2,1)S(1)}, bf16[512,256]{1,0:T(8,128)(2,1)}, u32[]{:S(2)}) copy-start(bf16[512,256]{1,0:T(8,128)(2,1)} %x_ref.5) | copy-start | bytes 786436
  2.2 0.9 %copy-start.2 = (bf16[512,256]{1,0:T(8,128)(2,1)S(1)}, bf16[512,256]{1,0:T(8,128)(2,1)}, u32[]{:S(2)}) copy-start(bf16[512,256]{1,0:T(8,128)(2,1)} %g_ref.5) | copy-start | bytes 786436
  3.2 0.7 copy-start.7
  3.9 0.7 copy-start.9
  4.6 0.7 copy-start.10
  5.2 15.8 %copy-start.3 = (bf16[512,256]{1,0:T(8,128)(2,1)S(1)}, bf16[512,256]{1,0:T(8,128)(2,1)}, u32[]{:S(2)}) copy-start(bf16[512,256]{1,0:T(8,128)(2,1)} %g_ref.5) | copy-start | bytes 786436
  6.3 14.7 %copy-start.1 = (bf16[512,256]{1,0:T(8,128)(2,1)S(1)}, bf16[512,256]{1,0:T(8,128)(2,1)}, u32[]{:S(2)}) copy-start(bf16[512,256]{1,0:T(8,128)(2,1)} %x_ref.5) | copy-start | bytes 786436
  6.3 14.7 %all-to-all-start = ((bf16[8,16,512]{2,1,0:T(8,128)(2,1)}), bf16[8,16,512]{2,1,0:T(8,128)(2,1)S(1)}, u32[]{:S(2)}, u32[]{:S(2)}) async-start(bf16[8,16,512]{2,1,0:T(8,128)(2,1)} %bitcast.2), calls=%async_computation | async-start | bytes 262144 | tf_op jit(solution)/shard_map/all_to_all | solution.py:270
  18.9 2.1 %copy-start.11 = (f32[1024]{0:T(1024)S(1)}, f32[1024]{0:T(1024)}, u32[]{:S(2)}) copy-start(f32[1024]{0:T(1024)} %param.14) | copy-start | bytes 12292
  21.0 1.0 %copy-start.4 = (bf16[256,1024]{1,0:T(8,128)(2,1)S(1)}, bf16[256,1024]{1,0:T(8,128)(2,1)}, u32[]{:S(2)}) copy-start(bf16[256,1024]{1,0:T(8,128)(2,1)} %w_in_ref.1) | copy-start | bytes 1572868
  22.1 1.0 %copy-start.5 = (bf16[256,1024]{1,0:T(8,128)(2,1)S(1)}, bf16[256,1024]{1,0:T(8,128)(2,1)}, u32[]{:S(2)}) copy-start(bf16[256,1024]{1,0:T(8,128)(2,1)} %w_net_ref.1) | copy-start | bytes 1572868
  23.1 1.0 %copy-start.6 = (bf16[1024,256]{1,0:T(8,128)(2,1)S(1)}, bf16[1024,256]{1,0:T(8,128)(2,1)}, u32[]{:S(2)}) copy-start(bf16[1024,256]{1,0:T(8,128)(2,1)} %w_out_ref.1) | copy-start | bytes 1572868
  38.5 21.4 %copy-start.8 = (s32[1,8,16]{2,1,0:T(8,128)S(1)}, s32[1,8,16]{2,1,0:T(8,128)}, u32[]{:S(2)}) copy-start(s32[1,8,16]{2,1,0:T(8,128)} %idx_ref.3) | copy-start | bytes 1540
  60.9 6.4 %collective-permute-start.7 = (bf16[96,256]{1,0:T(8,128)(2,1)S(1)}, bf16[96,256]{1,0:T(8,128)(2,1)S(1)}, u32[]{:S(2)}, u32[]{:S(2)}) collective-permute-start(bf16[96,256]{1,0:T(8,128)(2,1)S(1)} %get-tuple-element.31), channel_id=1, source_target_pairs={{0,24},{4,28},{8,16},{12,20},{16,8},{20,12},{24,0},{28,4},{1,25},{... | collective-permute-start | bytes 147464 | tf_op jit(solution)/shard_map/ppermute | solution.py:226
  62.4 5.8 %collective-permute-start.6 = (bf16[96,256]{1,0:T(8,128)(2,1)S(1)}, bf16[96,256]{1,0:T(8,128)(2,1)S(1)}, u32[]{:S(2)}, u32[]{:S(2)}) collective-permute-start(bf16[96,256]{1,0:T(8,128)(2,1)S(1)} %get-tuple-element.31), channel_id=1, source_target_pairs={{0,16},{4,20},{8,24},{12,28},{16,0},{20,4},{24,8},{28,12},{1,17},{... | collective-permute-start | bytes 147464 | tf_op jit(solution)/shard_map/ppermute | solution.py:226
  63.2 6.6 %collective-permute-start.3 = (bf16[96,256]{1,0:T(8,128)(2,1)S(1)}, bf16[96,256]{1,0:T(8,128)(2,1)S(1)}, u32[]{:S(2)}, u32[]{:S(2)}) collective-permute-start(bf16[96,256]{1,0:T(8,128)(2,1)S(1)} %get-tuple-element.31), channel_id=1, source_target_pairs={{0,8},{4,12},{8,0},{12,4},{16,24},{20,28},{24,16},{28,20},{1,9},{5... | collective-permute-start | bytes 147464 | tf_op jit(solution)/shard_map/ppermute | solution.py:226
  68.2 6.9 %collective-permute-start.8 = (bf16[2,96,256]{2,1,0:T(8,128)(2,1)S(1)}, bf16[2,96,256]{2,1,0:T(8,128)(2,1)S(1)}, u32[]{:S(2)}, u32[]{:S(2)}) collective-permute-start(bf16[2,96,256]{2,1,0:T(8,128)(2,1)S(1)} %pad_maximum_fusion.3), channel_id=1, source_target_pairs={{0,2},{1,3},{2,0},{3,1},{4,6},{5,7},{6,4},{7,5},{8,10},{9,11},{10,... | collective-permute-start | bytes 294920 | tf_op jit(solution)/shard_map/ppermute | solution.py:226
  69.8 5.2 %collective-permute-start.4 = (bf16[2,96,256]{2,1,0:T(8,128)(2,1)S(1)}, bf16[2,96,256]{2,1,0:T(8,128)(2,1)S(1)}, u32[]{:S(2)}, u32[]{:S(2)}) collective-permute-start(bf16[2,96,256]{2,1,0:T(8,128)(2,1)S(1)} %pad_maximum_fusion.2), channel_id=1, source_target_pairs={{0,4},{4,0},{8,12},{12,8},{16,20},{20,16},{24,28},{28,24},{1,5},{5... | collective-permute-start | bytes 294920 | tf_op jit(solution)/shard_map/ppermute | solution.py:226
  75.0 5.7 %collective-permute-start.5 = (bf16[4,96,256]{2,1,0:T(8,128)(2,1)S(1)}, bf16[4,96,256]{2,1,0:T(8,128)(2,1)S(1)}, u32[]{:S(2)}, u32[]{:S(2)}) collective-permute-start(bf16[4,96,256]{2,1,0:T(8,128)(2,1)S(1)} %pad_maximum_fusion), channel_id=1, source_target_pairs={{0,2},{1,3},{2,0},{3,1},{4,6},{5,7},{6,4},{7,5},{8,10},{9,11},{10,... | collective-permute-start | bytes 589832 | tf_op jit(solution)/shard_map/ppermute | solution.py:226
  75.1 5.7 %collective-permute-start.9 = (bf16[4,96,256]{2,1,0:T(8,128)(2,1)S(1)}, bf16[4,96,256]{2,1,0:T(8,128)(2,1)S(1)}, u32[]{:S(2)}, u32[]{:S(2)}) collective-permute-start(bf16[4,96,256]{2,1,0:T(8,128)(2,1)S(1)} %pad_maximum_fusion.1), channel_id=1, source_target_pairs={{0,4},{4,0},{8,12},{12,8},{16,20},{20,16},{24,28},{28,24},{1,5},{5... | collective-permute-start | bytes 589832 | tf_op jit(solution)/shard_map/ppermute | solution.py:226
  80.9 10.5 %collective-permute-start.10 = (bf16[16,96,256]{2,1,0:T(8,128)(2,1)S(1)}, bf16[16,96,256]{2,1,0:T(8,128)(2,1)S(1)}, u32[]{:S(2)}, u32[]{:S(2)}) collective-permute-start(bf16[16,96,256]{2,1,0:T(8,128)(2,1)S(1)} %constant_dynamic-update-slice_fusion.refs_0_), channel_id=1, source_target_pairs={{0,1},{1,0},{2,3},{3,2},{4,5},{5,4},{6,7},{7,6},{8,9},{9,8},{10,11... | collective-permute-start | bytes 2359304 | tf_op jit(solution)/shard_map/ppermute | solution.py:226
  81.0 2.5 %collective-permute-start = (bf16[144,512]{1,0:T(8,128)(2,1)S(1)}, bf16[144,512]{1,0:T(8,128)(2,1)S(1)}, u32[]{:S(2)}, u32[]{:S(2)}) collective-permute-start(bf16[144,512]{1,0:T(8,128)(2,1)S(1)} %get-tuple-element.26), channel_id=1, source_target_pairs={{0,1},{1,0},{2,3},{3,2},{4,5},{5,4},{6,7},{7,6},{8,9},{9,8},{10,11... | collective-permute-start | bytes 442376 | tf_op jit(solution)/shard_map/ppermute | solution.py:226
  81.5 6.7 %collective-permute-start.1 = (bf16[144,512]{1,0:T(8,128)(2,1)S(1)}, bf16[144,512]{1,0:T(8,128)(2,1)S(1)}, u32[]{:S(2)}, u32[]{:S(2)}) collective-permute-start(bf16[144,512]{1,0:T(8,128)(2,1)S(1)} %get-tuple-element.27), channel_id=1, source_target_pairs={{0,2},{1,3},{2,0},{3,1},{4,6},{5,7},{6,4},{7,5},{8,10},{9,11},{10,... | collective-permute-start | bytes 442376 | tf_op jit(solution)/shard_map/ppermute | solution.py:226
  83.5 6.7 %collective-permute-start.2 = (bf16[144,512]{1,0:T(8,128)(2,1)S(1)}, bf16[144,512]{1,0:T(8,128)(2,1)S(1)}, u32[]{:S(2)}, u32[]{:S(2)}) collective-permute-start(bf16[144,512]{1,0:T(8,128)(2,1)S(1)} %get-tuple-element.28), channel_id=1, source_target_pairs={{0,3},{1,2},{2,1},{3,0},{4,7},{5,6},{6,5},{7,4},{8,11},{9,10},{10,... | collective-permute-start | bytes 442376 | tf_op jit(solution)/shard_map/ppermute | solution.py:226

commit v2 on v0

v2 whole, which is shorter than its diff:
```python
import functools

import jax
import jax.numpy as jnp
from jax import lax
from jax.experimental import pallas as pl
from jax.experimental.pallas import tpu as pltpu
from jax.sharding import PartitionSpec as P

NETS_BLK = 128
BF16 = jnp.bfloat16
F32 = jnp.float32
VMEM_LIMIT = 40 * 1024 * 1024


def dot_nn(a, b):
    return jnp.dot(a, b, preferred_element_type=F32)


def dot_nt(a, b):
    return lax.dot_general(a, b, (((1,), (1,)), ((), ())), preferred_element_type=F32)


def dot_tn(a, b):
    return lax.dot_general(a, b, (((0,), (0,)), ((), ())), preferred_element_type=F32)


def slot_onehot(idx, first, cells):
    parts, slots = idx.shape
    lanes = parts * slots
    lane = lax.broadcasted_iota(jnp.int32, (slots, lanes), 1)
    spread = ((lane & (slots - 1)) == lax.broadcasted_iota(jnp.int32, (slots, lanes), 0)).astype(BF16)
    high = dot_nn((idx >> 6).astype(F32).astype(BF16), spread)
    low = dot_nn((idx & 63).astype(F32).astype(BF16), spread)
    wide = high * 64.0 + low
    lane = lax.broadcasted_iota(jnp.int32, (parts, lanes), 1)
    mine = (lane // slots) == lax.broadcasted_iota(jnp.int32, (parts, lanes), 0)
    row = jnp.sum(jnp.where(mine, wide, 0.0), axis=0, keepdims=True).astype(jnp.int32) - first
    return (lax.broadcasted_iota(jnp.int32, (cells, lanes), 0) == row).astype(BF16)


def idx_rows(idx_ref, parts):
    return jnp.concatenate([idx_ref[0, pl.ds(part, 1), :] for part in parts], axis=0)


def start_copies(pairs, sems):
    copies = [pltpu.make_async_copy(src, dst, sems.at[i]) for i, (src, dst) in enumerate(pairs)]
    for copy in copies:
        copy.start()
    return copies


def gather_kernel(count_ref, idx_hbm, x_hbm, g_hbm, net_hbm, ref_hbm, out_ref, ints_ref, *scratch):
    idx_ref, x_ref, g_ref, net_ref, ref_ref, sems = scratch
    copies = start_copies(
        [(idx_hbm, idx_ref), (x_hbm, x_ref), (g_hbm, g_ref), (net_hbm, net_ref), (ref_hbm, ref_ref)], sems
    )
    for copy in copies:
        copy.wait()
    part_count, slots = idx_ref.shape[1:]
    cells, feat = x_ref.shape
    group = 128 // slots
    for first in range(0, part_count, group):
        onehot = slot_onehot(idx_ref[0, first : first + group], 0, cells)
        for at, values in ((0, x_ref), (feat, g_ref)):
            rows = dot_tn(onehot, values[...]).astype(BF16)
            out_ref[first : first + group, :, at : at + feat] = rows.reshape(group, slots, feat)
    slot_max = net_ref.shape[2]
    ints_ref[0] = jnp.broadcast_to(count_ref[...], ints_ref.shape[1:])
    ints_ref[0, :slot_max, :] = net_ref[0, 0]
    ints_ref[0, slot_max : 2 * slot_max, :] = ref_ref[0, 0]


def split_bf16(x):
    high = x.astype(BF16)
    return high, (x - high.astype(F32)).astype(BF16)


def block_ids(ints_refs):
    nets, refs = [], []
    pins = ints_refs[0].shape[2]
    extra_net = jnp.zeros((1, pins), jnp.int32)
    extra_ref = jnp.zeros((1, pins), jnp.int32)
    for ints in [ref[i] for ref in ints_refs for i in range(ref.shape[0])]:
        nets.append(ints[0:1, :])
        refs.append(ints[2:3, :])
        second = ints[4:5, :] > 1
        extra_net += jnp.where(second, ints[1:2, :] + 1, 0)
        extra_ref += jnp.where(second, ints[3:4, :] + 1, 0)
    nets.append(extra_net - 1)
    refs.append(extra_ref - 1)
    return nets, refs


def row_onehot(rows, ids):
    return (lax.broadcasted_iota(jnp.int32, (rows, ids.shape[1]), 0) == ids).astype(BF16)


def column_onehot(ids, lanes):
    return (lax.broadcasted_iota(jnp.int32, (ids.shape[0], lanes), 1) == ids).astype(BF16)


def net_inverse(pin_net):
    return 1.0 / jnp.maximum(jnp.sum(pin_net.astype(F32), axis=1, keepdims=True), 1.0)


def layer_kernel(fast, pos_ref, halo_ref, *rest):
    ints_refs, rest = rest[:-26], rest[-26:]
    x_hbm, g_hbm, w_in_hbm, w_net_hbm, bias_hbm, w_out_hbm, grads_ref, ids_hbm, sums_hbm, net_grads_hbm, *rest = rest
    table, w_in_ref, w_net_ref, bias_ref, w_out_ref, in_sems, ids, sums, net_grads, out_sems, *rest = rest
    at_pin, at_row, net_pin, taken, net_feats, terms = rest
    cells, feat = x_hbm.shape
    hid = w_in_ref.shape[1]
    pin_count, table_len = at_pin.shape
    blocks = net_grads.shape[0] // NETS_BLK
    pins = pin_count // blocks
    mine = pl.ds(pl.multiple_of(pos_ref[1] * hid, hid), hid)
    copies = start_copies(
        [
            (x_hbm, table.at[:cells, :feat]),
            (g_hbm, table.at[:cells, feat:]),
            (w_net_hbm.at[:, mine], w_net_ref),
            (w_in_hbm.at[:, mine], w_in_ref),
            (bias_hbm.at[:, mine], bias_ref),
            (w_out_hbm.at[mine, :], w_out_ref),
        ],
        in_sems,
    )
    table[cells:, :] = halo_ref[...].reshape(table_len - cells, 2 * feat)
    nets, refs = block_ids(ints_refs)
    ids[...] = jnp.zeros_like(ids)
    for b in range(blocks):
        ids[b : b + 1, :] = nets[b].astype(F32)
        ids[64 + b : 65 + b, :] = refs[b].astype(F32)
    columns = ids[...].T.astype(jnp.int32)
    for b in range(blocks):
        of = slice(b * pins, (b + 1) * pins)
        at_pin[of, :] = column_onehot(columns[:, 64 + b : 65 + b], table_len)
        net_pin[of, :] = column_onehot(columns[:, b : b + 1], NETS_BLK)
        at_row[:, of] = row_onehot(table_len, refs[b])
    pin_nets = [row_onehot(NETS_BLK, net) for net in nets]
    for copy in copies:
        copy.wait()
    outgoing = start_copies([(ids, ids_hbm)], out_sems)
    for b in range(blocks):
        of = slice(b * pins, (b + 1) * pins)
        nets_of = slice(b * NETS_BLK, (b + 1) * NETS_BLK)
        taken[of, :] = dot_nn(at_pin[of, :], table[...]).astype(BF16)
        net_sum = dot_nn(pin_nets[b], taken[of, :feat])
        net_feats[nets_of, :] = (net_sum * net_inverse(pin_nets[b])).astype(BF16)
    net_pre = dot_nn(net_feats[...], w_net_ref[...]).astype(BF16)
    scale = 0.7978845608028654
    for b in range(blocks):
        of = slice(b * pins, (b + 1) * pins)
        nets_of = slice(b * NETS_BLK, (b + 1) * NETS_BLK)
        pre = dot_nn(taken[of, :feat], w_in_ref[...]) + dot_nn(net_pin[of, :], net_pre[nets_of]) + bias_ref[...]
        pulled = dot_nt(taken[of, feat:], w_out_ref[...])
        square = pre * pre
        bend = jnp.tanh(pre * (scale + (scale * 0.044715) * square))
        half = 0.5 * bend + 0.5
        terms[of, :hid] = (pre * half).astype(BF16)
        slope = half + (0.5 * pre) * (1.0 - bend * bend) * (scale + (3 * scale * 0.044715) * square)
        pre_grad = (pulled * slope).astype(BF16)
        terms[of, hid:] = pre_grad
        net_grads[nets_of, :] = dot_nn(pin_nets[b], pre_grad).astype(BF16)
    sums[...] = dot_nn(at_row[...], terms[...])
    outgoing += start_copies([(sums, sums_hbm), (net_grads, net_grads_hbm)], out_sems.at[1:])
    hidden_high, hidden_low = split_bf16(sums[:, :hid])
    grad_high, grad_low = split_bf16(sums[:, hid:])
    table_x, table_g = table[:, :feat], table[:, feat:]
    acc_in = dot_tn(table_x, grad_high) + dot_tn(table_x, grad_low)
    acc_out = dot_tn(hidden_high, table_g) + dot_tn(hidden_low, table_g)
    acc_net = dot_tn(net_feats[...], net_grads[...])
    acc_bias = jnp.broadcast_to(jnp.sum(sums[:, hid:], axis=0, keepdims=True), (8, hid))
    if fast:
        part_count, rows, _ = grads_ref.shape
        part = feat // part_count
        for to in range(part_count):
            of = slice(to * part, (to + 1) * part)
            blocks_of = [acc_in[of, :], acc_net[of, :], acc_out[of, :], acc_bias]
            grads_ref[to] = jnp.concatenate([x.astype(BF16) for x in blocks_of], axis=0)
    else:
        grads_ref[:feat, :] = acc_in
        grads_ref[feat : 2 * feat, :] = acc_net
        grads_ref[2 * feat : 2 * feat + hid, :] = acc_out
        grads_ref[2 * feat + hid :, :] = acc_bias
    for copy in outgoing:
        copy.wait()


def back_kernel(fast, pos_ref, ids_hbm, sums_hbm, net_grads_hbm, w_in_hbm, w_net_hbm, w_out_hbm, *rest):
    *outs, ids, sums, net_grads, w_in_ref, w_net_ref, w_out_ref, sems, at_row, net_backs, acc = rest
    table_len, wide = acc.shape
    feat, hid = w_in_ref.shape
    blocks = net_grads.shape[0] // NETS_BLK
    pins = ids.shape[1]
    mine = pl.ds(pl.multiple_of(pos_ref[1] * hid, hid), hid)
    copies = start_copies(
        [
            (ids_hbm, ids),
            (net_grads_hbm, net_grads),
            (w_net_hbm.at[:, mine], w_net_ref),
            (w_in_hbm.at[:, mine], w_in_ref),
            (w_out_hbm.at[mine, :], w_out_ref),
            (sums_hbm, sums),
        ],
        sems,
    )
    for copy in copies:
        copy.wait()
    columns = ids[...].T.astype(jnp.int32)
    rows = ids[...].astype(jnp.int32)
    for b in range(blocks):
        of = slice(b * pins, (b + 1) * pins)
        nets_of = slice(b * NETS_BLK, (b + 1) * NETS_BLK)
        at_row[:, of] = row_onehot(table_len, rows[64 + b : 65 + b, :])
        inverse = net_inverse(row_onehot(NETS_BLK, rows[b : b + 1, :]))
        feat_grad = (dot_nt(net_grads[nets_of, :], w_net_ref[...]) * inverse).astype(BF16)
        net_backs[of, :] = dot_nn(column_onehot(columns[:, b : b + 1], NETS_BLK), feat_grad).astype(BF16)
    hidden_high, hidden_low = split_bf16(sums[:, :hid])
    grad_high, grad_low = split_bf16(sums[:, hid:])
    acc[:, :feat] = dot_nn(hidden_high, w_out_ref[...]) + dot_nn(hidden_low, w_out_ref[...])
    acc[:, feat:] = (
        dot_nt(grad_high, w_in_ref[...]) + dot_nt(grad_low, w_in_ref[...]) + dot_nn(at_row[...], net_backs[...])
    )
    if fast:
        group_size = len(outs)
        share = (table_len - 128) // group_size
        cells = share * group_size
        for bits, share_ref in enumerate(outs):
            to = pos_ref[1] ^ bits
            rows = acc[pl.ds(pl.multiple_of(to * share, share), share), :]
            share_ref[:share, :] = rows.astype(share_ref.dtype)
            for odd in range(2):
                part = pos_ref[0] ^ (2 * to + odd)
                edge = acc[pl.ds(pl.multiple_of(cells + part * 16, 16), 16), :]
                share_ref[share + 16 * odd : share + 16 * (odd + 1), :] = edge.astype(share_ref.dtype)
        return
    own_ref, send_ref = outs
    cells = own_ref.shape[0]
    own_ref[...] = acc[:cells, :]
    part_count, rows, _ = send_ref.shape
    slots = rows // 2
    for part in range(part_count):
        of = slice(cells + part * slots, cells + (part + 1) * slots)
        send_ref[part, :slots, :] = acc[of, :feat].astype(BF16)
        send_ref[part, slots:, :] = acc[of, feat:].astype(BF16)


def sum_shares_kernel(after_ref, own_ref, *rest):
    *others, rows_ref, even_ref, odd_ref = rest
    total = own_ref[...]
    for other in others:
        total += other[...].astype(F32)
    share = rows_ref.shape[0]
    slots = even_ref.shape[0]
    rows_ref[...] = total[:share]
    even_ref[...] = total[share : share + slots].astype(BF16)
    odd_ref[...] = total[share + slots :].astype(BF16)


def sum_pieces_kernel(got_ref, piece_ref, bias_ref):
    total = got_ref[0].astype(F32)
    for part in range(1, got_ref.shape[0]):
        total += got_ref[part].astype(F32)
    rows = piece_ref.shape[0]
    piece_ref[...] = total[:rows].astype(BF16)
    bias_ref[...] = jnp.concatenate([jnp.concatenate([total[rows:]] * 2, axis=0)] * 2, axis=1).astype(BF16)


def rows_kernel(pos_ref, idx_ref, x_hbm, g_hbm, rows_ref, *rest):
    *edges, updated_ref, back_ref, bias_ref, x_ref, g_ref, sems = rest
    share, feat = updated_ref.shape
    net = pos_ref[1]
    mine = pl.ds(pl.multiple_of(net * share, share), share)
    copies = start_copies([(x_hbm.at[mine, :], x_ref), (g_hbm.at[mine, :], g_ref)], sems)
    order = [pos_ref[0] ^ (2 * (net ^ bits) + odd) for bits in range(len(edges)) for odd in range(2)]
    onehot = slot_onehot(idx_rows(idx_ref, order), net * share, share)
    halo = jnp.concatenate([edge[:32, :] for edge in edges], axis=0)
    total = rows_ref[...] + dot_nn(onehot, halo)
    for bits, edge in enumerate(edges):
        at = pl.multiple_of((net ^ bits) * feat, feat)
        bias_ref[:, pl.ds(at, feat)] = edge[32:, :feat].astype(F32)[:1]
    for copy in copies:
        copy.wait()
    updated_ref[...] = (x_ref[...].astype(F32) + total[:, :feat]).astype(BF16)
    back_ref[...] = (g_ref[...].astype(F32) + total[:, feat:]).astype(BF16)


def place_kernel(tags, olds, pos_ref, *refs):
    ins, refs = refs[: len(tags)], refs[len(tags) + olds :]
    outs, (buffer, sems) = refs[:3], refs[3:]
    part = ins[0].shape[1] // 3
    hid = ins[0].shape[2]
    columns = sorted({net_bits for tag in tags for _, net_bits in tag})
    copies = []
    for matrix in range(3):
        for column, net_bits in enumerate(columns):
            at = matrix * len(columns) + column
            for ref, tag in zip(ins, tags):
                for piece, (cell_bits, bits) in enumerate(tag):
                    if bits == net_bits:
                        row = pl.multiple_of((pos_ref[0] ^ cell_bits) * part, part)
                        values = ref[piece, matrix * part : (matrix + 1) * part, :].astype(F32)
                        buffer[at, pl.ds(row, part), :] = values
            first = pl.ds(pl.multiple_of((pos_ref[1] ^ net_bits) * hid, hid), hid)
            target = outs[2].at[first, :] if matrix == 2 else outs[matrix].at[:, first]
            copy = pltpu.make_async_copy(buffer.at[at], target, sems.at[at])
            copy.start()
            copies.append(copy)
    for copy in copies:
        copy.wait()


def combine_kernel(pos_ref, idx_ref, got_ref, own_ref, *outs):
    part_count, slots = idx_ref.shape[1:]
    cells, wide = own_ref.shape
    feat = wide // 2
    group = 128 // slots
    rows_y = own_ref[:, :feat]
    rows_x = own_ref[:, feat:]
    for first in range(0, part_count, group):
        onehot = slot_onehot(idx_ref[0, first : first + group], 0, cells)
        y = got_ref[first : first + group, :slots, :].reshape(128, feat)
        x = got_ref[first : first + group, slots:, :].reshape(128, feat)
        rows_y += dot_nn(onehot, y)
        rows_x += dot_nn(onehot, x)
    *shares, scratch = outs
    scratch[:, :feat] = rows_y
    scratch[:, feat:] = rows_x
    share = cells // len(shares)
    for bits, share_ref in enumerate(shares):
        at = pl.multiple_of((pos_ref[1] ^ bits) * share, share)
        share_ref[...] = scratch[pl.ds(at, share), :].astype(share_ref.dtype)


def plain_rows_kernel(pos_ref, x_hbm, g_hbm, own_ref, *rest):
    *others, updated_ref, back_ref, x_ref, g_ref, sems = rest
    share, feat = updated_ref.shape
    mine = pl.ds(pl.multiple_of(pos_ref[1] * share, share), share)
    copies = start_copies([(x_hbm.at[mine, :], x_ref), (g_hbm.at[mine, :], g_ref)], sems)
    total = own_ref[...]
    for other in others:
        total += other[...].astype(F32)
    for copy in copies:
        copy.wait()
    updated_ref[...] = (x_ref[...].astype(F32) + total[:, :feat]).astype(BF16)
    back_ref[...] = (g_ref[...].astype(F32) + total[:, feat:]).astype(BF16)


def whole(count):
    return [pl.BlockSpec(memory_space=pltpu.VMEM)] * count


SMEM = pl.BlockSpec(memory_space=pltpu.SMEM)
HBM = pl.BlockSpec(memory_space=pltpu.HBM)
PARAMS = dict(compiler_params=pltpu.CompilerParams(vmem_limit_bytes=VMEM_LIMIT))


def in_hbm(*arrays):
    return [pltpu.with_memory_space_constraint(x, pltpu.HBM) for x in arrays]


def flip(x, axis, bits):
    size = lax.axis_size(axis)
    return lax.ppermute(x, axis, [(i, i ^ bits) for i in range(size)])


def both(x, cell_bits, net_bits):
    parts, group = lax.axis_size("cell"), lax.axis_size("net")
    pairs = [
        (c * group + n, (c ^ cell_bits(n)) * group + (n ^ net_bits)) for c in range(parts) for n in range(group)
    ]
    return lax.ppermute(x, ("cell", "net"), pairs)


def local(cell_feat, out_grad, w_in, w_net, bias, w_out, send_idx, pin_net, pin_ref, block_count):
    part_count = lax.axis_size("cell")
    group_size = lax.axis_size("net")
    cells, feat = cell_feat.shape
    hidden_dim = w_in.shape[1]
    hid = hidden_dim // group_size
    slots = send_idx.shape[2]
    pins = pin_net.shape[3]
    table_len = cells + part_count * slots
    fast = part_count == 8 and group_size == 4
    pos = jnp.stack([lax.axis_index("cell"), lax.axis_index("net")]).astype(jnp.int32)

    def shape(dtype, *dims):
        return jax.ShapeDtypeStruct(dims, dtype)

    sent, ints = pl.pallas_call(
        gather_kernel,
        in_specs=whole(1) + [HBM] * 5,
        out_specs=whole(2),
        out_shape=[shape(BF16, part_count, slots, 2 * feat), shape(jnp.int32, 1, 8, pins)],
        scratch_shapes=[
            pltpu.VMEM(send_idx.shape, jnp.int32),
            pltpu.VMEM((cells, feat), BF16),
            pltpu.VMEM((cells, feat), BF16),
            pltpu.VMEM(pin_net.shape, jnp.int32),
            pltpu.VMEM(pin_ref.shape, jnp.int32),
            pltpu.SemaphoreType.DMA((5,)),
        ],
        name="take_boundary",
        **PARAMS,
    )(block_count, *in_hbm(send_idx, cell_feat, out_grad, pin_net, pin_ref))
    halo = lax.all_to_all(sent, "cell", split_axis=0, concat_axis=0, tiled=True)
    if fast:
        all_ints = [ints] + [flip(ints, "net", bits) for bits in range(1, group_size)]
    else:
        all_ints = [lax.all_gather(ints, "net", tiled=True)]

    blocks = group_size + 1
    part = feat // part_count
    share = cells // group_size
    edge = part_count * slots // group_size
    weights = [w_in, w_net, bias.reshape(1, hidden_dim), w_out]
    grads, ids, sums, net_grads = pl.pallas_call(
        functools.partial(layer_kernel, fast),
        in_specs=[SMEM] + whole(1 + len(all_ints)) + [HBM] * 6,
        out_specs=whole(1) + [HBM] * 3,
        out_shape=[
            shape(BF16, part_count, 3 * part + 8, feat) if fast else shape(F32, 2 * feat + hid + 8, hid),
            pltpu.HBM((128, pins), F32),
            pltpu.HBM((table_len, 2 * hid), F32),
            pltpu.HBM((blocks * NETS_BLK, hid), BF16),
        ],
        scratch_shapes=[
            pltpu.VMEM((table_len, 2 * feat), BF16),
            pltpu.VMEM((feat, hid), BF16),
            pltpu.VMEM((feat, hid), BF16),
            pltpu.VMEM((1, hid), F32),
            pltpu.VMEM((hid, feat), BF16),
            pltpu.SemaphoreType.DMA((6,)),
            pltpu.VMEM((128, pins), F32),
            pltpu.VMEM((table_len, 2 * hid), F32),
            pltpu.VMEM((blocks * NETS_BLK, hid), BF16),
            pltpu.SemaphoreType.DMA((3,)),
            pltpu.VMEM((blocks * pins, table_len), BF16),
            pltpu.VMEM((table_len, blocks * pins), BF16),
            pltpu.VMEM((blocks * pins, NETS_BLK), BF16),
            pltpu.VMEM((blocks * pins, 2 * feat), BF16),
            pltpu.VMEM((blocks * NETS_BLK, feat), BF16),
            pltpu.VMEM((blocks * pins, 2 * hid), BF16),
        ],
        name="layer",
        **PARAMS,
    )(pos, halo, *all_ints, *in_hbm(cell_feat, out_grad, *weights))

    if fast:
        got = lax.all_to_all(grads, "cell", split_axis=0, concat_axis=0, tiled=True)
        out_shape = [shape(BF16 if bits else F32, share + edge, 2 * feat) for bits in range(group_size)]
    else:
        out_shape = [shape(F32, cells, 2 * feat), shape(BF16, part_count, 2 * slots, feat)]
    outs = pl.pallas_call(
        functools.partial(back_kernel, fast),
        in_specs=[SMEM] + [HBM] * 6,
        out_specs=whole(len(out_shape)),
        out_shape=out_shape,
        scratch_shapes=[
            pltpu.VMEM((128, pins), F32),
            pltpu.VMEM((table_len, 2 * hid), F32),
            pltpu.VMEM((blocks * NETS_BLK, hid), BF16),
            pltpu.VMEM((feat, hid), BF16),
            pltpu.VMEM((feat, hid), BF16),
            pltpu.VMEM((hid, feat), BF16),
            pltpu.SemaphoreType.DMA((6,)),
            pltpu.VMEM((table_len, blocks * pins), BF16),
            pltpu.VMEM((blocks * pins, feat), BF16),
            pltpu.VMEM((table_len, 2 * feat), F32),
        ],
        name="back",
        **PARAMS,
    )(pos, *in_hbm(ids, sums, net_grads, w_in, w_net, w_out))

    row_shapes = [shape(BF16, share, feat)] * 2
    row_scratch = [
        pltpu.VMEM((share, feat), BF16),
        pltpu.VMEM((share, feat), BF16),
        pltpu.SemaphoreType.DMA((2,)),
    ]
    grad_shapes = [shape(F32, feat, hidden_dim), shape(F32, feat, hidden_dim), shape(F32, hidden_dim, feat)]
    if not fast:
        own, send = outs
        got = lax.all_to_all(send, "cell", split_axis=0, concat_axis=0, tiled=True)
        shares = pl.pallas_call(
            combine_kernel,
            in_specs=[SMEM] + whole(3),
            out_specs=whole(group_size),
            out_shape=[shape(BF16 if bits else F32, share, 2 * feat) for bits in range(group_size)],
            scratch_shapes=[pltpu.VMEM((cells, 2 * feat), F32)],
            name="combine",
            **PARAMS,
        )(pos, send_idx, got, own)
        others = [flip(shares[bits], "net", bits) for bits in range(1, group_size)]
        updated, cell_grad = pl.pallas_call(
            plain_rows_kernel,
            in_specs=[SMEM] + [HBM] * 2 + whole(group_size),
            out_specs=whole(2),
            out_shape=row_shapes,
            scratch_shapes=row_scratch,
            name="own_rows",
            **PARAMS,
        )(pos, *in_hbm(cell_feat, out_grad), shares[0], *others)
        summed = lax.all_gather(lax.psum(grads, "cell"), "net")
        grad_in = jnp.moveaxis(summed[:, :feat], 0, 1).reshape(feat, hidden_dim)
        grad_net = jnp.moveaxis(summed[:, feat : 2 * feat], 0, 1).reshape(feat, hidden_dim)
        grad_out = summed[:, 2 * feat : 2 * feat + hid].reshape(hidden_dim, feat)
        grad_bias = summed[:, 2 * feat + hid].reshape(hidden_dim)
        return (updated, cell_grad, grad_in, grad_net, grad_bias, grad_out)

    shares = outs
    others = [flip(shares[bits], "net", bits) for bits in range(1, group_size)]
    piece, bias_sum = pl.pallas_call(
        sum_pieces_kernel,
        in_specs=whole(1),
        out_specs=whole(2),
        out_shape=[shape(BF16, 3 * part, feat), shape(BF16, 16, 2 * feat)],
        name="sum_pieces",
        **PARAMS,
    )(got)
    rows, even, odd = pl.pallas_call(
        sum_shares_kernel,
        in_specs=[pl.BlockSpec(memory_space=pl.ANY)] + whole(group_size),
        out_specs=whole(3),
        out_shape=[shape(F32, share, 2 * feat), shape(BF16, slots, 2 * feat), shape(BF16, slots, 2 * feat)],
        name="sum_shares",
        **PARAMS,
    )(piece, shares[0], *others)
    near = [flip(piece, "cell", 2 * k) for k in (1, 2, 3)]
    even = both(even, lambda n: 2 * n, 0)
    odd = both(odd, lambda n: 2 * n + 1, 0)
    near, even, odd = lax.optimization_barrier((near, even, odd))
    edges = jnp.concatenate([even, odd, bias_sum])
    other_edges = [flip(edges, "net", bits) for bits in range(1, group_size)]
    first, second = jnp.stack([piece, near[0]]), jnp.stack(near[1:])
    first = jnp.concatenate([first, flip(first, "cell", 1)])
    second = jnp.concatenate([second, flip(second, "net", 2)])
    early = [flip(first, "net", 1), flip(second, "net", 1)]
    third, fourth = flip(first, "net", 2), flip(second, "cell", 1)
    first_tag = [(0, 0), (2, 0), (1, 0), (3, 0)]
    second_tag = [(4, 0), (6, 0), (4, 2), (6, 2)]
    tags = [first_tag, second_tag, [(a, b ^ 2) for a, b in first_tag], [(a ^ 1, b) for a, b in second_tag]]
    twin_tags = [[(a, b ^ 1) for a, b in tag] for tag in tags]

    updated, cell_grad, grad_bias = pl.pallas_call(
        rows_kernel,
        in_specs=[SMEM] + whole(1) + [HBM] * 2 + whole(1 + group_size),
        out_specs=whole(3),
        out_shape=row_shapes + [shape(F32, 1, hidden_dim)],
        scratch_shapes=row_scratch,
        name="own_rows",
        **PARAMS,
    )(pos, send_idx, *in_hbm(cell_feat, out_grad), rows, edges, *other_edges)

    third, fourth, updated, cell_grad = lax.optimization_barrier((third, fourth, updated, cell_grad))
    late = [flip(third, "net", 1), flip(fourth, "net", 1)]

    def place(arrays, tags, olds):
        return pl.pallas_call(
            functools.partial(place_kernel, tags, len(olds)),
            in_specs=[SMEM] + whole(len(arrays)) + [HBM] * len(olds),
            out_specs=[HBM] * 3,
            out_shape=grad_shapes,
            scratch_shapes=[pltpu.VMEM((6, feat, hid), F32), pltpu.SemaphoreType.DMA((6,))],
            input_output_aliases={1 + len(arrays) + i: i for i in range(len(olds))},
            name="place",
            **PARAMS,
        )(pos, *arrays, *olds)

    grads = place([first, second, third, fourth], tags, [])
    grad_in, grad_net, grad_out = place(early + late, twin_tags, grads)
    return (updated, cell_grad, grad_in, grad_net, grad_bias.reshape(hidden_dim), grad_out)


def solution(mesh):
    placed = (
        P("cell", None),
        P("cell", None),
        P(),
        P(),
        P(),
        P(),
        P("cell", None, None),
        P("cell", "net", None, None),
        P("cell", "net", None, None),
        P("cell", "net"),
    )
    return jax.shard_map(
        local,
        mesh=mesh,
        in_specs=placed,
        out_specs=(P(("cell", "net"), None), P(("cell", "net"), None), P(), P(), P(), P()),
        check_vma=False,
    )
```

time: 297 us -> 82.7 us (0.28)
  waiting for transfers between devices: 125 us -> 21.7 us
  matrix products: 42.8 us -> 0 us
  blocking collectives: 37.9 us -> 0 us
  local copies, waits for them, and re-layouts: 29.5 us -> 0.01 us
  Pallas kernels: 0 us -> 25.3 us
  other arithmetic: 24.8 us -> 0.14 us
  starting transfers between devices: 17.5 us -> 33.5 us
  between operations: 15.6 us -> 1.6 us
    psum x1 -> x0, waiting for transfers between devices: 100 us -> none  [local(): lax.psum((gradients[0], gradients[1], gradients[2], gradients[3]), ('cell...]
    dot_general x22 -> x0, matrix products: 42.8 us -> none  [the longest x2 7.7 us: block_pass(): lax.dot_general(hidden, pin_grad, (((0,), (0,)), ((), ())), preferred_ele...]
    psum x1 -> x0, blocking collectives: 37.9 us -> none  [local(): lax.psum((gradients[0], gradients[1], gradients[2], gradients[3]), ('cell...]
    pallas_call x0 -> x8, Pallas kernels: none -> 25.3 us  [the longest x1 12.8 us: local(): pl.pallas_call(functools.partial(layer_kernel, fast), in_specs=[SMEM] + w...]
    ppermute x0 -> x22, starting transfers between devices: none -> 22.6 us  [the longest x20 20.5 us: flip(): return lax.ppermute(x, axis, [(i, i ^ bits) for i in range(size)])]
    scatter-add x6 -> x0, other arithmetic: 18.3 us -> none  [the longest x2 8.12 us: accumulate(): acc_x.at[refs].add(pin_back)]
    all_to_all x4 -> x2, waiting for transfers between devices: 24 us -> 7.97 us  [the longest x1 5.21 us: local(): got = lax.all_to_all(grads, 'cell', split_axis=0, concat_axis=0, tiled=True)]
    gather x6 -> x0, local copies, waits for them, and re-layouts: 13.8 us -> none  [the longest x2 5.15 us: block_pass(): pin_grad = table_g[refs]]
  transfers between devices with their start and end apart: 7 -> 24, of which waited for: 5 -> 8; matrix products, arithmetic and copies ran while one was open for 3% -> 0% of each run, Pallas kernels for 0% -> 11%
where the time goes in v2:
time: 82.7 us; the launch traced here: 82.3 us
  starting transfers between devices  33.5 us (41%)
  Pallas kernels  25.3 us (31%)
  waiting for transfers between devices  21.7 us (26%)
  between operations  1.6 us (2%)
    ppermute x20, starting transfers between devices, flip(): return lax.ppermute(x, axis, [(i, i ^ bits) for i in range(size)])  20.5 us
    pallas_call x1, Pallas kernels, local(): pl.pallas_call(functools.partial(layer_kernel, fast), in_specs=[SMEM] + w...  12.8 us
    ppermute x20, waiting for transfers between devices, flip(): return lax.ppermute(x, axis, [(i, i ^ bits) for i in range(size)])  11.4 us
    all_to_all x1, starting transfers between devices, local(): halo = lax.all_to_all(sent, 'cell', split_axis=0, concat_axis=0, tiled=True)  7.26 us
    all_to_all x1, waiting for transfers between devices, local(): got = lax.all_to_all(grads, 'cell', split_axis=0, concat_axis=0, tiled=True)  5.21 us
    pallas_call x1, Pallas kernels, local(): pl.pallas_call(functools.partial(back_kernel, fast), in_specs=[SMEM] + [H...  4.69 us
    all_to_all x1, starting transfers between devices, local(): got = lax.all_to_all(grads, 'cell', split_axis=0, concat_axis=0, tiled=True)  3.66 us
    pallas_call x2, Pallas kernels, place(): pl.pallas_call(functools.partial(place_kernel, tags, len(olds)), in_specs...  3.5 us
  transfers between devices with their start and end apart: 24, of which 8 were waited for; matrix products, arithmetic and copies ran while one was open for 0% of the time, Pallas kernels for 11%

profile of v2, /device:TPU:0, one launch (start us, length us, event | category | flops | bytes accessed | tf_op | source)
XLA Modules:
  0.0 82.3 jit_solution(7386224895970352360)
XLA Ops:
  1.3 2.1 %take_boundary.1 = (bf16[8,16,512]{2,1,0:T(8,128)(2,1)}, s32[1,8,512]{2,1,0:T(8,128)S(1)}) custom-call(s32[1,1]{1,0:T(1,128)S(6)} %copy.24.count_ref, s32[1,8,16]{2,1,0:T(8,128)} %idx_ref.1, bf16[512,256]{1,0:T(8,128)(2,1)} %x_hbm.3, bf16[512,256]{1,0:T(8,128)(2,1)} %g_hbm.3, s32[1,1,2,512]{3,2,1,0:T(2,128)} %net_hbm.1, s32[1,1,2,512]{3,2,1,0:T(2,128)} %ref_hbm.1), custom_call_target="tpu_custom_call" | custom-call | tf_op jit(solution)/shard_map/take_boundary/pallas_call | solution.py:392
  3.4 7.3 %all-to-all-start = ((bf16[8,16,512]{2,1,0:T(8,128)(2,1)}), bf16[8,16,512]{2,1,0:T(8,128)(2,1)S(1)}, u32[]{:S(2)}, u32[]{:S(2)}) async-start(bf16[8,16,512]{2,1,0:T(8,128)(2,1)} %get-tuple-element.39), calls=%async_computation | async-start | bytes 262144 | tf_op jit(solution)/shard_map/all_to_all | solution.py:408
  10.7 0.7 collective-permute-start.2
  11.4 0.9 %collective-permute-start.1 = (s32[1,8,512]{2,1,0:T(8,128)S(1)}, s32[1,8,512]{2,1,0:T(8,128)S(1)}, u32[]{:S(2)}, u32[]{:S(2)}) collective-permute-start(s32[1,8,512]{2,1,0:T(8,128)S(1)} %get-tuple-element.40.rest_0_), channel_id=1, source_target_pairs={{0,2},{1,3},{2,0},{3,1},{4,6},{5,7},{6,4},{7,5},{8,10},{9,11},{10,... | collective-permute-start | bytes 49160 | tf_op jit(solution)/shard_map/ppermute | solution.py:366
  12.3 0.3 collective-permute-start
  12.5 0.1 pad_add_fusion.pos_ref
  12.6 1.3 %collective-permute-done.2.rest_3_ = s32[1,8,512]{2,1,0:T(8,128)S(1)} collective-permute-done((s32[1,8,512]{2,1,0:T(8,128)S(1)}, s32[1,8,512]{2,1,0:T(8,128)S(1)}, u32[]{:S(2)}, u32[]{:S(2)}) %collective-permute-start.2) | collective-permute-done | bytes 16416 | tf_op jit(solution)/shard_map/ppermute | solution.py:366
  14.0 1.3 %collective-permute-done.1.rest_2_ = s32[1,8,512]{2,1,0:T(8,128)S(1)} collective-permute-done((s32[1,8,512]{2,1,0:T(8,128)S(1)}, s32[1,8,512]{2,1,0:T(8,128)S(1)}, u32[]{:S(2)}, u32[]{:S(2)}) %collective-permute-start.1) | collective-permute-done | bytes 16416 | tf_op jit(solution)/shard_map/ppermute | solution.py:366
  15.3 0.0 collective-permute-done.rest_1_
  15.3 2.8 %all-to-all-done.halo_ref = bf16[8,16,512]{2,1,0:T(8,128)(2,1)S(1)} async-done(((bf16[8,16,512]{2,1,0:T(8,128)(2,1)}), bf16[8,16,512]{2,1,0:T(8,128)(2,1)S(1)}, u32[]{:S(2)}, u32[]{:S(2)}) %all-to-all-start) | async-done | bytes 131104 | tf_op jit(solution)/shard_map/all_to_all | solution.py:408
  18.0 12.8 %layer.1 = (bf16[8,104,256]{2,1,0:T(8,128)(2,1)}, f32[128,512]{1,0:T(8,128)}, f32[640,512]{1,0:T(8,128)}, bf16[640,256]{1,0:T(8,128)(2,1)}) custom-call(s32[2]{0:T(128)S(1)} %pad_add_fusion.pos_ref, bf16[8,16,512]{2,1,0:T(8,128)(2,1)S(1)} %all-to-all-done.halo_ref, s32[1,8,512]{2,1,0:T(8,128)S(1)} %get-tuple-element.40.rest_0_, ...), custom_call_target="tpu_custom_call" | custom-call | tf_op jit(solution)/shard_map/layer/pallas_call | solution.py:419
  30.8 3.7 %all-to-all-start.1 = ((bf16[8,104,256]{2,1,0:T(8,128)(2,1)}), bf16[8,104,256]{2,1,0:T(8,128)(2,1)S(1)}, u32[]{:S(2)}, u32[]{:S(2)}) async-start(bf16[8,104,256]{2,1,0:T(8,128)(2,1)} %get-tuple-element.41), calls=%async_computation.1 | async-start | bytes 851968 | tf_op jit(solution)/shard_map/all_to_all | solution.py:452
  34.5 4.7 %back.1 = (f32[160,512]{1,0:T(8,128)S(1)}, bf16[160,512]{1,0:T(8,128)(2,1)S(1)}, bf16[160,512]{1,0:T(8,128)(2,1)S(1)}, bf16[160,512]{1,0:T(8,128)(2,1)S(1)}) custom-call(s32[2]{0:T(128)S(1)} %pad_add_fusion.pos_ref, f32[128,512]{1,0:T(8,128)} %get-tuple-element.43.ids_hbm, f32[640,512]{1,0:T(8,128)} %get-tuple-element.44.sums_hbm, ...), custom_call_target="tpu_custom_call" | custom-call | tf_op jit(solution)/shard_map/back/pallas_call | solution.py:456
  39.2 0.0 copy-start
  39.2 0.1 collective-permute-start.6
  39.3 1.6 %collective-permute-start.7 = (bf16[160,512]{1,0:T(8,128)(2,1)S(1)}, bf16[160,512]{1,0:T(8,128)(2,1)S(1)}, u32[]{:S(2)}, u32[]{:S(2)}) collective-permute-start(bf16[160,512]{1,0:T(8,128)(2,1)S(1)} %get-tuple-element.48), channel_id=1, source_target_pairs={{0,2},{1,3},{2,0},{3,1},{4,6},{5,7},{6,4},{7,5},{8,10},{9,11},{10,... | collective-permute-start | bytes 491528 | tf_op jit(solution)/shard_map/ppermute | solution.py:366
  40.9 0.3 collective-permute-start.8
  41.1 5.2 %all-to-all-done.1.got_ref = bf16[8,104,256]{2,1,0:T(8,128)(2,1)S(1)} async-done(((bf16[8,104,256]{2,1,0:T(8,128)(2,1)}), bf16[8,104,256]{2,1,0:T(8,128)(2,1)S(1)}, u32[]{:S(2)}, u32[]{:S(2)}) %all-to-all-start.1) | async-done | bytes 426016 | tf_op jit(solution)/shard_map/all_to_all | solution.py:452
  46.3 0.1 sum_pieces.1
  46.4 1.2 %collective-permute-start.5 = (bf16[96,256]{1,0:T(8,128)(2,1)S(1)}, bf16[96,256]{1,0:T(8,128)(2,1)S(1)}, u32[]{:S(2)}, u32[]{:S(2)}) collective-permute-start(bf16[96,256]{1,0:T(8,128)(2,1)S(1)} %get-tuple-element.42.after_ref), channel_id=1, source_target_pairs={{0,24},{4,28},{8,16},{12,20},{16,8},{20,12},{24,0},{28,4},{1,25},{... | collective-permute-start | bytes 147464 | tf_op jit(solution)/shard_map/ppermute | solution.py:366
  47.6 1.2 %collective-permute-start.4 = (bf16[96,256]{1,0:T(8,128)(2,1)S(1)}, bf16[96,256]{1,0:T(8,128)(2,1)S(1)}, u32[]{:S(2)}, u32[]{:S(2)}) collective-permute-start(bf16[96,256]{1,0:T(8,128)(2,1)S(1)} %get-tuple-element.42.after_ref), channel_id=1, source_target_pairs={{0,16},{4,20},{8,24},{12,28},{16,0},{20,4},{24,8},{28,12},{1,17},{... | collective-permute-start | bytes 147464 | tf_op jit(solution)/shard_map/ppermute | solution.py:366
  48.8 0.0 collective-permute-done.6.rest_0_
  48.8 2.1 %collective-permute-start.3 = (bf16[96,256]{1,0:T(8,128)(2,1)S(1)}, bf16[96,256]{1,0:T(8,128)(2,1)S(1)}, u32[]{:S(2)}, u32[]{:S(2)}) collective-permute-start(bf16[96,256]{1,0:T(8,128)(2,1)S(1)} %get-tuple-element.42.after_ref), channel_id=1, source_target_pairs={{0,8},{4,12},{8,0},{12,4},{16,24},{20,28},{24,16},{28,20},{1,9},{5... | collective-permute-start | bytes 147464 | tf_op jit(solution)/shard_map/ppermute | solution.py:366
  50.9 0.0 collective-permute-done.7.rest_1_
  50.9 0.0 collective-permute-done.8.rest_2_
  50.9 0.1 sum_shares.1
  50.9 0.7 collective-permute-start.9
  51.6 1.5 %collective-permute-start.10 = (bf16[16,512]{1,0:T(8,128)(2,1)S(1)}, bf16[16,512]{1,0:T(8,128)(2,1)S(1)}, u32[]{:S(2)}, u32[]{:S(2)}) collective-permute-start(bf16[16,512]{1,0:T(8,128)(2,1)S(1)} %get-tuple-element.51), channel_id=1, source_target_pairs={{0,4},{1,13},{2,22},{3,31},{4,0},{5,9},{6,18},{7,27},{8,12},{9,5},... | collective-permute-start | bytes 49160 | tf_op jit(solution)/shard_map/ppermute | solution.py:374
  53.1 0.0 collective-permute-done.9
  53.1 2.3 %collective-permute-done.10 = bf16[16,512]{1,0:T(8,128)(2,1)S(1)} collective-permute-done((bf16[16,512]{1,0:T(8,128)(2,1)S(1)}, bf16[16,512]{1,0:T(8,128)(2,1)S(1)}, u32[]{:S(2)}, u32[]{:S(2)}) %collective-permute-start.10) | collective-permute-done | bytes 16416 | tf_op jit(solution)/shard_map/ppermute | solution.py:374
  55.4 0.0 collective-permute-done.5
  55.4 0.0 collective-permute-done.4
  55.4 0.0 collective-permute-done.3
  55.4 1.5 %collective-permute-start.11 = (bf16[2,96,256]{2,1,0:T(8,128)(2,1)S(1)}, bf16[2,96,256]{2,1,0:T(8,128)(2,1)S(1)}, u32[]{:S(2)}, u32[]{:S(2)}) collective-permute-start(bf16[2,96,256]{2,1,0:T(8,128)(2,1)S(1)} %pad_maximum_fusion.2), channel_id=1, source_target_pairs={{0,4},{4,0},{8,12},{12,8},{16,20},{20,16},{24,28},{28,24},{1,5},{5... | collective-permute-start | bytes 294920 | tf_op jit(solution)/shard_map/ppermute | solution.py:366
  56.9 5.4 %collective-permute-start.13 = (bf16[2,96,256]{2,1,0:T(8,128)(2,1)S(1)}, bf16[2,96,256]{2,1,0:T(8,128)(2,1)S(1)}, u32[]{:S(2)}, u32[]{:S(2)}) collective-permute-start(bf16[2,96,256]{2,1,0:T(8,128)(2,1)S(1)} %pad_maximum_fusion.3), channel_id=1, source_target_pairs={{0,2},{1,3},{2,0},{3,1},{4,6},{5,7},{6,4},{7,5},{8,10},{9,11},{10,... | collective-permute-start | bytes 294920 | tf_op jit(solution)/shard_map/ppermute | solution.py:366
  62.4 3.6 %collective-permute-done.13 = bf16[2,96,256]{2,1,0:T(8,128)(2,1)S(1)} collective-permute-done((bf16[2,96,256]{2,1,0:T(8,128)(2,1)S(1)}, bf16[2,96,256]{2,1,0:T(8,128)(2,1)S(1)}, u32[]{:S(2)}, u32[]{:S(2)}) %collective-permute-start.13) | collective-permute-done | bytes 98336 | tf_op jit(solution)/shard_map/ppermute | solution.py:366
  66.0 0.6 collective-permute-start.14
  66.6 0.0 collective-permute-done.11
  66.6 1.8 %collective-permute-start.12 = (bf16[4,96,256]{2,1,0:T(8,128)(2,1)S(1)}, bf16[4,96,256]{2,1,0:T(8,128)(2,1)S(1)}, u32[]{:S(2)}, u32[]{:S(2)}) collective-permute-start(bf16[4,96,256]{2,1,0:T(8,128)(2,1)S(1)} %pad_maximum_fusion.refs_0_), channel_id=1, source_target_pairs={{0,2},{1,3},{2,0},{3,1},{4,6},{5,7},{6,4},{7,5},{8,10},{9,11},{10,... | collective-permute-start | bytes 589832 | tf_op jit(solution)/shard_map/ppermute | solution.py:366
  68.4 0.0 collective-permute-start.17
  68.4 0.8 %collective-permute-start.16 = (bf16[48,512]{1,0:T(8,128)(2,1)S(1)}, bf16[48,512]{1,0:T(8,128)(2,1)S(1)}, u32[]{:S(2)}, u32[]{:S(2)}) collective-permute-start(bf16[48,512]{1,0:T(8,128)(2,1)S(1)} %constant_dynamic-update-slice_fusion.rest_0_), channel_id=1, source_target_pairs={{0,2},{1,3},{2,0},{3,1},{4,6},{5,7},{6,4},{7,5},{8,10},{9,11},{10,... | collective-permute-start | bytes 147464 | tf_op jit(solution)/shard_map/ppermute | solution.py:366
  69.3 1.0 %collective-permute-start.15 = (bf16[48,512]{1,0:T(8,128)(2,1)S(1)}, bf16[48,512]{1,0:T(8,128)(2,1)S(1)}, u32[]{:S(2)}, u32[]{:S(2)}) collective-permute-start(bf16[48,512]{1,0:T(8,128)(2,1)S(1)} %constant_dynamic-update-slice_fusion.rest_0_), channel_id=1, source_target_pairs={{0,1},{1,0},{2,3},{3,2},{4,5},{5,4},{6,7},{7,6},{8,9},{9,8},{10,11... | collective-permute-start | bytes 147464 | tf_op jit(solution)/shard_map/ppermute | solution.py:366
  70.3 3.5 %collective-permute-done.17.rest_3_ = bf16[48,512]{1,0:T(8,128)(2,1)S(1)} collective-permute-done((bf16[48,512]{1,0:T(8,128)(2,1)S(1)}, bf16[48,512]{1,0:T(8,128)(2,1)S(1)}, u32[]{:S(2)}, u32[]{:S(2)}) %collective-permute-start.17) | collective-permute-done | bytes 49184 | tf_op jit(solution)/shard_map/ppermute | solution.py:366
  73.8 1.5 %collective-permute-done.16.rest_2_ = bf16[48,512]{1,0:T(8,128)(2,1)S(1)} collective-permute-done((bf16[48,512]{1,0:T(8,128)(2,1)S(1)}, bf16[48,512]{1,0:T(8,128)(2,1)S(1)}, u32[]{:S(2)}, u32[]{:S(2)}) %collective-permute-start.16) | collective-permute-done | bytes 49184 | tf_op jit(solution)/shard_map/ppermute | solution.py:366
  75.4 0.0 collective-permute-done.15.rest_1_
  75.4 0.0 copy-done
  75.4 2.1 %own_rows.1 = (bf16[128,256]{1,0:T(8,128)(2,1)}, bf16[128,256]{1,0:T(8,128)(2,1)}, f32[1,1024]{1,0:T(1,128)}) custom-call(s32[2]{0:T(128)S(1)} %pad_add_fusion.pos_ref, s32[1,8,16]{2,1,0:T(8,128)S(1)} %copy-done, bf16[512,256]{1,0:T(8,128)(2,1)} %x_hbm.3, bf16[512,256]{1,0:T(8,128)(2,1)} %g_hbm.3, f32[128,512]{1,0:T(8,128)S(1)} %get-tuple-element.55.rows_ref, ...), custom_call_target="tpu_custom_call" | custom-call | tf_op jit(solution)/shard_map/own_rows/pallas_call | solution.py:547
  77.5 0.1 collective-permute-start.19
  77.6 0.5 collective-permute-start.18
  78.1 0.0 collective-permute-done.14.refs_3_
  78.1 0.0 collective-permute-done.12.refs_2_
  78.1 0.1 collective-permute-start.20
  78.2 0.4 collective-permute-start.21
  78.6 1.7 %place.2 = (f32[256,1024]{1,0:T(8,128)}, f32[256,1024]{1,0:T(8,128)}, f32[1024,256]{1,0:T(8,128)}) custom-call(s32[2]{0:T(128)S(1)} %pad_add_fusion.pos_ref, bf16[4,96,256]{2,1,0:T(8,128)(2,1)S(1)} %pad_maximum_fusion.refs_0_, bf16[4,96,256]{2,1,0:T(8,128)(2,1)S(1)} %pad_maximum_fusion.1.refs_1_, bf16[4,96,256]{2,1,0:T(8,128)(2,1)S(1)} %collective-permute-done.12.refs_2_, ...), custom_call_target="tpu_custom_call" | custom-call | tf_op jit(solution)/shard_map/place/pallas_call | solution.py:561
  80.3 0.0 collective-permute-done.19.refs_1_
  80.4 0.0 collective-permute-done.18.refs_0_
  80.4 0.0 collective-permute-done.20.refs_2_
  80.4 0.0 collective-permute-done.21.refs_3_
  80.4 1.8 %place.3 = (f32[256,1024]{1,0:T(8,128)}, f32[256,1024]{1,0:T(8,128)}, f32[1024,256]{1,0:T(8,128)}) custom-call(s32[2]{0:T(128)S(1)} %pad_add_fusion.pos_ref, bf16[4,96,256]{2,1,0:T(8,128)(2,1)S(1)} %collective-permute-done.18.refs_0_, ...), custom_call_target="tpu_custom_call", output_to_operand_aliasing={{0}: (5, {}), {1}: (6, {}), {2}: (7, {})} | custom-call | tf_op jit(solution)/shard_map/place/pallas_call | solution.py:561
  (7 shorter events, 0.1 us)
Async XLA Ops:
  3.4 14.6 %all-to-all-start = ((bf16[8,16,512]{2,1,0:T(8,128)(2,1)}), bf16[8,16,512]{2,1,0:T(8,128)(2,1)S(1)}, u32[]{:S(2)}, u32[]{:S(2)}) async-start(bf16[8,16,512]{2,1,0:T(8,128)(2,1)} %get-tuple-element.39), calls=%async_computation | async-start | bytes 262144 | tf_op jit(solution)/shard_map/all_to_all | solution.py:408
  10.7 3.3 %collective-permute-start.2 = (s32[1,8,512]{2,1,0:T(8,128)S(1)}, s32[1,8,512]{2,1,0:T(8,128)S(1)}, u32[]{:S(2)}, u32[]{:S(2)}) collective-permute-start(s32[1,8,512]{2,1,0:T(8,128)S(1)} %get-tuple-element.40.rest_0_), channel_id=1, source_target_pairs={{0,3},{1,2},{2,1},{3,0},{4,7},{5,6},{6,5},{7,4},{8,11},{9,10},{10,... | collective-permute-start | bytes 49160 | tf_op jit(solution)/shard_map/ppermute | solution.py:366
  11.4 3.9 %collective-permute-start.1 = (s32[1,8,512]{2,1,0:T(8,128)S(1)}, s32[1,8,512]{2,1,0:T(8,128)S(1)}, u32[]{:S(2)}, u32[]{:S(2)}) collective-permute-start(s32[1,8,512]{2,1,0:T(8,128)S(1)} %get-tuple-element.40.rest_0_), channel_id=1, source_target_pairs={{0,2},{1,3},{2,0},{3,1},{4,6},{5,7},{6,4},{7,5},{8,10},{9,11},{10,... | collective-permute-start | bytes 49160 | tf_op jit(solution)/shard_map/ppermute | solution.py:366
  12.3 3.0 %collective-permute-start = (s32[1,8,512]{2,1,0:T(8,128)S(1)}, s32[1,8,512]{2,1,0:T(8,128)S(1)}, u32[]{:S(2)}, u32[]{:S(2)}) collective-permute-start(s32[1,8,512]{2,1,0:T(8,128)S(1)} %get-tuple-element.40.rest_0_), channel_id=1, source_target_pairs={{0,1},{1,0},{2,3},{3,2},{4,5},{5,4},{6,7},{7,6},{8,9},{9,8},{10,11... | collective-permute-start | bytes 49160 | tf_op jit(solution)/shard_map/ppermute | solution.py:366
  30.8 15.5 %all-to-all-start.1 = ((bf16[8,104,256]{2,1,0:T(8,128)(2,1)}), bf16[8,104,256]{2,1,0:T(8,128)(2,1)S(1)}, u32[]{:S(2)}, u32[]{:S(2)}) async-start(bf16[8,104,256]{2,1,0:T(8,128)(2,1)} %get-tuple-element.41), calls=%async_computation.1 | async-start | bytes 851968 | tf_op jit(solution)/shard_map/all_to_all | solution.py:452
  39.2 36.2 %copy-start = (s32[1,8,16]{2,1,0:T(8,128)S(1)}, s32[1,8,16]{2,1,0:T(8,128)}, u32[]{:S(2)}) copy-start(s32[1,8,16]{2,1,0:T(8,128)} %idx_ref.1) | copy-start | bytes 1540
  39.2 9.6 %collective-permute-start.6 = (bf16[160,512]{1,0:T(8,128)(2,1)S(1)}, bf16[160,512]{1,0:T(8,128)(2,1)S(1)}, u32[]{:S(2)}, u32[]{:S(2)}) collective-permute-start(bf16[160,512]{1,0:T(8,128)(2,1)S(1)} %get-tuple-element.47), channel_id=1, source_target_pairs={{0,1},{1,0},{2,3},{3,2},{4,5},{5,4},{6,7},{7,6},{8,9},{9,8},{10,11... | collective-permute-start | bytes 491528 | tf_op jit(solution)/shard_map/ppermute | solution.py:366
  39.3 11.6 %collective-permute-start.7 = (bf16[160,512]{1,0:T(8,128)(2,1)S(1)}, bf16[160,512]{1,0:T(8,128)(2,1)S(1)}, u32[]{:S(2)}, u32[]{:S(2)}) collective-permute-start(bf16[160,512]{1,0:T(8,128)(2,1)S(1)} %get-tuple-element.48), channel_id=1, source_target_pairs={{0,2},{1,3},{2,0},{3,1},{4,6},{5,7},{6,4},{7,5},{8,10},{9,11},{10,... | collective-permute-start | bytes 491528 | tf_op jit(solution)/shard_map/ppermute | solution.py:366
  40.9 10.0 %collective-permute-start.8 = (bf16[160,512]{1,0:T(8,128)(2,1)S(1)}, bf16[160,512]{1,0:T(8,128)(2,1)S(1)}, u32[]{:S(2)}, u32[]{:S(2)}) collective-permute-start(bf16[160,512]{1,0:T(8,128)(2,1)S(1)} %get-tuple-element.49), channel_id=1, source_target_pairs={{0,3},{1,2},{2,1},{3,0},{4,7},{5,6},{6,5},{7,4},{8,11},{9,10},{10,... | collective-permute-start | bytes 491528 | tf_op jit(solution)/shard_map/ppermute | solution.py:366
  46.4 9.0 %collective-permute-start.5 = (bf16[96,256]{1,0:T(8,128)(2,1)S(1)}, bf16[96,256]{1,0:T(8,128)(2,1)S(1)}, u32[]{:S(2)}, u32[]{:S(2)}) collective-permute-start(bf16[96,256]{1,0:T(8,128)(2,1)S(1)} %get-tuple-element.42.after_ref), channel_id=1, source_target_pairs={{0,24},{4,28},{8,16},{12,20},{16,8},{20,12},{24,0},{28,4},{1,25},{... | collective-permute-start | bytes 147464 | tf_op jit(solution)/shard_map/ppermute | solution.py:366
  47.6 7.8 %collective-permute-start.4 = (bf16[96,256]{1,0:T(8,128)(2,1)S(1)}, bf16[96,256]{1,0:T(8,128)(2,1)S(1)}, u32[]{:S(2)}, u32[]{:S(2)}) collective-permute-start(bf16[96,256]{1,0:T(8,128)(2,1)S(1)} %get-tuple-element.42.after_ref), channel_id=1, source_target_pairs={{0,16},{4,20},{8,24},{12,28},{16,0},{20,4},{24,8},{28,12},{1,17},{... | collective-permute-start | bytes 147464 | tf_op jit(solution)/shard_map/ppermute | solution.py:366
  48.8 6.6 %collective-permute-start.3 = (bf16[96,256]{1,0:T(8,128)(2,1)S(1)}, bf16[96,256]{1,0:T(8,128)(2,1)S(1)}, u32[]{:S(2)}, u32[]{:S(2)}) collective-permute-start(bf16[96,256]{1,0:T(8,128)(2,1)S(1)} %get-tuple-element.42.after_ref), channel_id=1, source_target_pairs={{0,8},{4,12},{8,0},{12,4},{16,24},{20,28},{24,16},{28,20},{1,9},{5... | collective-permute-start | bytes 147464 | tf_op jit(solution)/shard_map/ppermute | solution.py:366
  50.9 2.2 %collective-permute-start.9 = (bf16[16,512]{1,0:T(8,128)(2,1)S(1)}, bf16[16,512]{1,0:T(8,128)(2,1)S(1)}, u32[]{:S(2)}, u32[]{:S(2)}) collective-permute-start(bf16[16,512]{1,0:T(8,128)(2,1)S(1)} %get-tuple-element.50), channel_id=1, source_target_pairs={{0,0},{1,9},{2,18},{3,27},{4,4},{5,13},{6,22},{7,31},{8,8},{9,1},{... | collective-permute-start | bytes 49160 | tf_op jit(solution)/shard_map/ppermute | solution.py:374
  51.6 3.8 %collective-permute-start.10 = (bf16[16,512]{1,0:T(8,128)(2,1)S(1)}, bf16[16,512]{1,0:T(8,128)(2,1)S(1)}, u32[]{:S(2)}, u32[]{:S(2)}) collective-permute-start(bf16[16,512]{1,0:T(8,128)(2,1)S(1)} %get-tuple-element.51), channel_id=1, source_target_pairs={{0,4},{1,13},{2,22},{3,31},{4,0},{5,9},{6,18},{7,27},{8,12},{9,5},... | collective-permute-start | bytes 49160 | tf_op jit(solution)/shard_map/ppermute | solution.py:374
  55.4 11.1 %collective-permute-start.11 = (bf16[2,96,256]{2,1,0:T(8,128)(2,1)S(1)}, bf16[2,96,256]{2,1,0:T(8,128)(2,1)S(1)}, u32[]{:S(2)}, u32[]{:S(2)}) collective-permute-start(bf16[2,96,256]{2,1,0:T(8,128)(2,1)S(1)} %pad_maximum_fusion.2), channel_id=1, source_target_pairs={{0,4},{4,0},{8,12},{12,8},{16,20},{20,16},{24,28},{28,24},{1,5},{5... | collective-permute-start | bytes 294920 | tf_op jit(solution)/shard_map/ppermute | solution.py:366
  56.9 9.0 %collective-permute-start.13 = (bf16[2,96,256]{2,1,0:T(8,128)(2,1)S(1)}, bf16[2,96,256]{2,1,0:T(8,128)(2,1)S(1)}, u32[]{:S(2)}, u32[]{:S(2)}) collective-permute-start(bf16[2,96,256]{2,1,0:T(8,128)(2,1)S(1)} %pad_maximum_fusion.3), channel_id=1, source_target_pairs={{0,2},{1,3},{2,0},{3,1},{4,6},{5,7},{6,4},{7,5},{8,10},{9,11},{10,... | collective-permute-start | bytes 294920 | tf_op jit(solution)/shard_map/ppermute | solution.py:366
  66.0 12.1 %collective-permute-start.14 = (bf16[4,96,256]{2,1,0:T(8,128)(2,1)S(1)}, bf16[4,96,256]{2,1,0:T(8,128)(2,1)S(1)}, u32[]{:S(2)}, u32[]{:S(2)}) collective-permute-start(bf16[4,96,256]{2,1,0:T(8,128)(2,1)S(1)} %pad_maximum_fusion.1.refs_1_), channel_id=1, source_target_pairs={{0,4},{4,0},{8,12},{12,8},{16,20},{20,16},{24,28},{28,24},{1,5},{5... | collective-permute-start | bytes 589832 | tf_op jit(solution)/shard_map/ppermute | solution.py:366
  66.6 11.5 %collective-permute-start.12 = (bf16[4,96,256]{2,1,0:T(8,128)(2,1)S(1)}, bf16[4,96,256]{2,1,0:T(8,128)(2,1)S(1)}, u32[]{:S(2)}, u32[]{:S(2)}) collective-permute-start(bf16[4,96,256]{2,1,0:T(8,128)(2,1)S(1)} %pad_maximum_fusion.refs_0_), channel_id=1, source_target_pairs={{0,2},{1,3},{2,0},{3,1},{4,6},{5,7},{6,4},{7,5},{8,10},{9,11},{10,... | collective-permute-start | bytes 589832 | tf_op jit(solution)/shard_map/ppermute | solution.py:366
  68.4 5.4 %collective-permute-start.17 = (bf16[48,512]{1,0:T(8,128)(2,1)S(1)}, bf16[48,512]{1,0:T(8,128)(2,1)S(1)}, u32[]{:S(2)}, u32[]{:S(2)}) collective-permute-start(bf16[48,512]{1,0:T(8,128)(2,1)S(1)} %constant_dynamic-update-slice_fusion.rest_0_), channel_id=1, source_target_pairs={{0,3},{1,2},{2,1},{3,0},{4,7},{5,6},{6,5},{7,4},{8,11},{9,10},{10,... | collective-permute-start | bytes 147464 | tf_op jit(solution)/shard_map/ppermute | solution.py:366
  68.4 6.9 %collective-permute-start.16 = (bf16[48,512]{1,0:T(8,128)(2,1)S(1)}, bf16[48,512]{1,0:T(8,128)(2,1)S(1)}, u32[]{:S(2)}, u32[]{:S(2)}) collective-permute-start(bf16[48,512]{1,0:T(8,128)(2,1)S(1)} %constant_dynamic-update-slice_fusion.rest_0_), channel_id=1, source_target_pairs={{0,2},{1,3},{2,0},{3,1},{4,6},{5,7},{6,4},{7,5},{8,10},{9,11},{10,... | collective-permute-start | bytes 147464 | tf_op jit(solution)/shard_map/ppermute | solution.py:366
  69.3 6.1 %collective-permute-start.15 = (bf16[48,512]{1,0:T(8,128)(2,1)S(1)}, bf16[48,512]{1,0:T(8,128)(2,1)S(1)}, u32[]{:S(2)}, u32[]{:S(2)}) collective-permute-start(bf16[48,512]{1,0:T(8,128)(2,1)S(1)} %constant_dynamic-update-slice_fusion.rest_0_), channel_id=1, source_target_pairs={{0,1},{1,0},{2,3},{3,2},{4,5},{5,4},{6,7},{7,6},{8,9},{9,8},{10,11... | collective-permute-start | bytes 147464 | tf_op jit(solution)/shard_map/ppermute | solution.py:366
  77.5 2.9 %collective-permute-start.19 = (bf16[4,96,256]{2,1,0:T(8,128)(2,1)S(1)}, bf16[4,96,256]{2,1,0:T(8,128)(2,1)S(1)}, u32[]{:S(2)}, u32[]{:S(2)}) collective-permute-start(bf16[4,96,256]{2,1,0:T(8,128)(2,1)S(1)} %pad_maximum_fusion.1.refs_1_), channel_id=1, source_target_pairs={{0,1},{1,0},{2,3},{3,2},{4,5},{5,4},{6,7},{7,6},{8,9},{9,8},{10,11... | collective-permute-start | bytes 589832 | tf_op jit(solution)/shard_map/ppermute | solution.py:366
  77.6 2.8 %collective-permute-start.18 = (bf16[4,96,256]{2,1,0:T(8,128)(2,1)S(1)}, bf16[4,96,256]{2,1,0:T(8,128)(2,1)S(1)}, u32[]{:S(2)}, u32[]{:S(2)}) collective-permute-start(bf16[4,96,256]{2,1,0:T(8,128)(2,1)S(1)} %pad_maximum_fusion.refs_0_), channel_id=1, source_target_pairs={{0,1},{1,0},{2,3},{3,2},{4,5},{5,4},{6,7},{7,6},{8,9},{9,8},{10,11... | collective-permute-start | bytes 589832 | tf_op jit(solution)/shard_map/ppermute | solution.py:366
  78.1 2.3 %collective-permute-start.20 = (bf16[4,96,256]{2,1,0:T(8,128)(2,1)S(1)}, bf16[4,96,256]{2,1,0:T(8,128)(2,1)S(1)}, u32[]{:S(2)}, u32[]{:S(2)}) collective-permute-start(bf16[4,96,256]{2,1,0:T(8,128)(2,1)S(1)} %collective-permute-done.12.refs_2_), channel_id=1, source_target_pairs={{0,1},{1,0},{2,3},{3,2},{4,5},{5,4},{6,7},{7,6},{8,9},{9,8},{10,11... | collective-permute-start | bytes 589832 | tf_op jit(solution)/shard_map/ppermute | solution.py:366
  78.2 2.2 %collective-permute-start.21 = (bf16[4,96,256]{2,1,0:T(8,128)(2,1)S(1)}, bf16[4,96,256]{2,1,0:T(8,128)(2,1)S(1)}, u32[]{:S(2)}, u32[]{:S(2)}) collective-permute-start(bf16[4,96,256]{2,1,0:T(8,128)(2,1)S(1)} %collective-permute-done.14.refs_3_), channel_id=1, source_target_pairs={{0,1},{1,0},{2,3},{3,2},{4,5},{5,4},{6,7},{7,6},{8,9},{9,8},{10,11... | collective-permute-start | bytes 589832 | tf_op jit(solution)/shard_map/ppermute | solution.py:366

commit v3 on v2

v3 whole, which is shorter than its diff:
```python
import functools

import jax
import jax.numpy as jnp
from jax import lax
from jax.experimental import pallas as pl
from jax.experimental.pallas import tpu as pltpu
from jax.sharding import PartitionSpec as P

NETS_BLK = 128
BF16 = jnp.bfloat16
F32 = jnp.float32
VMEM_LIMIT = 40 * 1024 * 1024


def dot_nn(a, b):
    return jnp.dot(a, b, preferred_element_type=F32)


def dot_nt(a, b):
    return lax.dot_general(a, b, (((1,), (1,)), ((), ())), preferred_element_type=F32)


def dot_tn(a, b):
    return lax.dot_general(a, b, (((0,), (0,)), ((), ())), preferred_element_type=F32)


def pick_ids(idx, part_of, slot_of):
    parts, slots = idx.shape
    lanes = part_of.shape[1]
    spread = (lax.broadcasted_iota(jnp.int32, (slots, lanes), 0) == slot_of).astype(BF16)
    high = dot_nn((idx >> 6).astype(F32).astype(BF16), spread)
    low = dot_nn((idx & 63).astype(F32).astype(BF16), spread)
    mine = lax.broadcasted_iota(jnp.int32, (parts, lanes), 0) == part_of
    return jnp.sum(jnp.where(mine, high * 64.0 + low, 0.0), axis=0, keepdims=True).astype(jnp.int32)


def slot_onehot(idx, cells):
    parts, slots = idx.shape
    lane = lax.broadcasted_iota(jnp.int32, (1, parts * slots), 1)
    return row_onehot(cells, pick_ids(idx, lane // slots, lane % slots))


def start_copies(pairs, sems):
    copies = [pltpu.make_async_copy(src, dst, sems.at[i]) for i, (src, dst) in enumerate(pairs)]
    for copy in copies:
        copy.start()
    return copies


def gather_kernel(fast, pos_ref, count_ref, idx_hbm, x_hbm, g_hbm, net_hbm, ref_hbm, ints_ref, *rest):
    *outs, idx_ref, x_ref, g_ref, net_ref, ref_ref, sems = rest
    copies = start_copies(
        [(idx_hbm, idx_ref), (x_hbm, x_ref), (g_hbm, g_ref), (net_hbm, net_ref), (ref_hbm, ref_ref)], sems
    )
    for copy in copies:
        copy.wait()
    slot_max = net_ref.shape[2]
    ints_ref[0] = jnp.broadcast_to(count_ref[...], ints_ref.shape[1:])
    ints_ref[0, :slot_max, :] = net_ref[0, 0]
    ints_ref[0, slot_max : 2 * slot_max, :] = ref_ref[0, 0]
    part_count, slots = idx_ref.shape[1:]
    cells, feat = x_ref.shape
    if fast:
        order = [pos_ref[0] ^ bits for bits in (0, 2, 4, 6, 1, 3, 5, 7)]
        idx = jnp.concatenate([idx_ref[0, pl.ds(part, 1), :] for part in order], axis=0)
        onehot = slot_onehot(idx, cells)
        for at, values in ((0, x_ref), (feat, g_ref)):
            rows = dot_tn(onehot, values[...]).astype(BF16)
            for half, out_ref in enumerate(outs):
                out_ref[:, :, at : at + feat] = rows[64 * half : 64 * (half + 1)].reshape(4, slots, feat)
        return
    (out_ref,) = outs
    group = 128 // slots
    for first in range(0, part_count, group):
        onehot = slot_onehot(idx_ref[0, first : first + group], cells)
        for at, values in ((0, x_ref), (feat, g_ref)):
            rows = dot_tn(onehot, values[...]).astype(BF16)
            out_ref[first : first + group, :, at : at + feat] = rows.reshape(group, slots, feat)


def split_bf16(x):
    high = x.astype(BF16)
    return high, (x - high.astype(F32)).astype(BF16)


def block_ids(ints_refs):
    nets, refs = [], []
    pins = ints_refs[0].shape[2]
    extra_net = jnp.zeros((1, pins), jnp.int32)
    extra_ref = jnp.zeros((1, pins), jnp.int32)
    for ints in [ref[i] for ref in ints_refs for i in range(ref.shape[0])]:
        nets.append(ints[0:1, :])
        refs.append(ints[2:3, :])
        second = ints[4:5, :] > 1
        extra_net += jnp.where(second, ints[1:2, :] + 1, 0)
        extra_ref += jnp.where(second, ints[3:4, :] + 1, 0)
    nets.append(extra_net - 1)
    refs.append(extra_ref - 1)
    return nets, refs


def row_onehot(rows, ids):
    return (lax.broadcasted_iota(jnp.int32, (rows, ids.shape[1]), 0) == ids).astype(BF16)


def column_onehot(ids, lanes):
    return (lax.broadcasted_iota(jnp.int32, (ids.shape[0], lanes), 1) == ids).astype(BF16)


def tiled_columns(ids, length):
    low = column_onehot(ids & 127, 128)
    high = jnp.broadcast_to((ids >> 7).astype(F32).astype(BF16), low.shape)
    return [jnp.where(high == t, low, jnp.zeros((), BF16)) for t in range(length // 128)]


def tiled_rows(ids, length):
    low = row_onehot(128, ids & 127)
    high = jnp.broadcast_to((ids >> 7).astype(F32).astype(BF16), low.shape)
    return [jnp.where(high == t, low, jnp.zeros((), BF16)) for t in range(length // 128)]


def net_inverse(pin_net):
    return 1.0 / jnp.maximum(jnp.sum(pin_net.astype(F32), axis=1, keepdims=True), 1.0)


def id_columns(ids, wide):
    wide[...] = jnp.zeros_like(wide)
    wide[:16, :] = ids[...]
    return wide[...].T.astype(jnp.int32)


def spread_kernel(fast, slots, pos_ref, *refs):
    ints_refs, refs = refs[:-18], refs[-18:]
    w_in_hbm, w_net_hbm, bias_hbm, w_out_hbm, ids_hbm, *refs = refs
    at_pin, at_row, net_pin, pin_net, edge_pin, w_in_ref, w_net_ref, bias_ref, w_out_ref, *refs = refs
    ids, wide, sems, out_sem = refs
    cells = at_pin.shape[1]
    hid = w_in_ref.shape[1]
    pins = ids.shape[1]
    table_len = at_row.shape[0]
    mine = pl.ds(pl.multiple_of(pos_ref[1] * hid, hid), hid)
    copies = start_copies(
        [
            (w_in_hbm.at[:, mine], w_in_ref),
            (w_net_hbm.at[:, mine], w_net_ref),
            (bias_hbm.at[:, mine], bias_ref),
            (w_out_hbm.at[mine, :], w_out_ref),
        ],
        sems,
    )
    nets, refs = block_ids(ints_refs)
    blocks = len(nets)
    if fast:
        refs = [jnp.where(row < cells, row, ((row - cells) ^ (pos_ref[0] * slots)) + cells) for row in refs]
    ids[...] = jnp.zeros_like(ids)
    for b in range(blocks):
        ids[b : b + 1, :] = nets[b].astype(F32)
        ids[8 + b : 9 + b, :] = refs[b].astype(F32)
    outgoing = pltpu.make_async_copy(ids, ids_hbm, out_sem)
    outgoing.start()
    columns = id_columns(ids, wide)
    for b in range(blocks):
        of = slice(b * pins, (b + 1) * pins)
        as_columns, as_rows = tiled_columns(columns[:, 8 + b : 9 + b], table_len), tiled_rows(refs[b], table_len)
        for t, (tile_column, tile_row) in enumerate(zip(as_columns, as_rows)):
            if t < cells // 128:
                at_pin[of, t * 128 : (t + 1) * 128] = tile_column
            else:
                edge_pin[of, t * 128 - cells : (t + 1) * 128 - cells] = tile_column
            at_row[t * 128 : (t + 1) * 128, of] = tile_row
        net_pin[of, :] = column_onehot(columns[:, b : b + 1], NETS_BLK)
        pin_net[:, of] = row_onehot(NETS_BLK, nets[b])
    for copy in copies:
        copy.wait()
    outgoing.wait()


def own_pins_kernel(after_ref, at_pin, x_hbm, g_hbm, taken, table, sems):
    feat = x_hbm.shape[1]
    copies = start_copies([(x_hbm, table.at[:, :feat]), (g_hbm, table.at[:, feat:])], sems)
    for copy in copies:
        copy.wait()
    taken[...] = dot_nn(at_pin[...], table[...]).astype(BF16)


def layer_kernel(fast, halos, *refs):
    halo_refs, refs = refs[:halos], refs[halos:]
    at_row, net_pin, pin_net, edge_pin, w_in_ref, w_net_ref, bias_ref, w_out_ref, local_taken, *refs = refs
    x_hbm, g_hbm, grads_ref, sums_hbm, net_grads_hbm, *refs = refs
    table, sems, sums, net_grads, out_sems, taken, net_feats, terms = refs
    cells, feat = x_hbm.shape
    hid = w_in_ref.shape[1]
    table_len, pin_count = at_row.shape
    blocks = net_grads.shape[0] // NETS_BLK
    pins = pin_count // blocks
    copies = start_copies([(x_hbm, table.at[:cells, :feat]), (g_hbm, table.at[:cells, feat:])], sems)
    at = cells
    for ref in halo_refs:
        for part in range(ref.shape[0]):
            table[at : at + ref.shape[1], :] = ref[part]
            at += ref.shape[1]
    for b in range(blocks):
        of = slice(b * pins, (b + 1) * pins)
        nets_of = slice(b * NETS_BLK, (b + 1) * NETS_BLK)
        edge = dot_nn(edge_pin[of, :], table[cells:, :])
        taken[of, :] = (edge + local_taken[of, :].astype(F32)).astype(BF16)
        net_sum = dot_nn(pin_net[:, of], taken[of, :feat])
        net_feats[nets_of, :] = (net_sum * net_inverse(pin_net[:, of])).astype(BF16)
    net_pre = dot_nn(net_feats[...], w_net_ref[...]).astype(BF16)
    scale = 0.7978845608028654
    for b in range(blocks):
        of = slice(b * pins, (b + 1) * pins)
        nets_of = slice(b * NETS_BLK, (b + 1) * NETS_BLK)
        pre = dot_nn(taken[of, :feat], w_in_ref[...]) + dot_nn(net_pin[of, :], net_pre[nets_of]) + bias_ref[...]
        pulled = dot_nt(taken[of, feat:], w_out_ref[...])
        square = pre * pre
        bend = jnp.tanh(pre * (scale + (scale * 0.044715) * square))
        half = 0.5 * bend + 0.5
        terms[of, :hid] = (pre * half).astype(BF16)
        slope = half + (0.5 * pre) * (1.0 - bend * bend) * (scale + (3 * scale * 0.044715) * square)
        pre_grad = (pulled * slope).astype(BF16)
        terms[of, hid:] = pre_grad
        net_grads[nets_of, :] = dot_nn(pin_net[:, of], pre_grad).astype(BF16)
    sums[...] = dot_nn(at_row[...], terms[...])
    outgoing = start_copies([(sums, sums_hbm), (net_grads, net_grads_hbm)], out_sems)
    hidden_high, hidden_low = split_bf16(sums[:, :hid])
    grad_high, grad_low = split_bf16(sums[:, hid:])
    for copy in copies:
        copy.wait()
    table_x, table_g = table[:, :feat], table[:, feat:]
    acc_in = dot_tn(table_x, grad_high) + dot_tn(table_x, grad_low)
    acc_out = dot_tn(hidden_high, table_g) + dot_tn(hidden_low, table_g)
    acc_net = dot_tn(net_feats[...], net_grads[...])
    acc_bias = jnp.broadcast_to(jnp.sum(sums[:, hid:], axis=0, keepdims=True), (8, hid))
    if fast:
        part_count, rows, _ = grads_ref.shape
        part = feat // part_count
        for to in range(part_count):
            of = slice(to * part, (to + 1) * part)
            blocks_of = [acc_in[of, :], acc_net[of, :], acc_out[of, :], acc_bias]
            grads_ref[to] = jnp.concatenate([x.astype(BF16) for x in blocks_of], axis=0)
    else:
        grads_ref[:feat, :] = acc_in
        grads_ref[feat : 2 * feat, :] = acc_net
        grads_ref[2 * feat : 2 * feat + hid, :] = acc_out
        grads_ref[2 * feat + hid :, :] = acc_bias
    for copy in outgoing:
        copy.wait()


def back_kernel(fast, pos_ref, ids_hbm, sums_hbm, net_grads_hbm, w_in_hbm, w_net_hbm, w_out_hbm, *rest):
    *outs, ids, wide, sums, net_grads, w_in_ref, w_net_ref, w_out_ref, sems, at_row, net_backs, acc = rest
    table_len = acc.shape[0]
    feat, hid = w_in_ref.shape
    blocks = net_grads.shape[0] // NETS_BLK
    pins = ids.shape[1]
    mine = pl.ds(pl.multiple_of(pos_ref[1] * hid, hid), hid)
    copies = start_copies(
        [
            (ids_hbm, ids),
            (net_grads_hbm, net_grads),
            (w_net_hbm.at[:, mine], w_net_ref),
            (w_in_hbm.at[:, mine], w_in_ref),
            (w_out_hbm.at[mine, :], w_out_ref),
            (sums_hbm, sums),
        ],
        sems,
    )
    copies[0].wait()
    columns = id_columns(ids, wide)
    rows = ids[...].astype(jnp.int32)
    for b in range(blocks):
        of = slice(b * pins, (b + 1) * pins)
        for t, tile in enumerate(tiled_rows(rows[8 + b : 9 + b, :], table_len)):
            at_row[t * 128 : (t + 1) * 128, of] = tile
    for copy in copies[1:3]:
        copy.wait()
    for b in range(blocks):
        of = slice(b * pins, (b + 1) * pins)
        nets_of = slice(b * NETS_BLK, (b + 1) * NETS_BLK)
        inverse = net_inverse(row_onehot(NETS_BLK, rows[b : b + 1, :]))
        feat_grad = (dot_nt(net_grads[nets_of, :], w_net_ref[...]) * inverse).astype(BF16)
        net_backs[of, :] = dot_nn(column_onehot(columns[:, b : b + 1], NETS_BLK), feat_grad).astype(BF16)
    for copy in copies[3:]:
        copy.wait()
    hidden_high, hidden_low = split_bf16(sums[:, :hid])
    grad_high, grad_low = split_bf16(sums[:, hid:])
    acc[:, :feat] = dot_nn(hidden_high, w_out_ref[...]) + dot_nn(hidden_low, w_out_ref[...])
    acc[:, feat:] = (
        dot_nt(grad_high, w_in_ref[...]) + dot_nt(grad_low, w_in_ref[...]) + dot_nn(at_row[...], net_backs[...])
    )
    if fast:
        own_ref, far_ref, twin_ref = outs
        length = own_ref.shape[0]
        cells = table_len - 128
        share = cells // 4
        edges = acc[cells:, :].astype(BF16)
        row = lax.broadcasted_iota(jnp.int32, (length - share, 128), 0)
        lane = lax.broadcasted_iota(jnp.int32, row.shape, 1)
        for bits, ref, at in ((0, own_ref, 0), (2, far_ref, 0), (1, twin_ref, 0), (3, twin_ref, length)):
            to = pos_ref[1] ^ bits
            rows = acc[pl.ds(pl.multiple_of(to * share, share), share), :]
            ref[at : at + share, :] = rows.astype(ref.dtype)
            of = lane == ((row >> 2) * 16 + to * 4 + (row & 3))
            ref[at + share : at + length, :] = dot_nn(of.astype(BF16), edges).astype(ref.dtype)
        return
    own_ref, send_ref = outs
    cells = own_ref.shape[0]
    own_ref[...] = acc[:cells, :]
    part_count, rows, _ = send_ref.shape
    slots = rows // 2
    for part in range(part_count):
        of = slice(cells + part * slots, cells + (part + 1) * slots)
        send_ref[part, :slots, :] = acc[of, :feat].astype(BF16)
        send_ref[part, slots:, :] = acc[of, feat:].astype(BF16)


def pair_kernel(own_ref, far_ref, twin_ref, own_sum_ref, far_sum_ref):
    length = own_ref.shape[0]
    own_sum_ref[...] = own_ref[...] + twin_ref[:length, :].astype(F32)
    far_sum_ref[...] = (far_ref[...] + twin_ref[length:, :].astype(F32)).astype(BF16)


def sum_kernel(got_ref, own_ref, *rest):
    far_ref, *payloads, rows_ref, bias_ref = rest
    total = own_ref[...] + far_ref[...].astype(F32)
    share, wide = rows_ref.shape
    feat = wide // 2
    rows_ref[...] = total[:share]
    piece = got_ref[0].astype(F32)
    for part in range(1, got_ref.shape[0]):
        piece += got_ref[part].astype(F32)
    rows = piece.shape[0] - 8
    bias_ref[...] = jnp.concatenate([piece[rows:]] * 2, axis=0).astype(BF16)
    for k, payload in enumerate(payloads):
        edges = []
        for odd in range(2):
            at = share + 4 * (2 * k + odd)
            edges += [total[at : at + 4, :feat], total[at : at + 4, feat:]]
        payload[...] = jnp.concatenate([piece[:rows]] + edges, axis=0).astype(BF16)


def place(pos_ref, parts, outs, buffer, sems):
    rows, hid = buffer.shape[1:]
    part = rows // 3
    copies = []
    for at, (ref, start, cell_bits, net_bits) in enumerate(parts):
        row = pl.multiple_of((pos_ref[0] ^ cell_bits) * part, part)
        first = pl.multiple_of((pos_ref[1] ^ net_bits) * hid, hid)
        buffer[at] = ref[start : start + rows, :].astype(F32)
        targets = [
            outs[0].at[pl.ds(row, part), pl.ds(first, hid)],
            outs[1].at[pl.ds(row, part), pl.ds(first, hid)],
            outs[2].at[pl.ds(pl.multiple_of(first + row, part), part), :],
        ]
        for matrix, target in enumerate(targets):
            source = buffer.at[at, matrix * part : (matrix + 1) * part, :]
            copies.append(pltpu.make_async_copy(source, target, sems.at[3 * at + matrix]))
            copies[-1].start()
    return copies


def place_kernel(tags, olds, pos_ref, *refs):
    ins, refs = refs[: len(tags)], refs[len(tags) + olds :]
    outs, (buffer, sems) = refs[:3], refs[3:]
    parts = [(ref,) + tag for ref, some in zip(ins, tags) for tag in some]
    for copy in place(pos_ref, parts, outs, buffer, sems):
        copy.wait()


def edge_rows(edges):
    return jnp.concatenate([edge[:64, :] for edge in edges], axis=0)


def first_kernel(tags, pos_ref, idx_ref, x_hbm, g_hbm, rows_ref, *refs):
    ins, refs = refs[: len(tags)], refs[len(tags) :]
    edges, refs = refs[:2], refs[2:]
    grads, (total_ref, pick_y_ref, pick_x_ref, buffer, sems, x_ref, g_ref, row_sems) = refs[:3], refs[3:]
    share, wide = rows_ref.shape
    feat = wide // 2
    cell, net = pos_ref[0], pos_ref[1]
    mine = pl.ds(pl.multiple_of(net * share, share), share)
    copies = start_copies([(x_hbm.at[mine, :], x_ref), (g_hbm.at[mine, :], g_ref)], row_sems)
    parts = [(ref,) + tag for ref, some in zip(ins, tags) for tag in some]
    placed = place(pos_ref, parts, grads, buffer, sems)
    lane = lax.broadcasted_iota(jnp.int32, (1, 256), 1)
    bits, source, is_back, slot = lane >> 6, (lane >> 3) & 7, (lane >> 2) & 1, lane & 3
    part_of = cell ^ (((source & 3) << 1) | (source >> 2))
    ids = pick_ids(idx_ref[0], part_of, ((net ^ bits) << 2) | slot) - net * share
    pick_y = row_onehot(share, jnp.where(is_back == 0, ids, -1))
    pick_x = row_onehot(share, jnp.where(is_back == 1, ids, -1))
    pick_y_ref[...] = pick_y[:, 128:]
    pick_x_ref[...] = pick_x[:, 128:]
    halo = edge_rows(edges)
    for copy in copies:
        copy.wait()
    total_ref[:, :feat] = x_ref[...].astype(F32) + rows_ref[:, :feat] + dot_nn(pick_y[:, :128], halo)
    total_ref[:, feat:] = g_ref[...].astype(F32) + rows_ref[:, feat:] + dot_nn(pick_x[:, :128], halo)
    for copy in placed:
        copy.wait()


def finish_kernel(tags, pos_ref, total_ref, pick_y_ref, pick_x_ref, *refs):
    ins, refs = refs[: len(tags)], refs[len(tags) :]
    edges, refs = refs[:4], refs[4 + 3 :]
    grads, (updated_ref, back_ref, bias_ref, buffer, sems) = refs[:3], refs[3:]
    feat = updated_ref.shape[1]
    parts = [(ref,) + tag for ref, some in zip(ins, tags) for tag in some]
    placed = place(pos_ref, parts, grads, buffer, sems)
    halo = edge_rows(edges[2:])
    updated_ref[...] = (total_ref[:, :feat] + dot_nn(pick_y_ref[...], halo)).astype(BF16)
    back_ref[...] = (total_ref[:, feat:] + dot_nn(pick_x_ref[...], halo)).astype(BF16)
    for bits, edge in enumerate(edges):
        at = pl.multiple_of((pos_ref[1] ^ bits) * feat, feat)
        bias_ref[:, pl.ds(at, feat)] = edge[64:, :].astype(F32)[:1]
    for copy in placed:
        copy.wait()


def combine_kernel(pos_ref, idx_ref, got_ref, own_ref, *outs):
    part_count, slots = idx_ref.shape[1:]
    cells, wide = own_ref.shape
    feat = wide // 2
    group = 128 // slots
    rows_y = own_ref[:, :feat]
    rows_x = own_ref[:, feat:]
    for first in range(0, part_count, group):
        onehot = slot_onehot(idx_ref[0, first : first + group], cells)
        y = got_ref[first : first + group, :slots, :].reshape(128, feat)
        x = got_ref[first : first + group, slots:, :].reshape(128, feat)
        rows_y += dot_nn(onehot, y)
        rows_x += dot_nn(onehot, x)
    *shares, scratch = outs
    scratch[:, :feat] = rows_y
    scratch[:, feat:] = rows_x
    share = cells // len(shares)
    for bits, share_ref in enumerate(shares):
        at = pl.multiple_of((pos_ref[1] ^ bits) * share, share)
        share_ref[...] = scratch[pl.ds(at, share), :].astype(share_ref.dtype)


def plain_rows_kernel(pos_ref, x_hbm, g_hbm, own_ref, *rest):
    *others, updated_ref, back_ref, x_ref, g_ref, sems = rest
    share, feat = updated_ref.shape
    mine = pl.ds(pl.multiple_of(pos_ref[1] * share, share), share)
    copies = start_copies([(x_hbm.at[mine, :], x_ref), (g_hbm.at[mine, :], g_ref)], sems)
    total = own_ref[...]
    for other in others:
        total += other[...].astype(F32)
    for copy in copies:
        copy.wait()
    updated_ref[...] = (x_ref[...].astype(F32) + total[:, :feat]).astype(BF16)
    back_ref[...] = (g_ref[...].astype(F32) + total[:, feat:]).astype(BF16)


def whole(count):
    return [pl.BlockSpec(memory_space=pltpu.VMEM)] * count


SMEM = pl.BlockSpec(memory_space=pltpu.SMEM)
HBM = pl.BlockSpec(memory_space=pltpu.HBM)
PARAMS = dict(compiler_params=pltpu.CompilerParams(vmem_limit_bytes=VMEM_LIMIT))


def about(microseconds):
    return pl.CostEstimate(flops=0, transcendentals=0, bytes_accessed=int(microseconds * 3.6e6))


def in_hbm(*arrays):
    return [pltpu.with_memory_space_constraint(x, pltpu.HBM) for x in arrays]


def flip(x, axis, bits):
    size = lax.axis_size(axis)
    return lax.ppermute(x, axis, [(i, i ^ bits) for i in range(size)])


def both(x, cell_bits, net_bits):
    parts, group = lax.axis_size("cell"), lax.axis_size("net")
    pairs = [
        (c * group + n, (c ^ cell_bits(n)) * group + (n ^ net_bits)) for c in range(parts) for n in range(group)
    ]
    return lax.ppermute(x, ("cell", "net"), pairs)


def local(cell_feat, out_grad, w_in, w_net, bias, w_out, send_idx, pin_net, pin_ref, block_count):
    part_count = lax.axis_size("cell")
    group_size = lax.axis_size("net")
    cells, feat = cell_feat.shape
    hidden_dim = w_in.shape[1]
    hid = hidden_dim // group_size
    slots = send_idx.shape[2]
    pins = pin_net.shape[3]
    table_len = cells + part_count * slots
    fast = part_count == 8 and group_size == 4
    pos = jnp.stack([lax.axis_index("cell"), lax.axis_index("net")]).astype(jnp.int32)

    def shape(dtype, *dims):
        return jax.ShapeDtypeStruct(dims, dtype)

    if fast:
        sent_shape = [shape(BF16, 4, slots, 2 * feat)] * 2
    else:
        sent_shape = [shape(BF16, part_count, slots, 2 * feat)]
    ints, *sent = pl.pallas_call(
        functools.partial(gather_kernel, fast),
        in_specs=[SMEM] + whole(1) + [HBM] * 5,
        out_specs=whole(1 + len(sent_shape)),
        out_shape=[shape(jnp.int32, 1, 8, pins)] + sent_shape,
        scratch_shapes=[
            pltpu.VMEM(send_idx.shape, jnp.int32),
            pltpu.VMEM((cells, feat), BF16),
            pltpu.VMEM((cells, feat), BF16),
            pltpu.VMEM(pin_net.shape, jnp.int32),
            pltpu.VMEM(pin_ref.shape, jnp.int32),
            pltpu.SemaphoreType.DMA((5,)),
        ],
        name="take_boundary",
        cost_estimate=about(2.0),
        **PARAMS,
    )(pos, block_count, *in_hbm(send_idx, cell_feat, out_grad, pin_net, pin_ref))
    if fast:
        keep, cross = sent
        all_ints = [ints] + [flip(ints, "net", bits) for bits in range(1, group_size)]
        cross = flip(cross, "cell", 1)
        near = [jnp.stack([keep[k], cross[k]]) for k in range(4)]
        near, all_ints = lax.optimization_barrier((near, all_ints))
        halo = [near[0]] + [flip(near[k], "cell", 2 * k) for k in (1, 2, 3)]
    else:
        halo = [lax.all_to_all(sent[0], "cell", split_axis=0, concat_axis=0, tiled=True)]
        all_ints = [lax.all_gather(ints, "net", tiled=True)]

    blocks = group_size + 1
    part = feat // part_count
    share = cells // group_size
    edge = part_count * slots // group_size
    all_pins = blocks * pins
    spread_shape = [
        shape(BF16, all_pins, cells),
        shape(BF16, table_len, all_pins),
        shape(BF16, all_pins, NETS_BLK),
        shape(BF16, NETS_BLK, all_pins),
        shape(BF16, all_pins, table_len - cells),
        shape(BF16, feat, hid),
        shape(BF16, feat, hid),
        shape(F32, 1, hid),
        shape(BF16, hid, feat),
    ]
    ids, at_pin, *spread = pl.pallas_call(
        functools.partial(spread_kernel, fast, slots),
        in_specs=[SMEM] + whole(len(all_ints)) + [HBM] * 4,
        out_specs=[HBM] + whole(9),
        out_shape=[pltpu.HBM((16, pins), F32)] + spread_shape,
        scratch_shapes=[
            pltpu.VMEM((16, pins), F32),
            pltpu.VMEM((128, pins), F32),
            pltpu.SemaphoreType.DMA((4,)),
            pltpu.SemaphoreType.DMA,
        ],
        name="spread",
        cost_estimate=about(4.5),
        **PARAMS,
    )(pos, *all_ints, *in_hbm(w_in, w_net, bias.reshape(1, hidden_dim), w_out))
    taken = pl.pallas_call(
        own_pins_kernel,
        in_specs=[pl.BlockSpec(memory_space=pl.ANY)] + whole(1) + [HBM] * 2,
        out_specs=whole(1)[0],
        out_shape=shape(BF16, all_pins, 2 * feat),
        scratch_shapes=[pltpu.VMEM((cells, 2 * feat), BF16), pltpu.SemaphoreType.DMA((2,))],
        name="own_pins",
        cost_estimate=about(2.5),
        **PARAMS,
    )(halo[0], at_pin, *in_hbm(cell_feat, out_grad))

    grads, sums, net_grads = pl.pallas_call(
        functools.partial(layer_kernel, fast, len(halo)),
        in_specs=whole(len(halo) + 9) + [HBM] * 2,
        out_specs=whole(1) + [HBM] * 2,
        out_shape=[
            shape(BF16, part_count, 3 * part + 8, feat) if fast else shape(F32, 2 * feat + hid + 8, hid),
            pltpu.HBM((table_len, 2 * hid), F32),
            pltpu.HBM((blocks * NETS_BLK, hid), BF16),
        ],
        scratch_shapes=[
            pltpu.VMEM((table_len, 2 * feat), BF16),
            pltpu.SemaphoreType.DMA((2,)),
            pltpu.VMEM((table_len, 2 * hid), F32),
            pltpu.VMEM((blocks * NETS_BLK, hid), BF16),
            pltpu.SemaphoreType.DMA((2,)),
            pltpu.VMEM((all_pins, 2 * feat), BF16),
            pltpu.VMEM((blocks * NETS_BLK, feat), BF16),
            pltpu.VMEM((all_pins, 2 * hid), BF16),
        ],
        name="layer",
        cost_estimate=about(7.7),
        **PARAMS,
    )(*halo, *spread, taken, *in_hbm(cell_feat, out_grad))

    if fast:
        got = lax.all_to_all(grads, "cell", split_axis=0, concat_axis=0, tiled=True)
        length = share + edge
        out_shape = [shape(F32, length, 2 * feat)] * 2 + [shape(BF16, 2 * length, 2 * feat)]
    else:
        out_shape = [shape(F32, cells, 2 * feat), shape(BF16, part_count, 2 * slots, feat)]
    outs = pl.pallas_call(
        functools.partial(back_kernel, fast),
        in_specs=[SMEM] + [HBM] * 6,
        out_specs=whole(len(out_shape)),
        out_shape=out_shape,
        scratch_shapes=[
            pltpu.VMEM((16, pins), F32),
            pltpu.VMEM((128, pins), F32),
            pltpu.VMEM((table_len, 2 * hid), F32),
            pltpu.VMEM((blocks * NETS_BLK, hid), BF16),
            pltpu.VMEM((feat, hid), BF16),
            pltpu.VMEM((feat, hid), BF16),
            pltpu.VMEM((hid, feat), BF16),
            pltpu.SemaphoreType.DMA((6,)),
            pltpu.VMEM((table_len, blocks * pins), BF16),
            pltpu.VMEM((blocks * pins, feat), BF16),
            pltpu.VMEM((table_len, 2 * feat), F32),
        ],
        name="back",
        cost_estimate=about(4.6),
        **PARAMS,
    )(pos, *in_hbm(ids, sums, net_grads, w_in, w_net, w_out))

    row_shapes = [shape(BF16, share, feat)] * 2
    row_scratch = [
        pltpu.VMEM((share, feat), BF16),
        pltpu.VMEM((share, feat), BF16),
        pltpu.SemaphoreType.DMA((2,)),
    ]
    grad_shapes = [shape(F32, feat, hidden_dim), shape(F32, feat, hidden_dim), shape(F32, hidden_dim, feat)]
    if not fast:
        own, send = outs
        got = lax.all_to_all(send, "cell", split_axis=0, concat_axis=0, tiled=True)
        shares = pl.pallas_call(
            combine_kernel,
            in_specs=[SMEM] + whole(3),
            out_specs=whole(group_size),
            out_shape=[shape(BF16 if bits else F32, share, 2 * feat) for bits in range(group_size)],
            scratch_shapes=[pltpu.VMEM((cells, 2 * feat), F32)],
            name="combine",
            **PARAMS,
        )(pos, send_idx, got, own)
        others = [flip(shares[bits], "net", bits) for bits in range(1, group_size)]
        updated, cell_grad = pl.pallas_call(
            plain_rows_kernel,
            in_specs=[SMEM] + [HBM] * 2 + whole(group_size),
            out_specs=whole(2),
            out_shape=row_shapes,
            scratch_shapes=row_scratch,
            name="own_rows",
            **PARAMS,
        )(pos, *in_hbm(cell_feat, out_grad), shares[0], *others)
        summed = lax.all_gather(lax.psum(grads, "cell"), "net")
        grad_in = jnp.moveaxis(summed[:, :feat], 0, 1).reshape(feat, hidden_dim)
        grad_net = jnp.moveaxis(summed[:, feat : 2 * feat], 0, 1).reshape(feat, hidden_dim)
        grad_out = summed[:, 2 * feat : 2 * feat + hid].reshape(hidden_dim, feat)
        grad_bias = summed[:, 2 * feat + hid].reshape(hidden_dim)
        return (updated, cell_grad, grad_in, grad_net, grad_bias, grad_out)

    own, far, twin_share = outs
    own, far = pl.pallas_call(
        pair_kernel,
        in_specs=whole(3),
        out_specs=whole(2),
        out_shape=[shape(F32, length, 2 * feat), shape(BF16, length, 2 * feat)],
        name="pairs",
        **PARAMS,
    )(own, far, flip(twin_share, "net", 1))
    rows_of = 3 * part
    *pays, rows, bias_sum = pl.pallas_call(
        sum_kernel,
        in_specs=whole(3),
        out_specs=whole(6),
        out_shape=[shape(BF16, rows_of + 16, feat)] * 4 + [shape(F32, share, 2 * feat), shape(BF16, 16, feat)],
        name="sums",
        cost_estimate=about(0.2),
        **PARAMS,
    )(got, own, flip(far, "net", 2))
    near = [pays[0]] + [flip(pays[k], "cell", 2 * k) for k in (1, 2, 3)]
    across = flip(jnp.concatenate(near[:2] + [a[rows_of:] for a in near[2:]]), "cell", 1)
    second = jnp.concatenate([a[:rows_of] for a in near[2:]])
    second = jnp.concatenate([second, flip(second, "net", 2)])
    starts = [rows_of, 2 * rows_of + 16, 2 * rows_of + 32, 2 * rows_of + 48]
    edges = [a[rows_of : rows_of + 8] for a in near] + [across[at + 8 : at + 16] for at in starts]
    full = rows_of + 16
    pieces = [near[0][:rows_of], near[1][:rows_of], across[:rows_of], across[full : full + rows_of]]
    first = jnp.concatenate(pieces + edges + [bias_sum])
    early = [flip(first, "net", 1), flip(second, "net", 1)]
    third, fourth = flip(first, "net", 2), flip(second, "cell", 1)
    first_tag = [(0, 0, 0), (rows_of, 2, 0), (2 * rows_of, 1, 0), (3 * rows_of, 3, 0)]
    second_tag = [(0, 4, 0), (rows_of, 6, 0), (2 * rows_of, 4, 2), (3 * rows_of, 6, 2)]
    early_tags = [first_tag, second_tag]
    late_tags = [[(at, c, n ^ 2) for at, c, n in first_tag], [(at, c ^ 1, n) for at, c, n in second_tag]]

    def twin(tags):
        return [[(at, c, n ^ 1) for at, c, n in tag] for tag in tags]

    def scratch(arrays):
        return [pltpu.VMEM((4 * len(arrays), rows_of, hid), F32), pltpu.SemaphoreType.DMA((12 * len(arrays),))]

    *grads, total, pick_y, pick_x = pl.pallas_call(
        functools.partial(first_kernel, early_tags + twin(early_tags)),
        in_specs=[SMEM] + whole(1) + [HBM] * 2 + whole(1 + 4 + 2),
        out_specs=[HBM] * 3 + whole(3),
        out_shape=grad_shapes + [shape(F32, share, 2 * feat)] + [shape(BF16, share, 128)] * 2,
        scratch_shapes=scratch([0] * 4) + row_scratch,
        name="first_pieces",
        **PARAMS,
    )(pos, send_idx, *in_hbm(cell_feat, out_grad), rows, first, second, *early, first[4 * rows_of :], early[0][4 * rows_of :])
    third, fourth, grads = lax.optimization_barrier((third, fourth, grads))
    late = [flip(third, "net", 1), flip(fourth, "net", 1)]
    grads = pl.pallas_call(
        functools.partial(place_kernel, late_tags, 3),
        in_specs=[SMEM] + whole(2) + [HBM] * 3,
        out_specs=[HBM] * 3,
        out_shape=grad_shapes,
        scratch_shapes=scratch(late),
        input_output_aliases={3 + i: i for i in range(3)},
        name="place",
        **PARAMS,
    )(pos, third, fourth, *grads)
    all_edges = [a[4 * rows_of :] for a in (first, early[0], third, late[0])]
    grad_in, grad_net, grad_out, updated, cell_grad, grad_bias = pl.pallas_call(
        functools.partial(finish_kernel, twin(late_tags)),
        in_specs=[SMEM] + whole(3 + 2 + 4) + [HBM] * 3,
        out_specs=[HBM] * 3 + whole(3),
        out_shape=grad_shapes + row_shapes + [shape(F32, 1, hidden_dim)],
        scratch_shapes=scratch(late),
        input_output_aliases={4 + 2 + 4 + i: i for i in range(3)},
        name="finish",
        **PARAMS,
    )(pos, total, pick_y, pick_x, *late, *all_edges, *grads)
    return (updated, cell_grad, grad_in, grad_net, grad_bias.reshape(hidden_dim), grad_out)


def solution(mesh):
    placed = (
        P("cell", None),
        P("cell", None),
        P(),
        P(),
        P(),
        P(),
        P("cell", None, None),
        P("cell", "net", None, None),
        P("cell", "net", None, None),
        P("cell", "net"),
    )
    return jax.shard_map(
        local,
        mesh=mesh,
        in_specs=placed,
        out_specs=(P(("cell", "net"), None), P(("cell", "net"), None), P(), P(), P(), P()),
        check_vma=False,
    )
```

time: 82.7 us -> 77.3 us (0.935)
  starting transfers between devices: 33.5 us -> 27.4 us
    ppermute x20, waiting for transfers between devices: 11.4 us -> 21.7 us  [flip(): return lax.ppermute(x, axis, [(i, i ^ bits) for i in range(size)])]
    all_to_all x1 -> x0, starting transfers between devices: 7.26 us -> none  [local(): halo = lax.all_to_all(sent, 'cell', split_axis=0, concat_axis=0, tiled=True)]
    all_to_all x1, waiting for transfers between devices: 5.21 us -> 0.01 us  [local(): got = lax.all_to_all(grads, 'cell', split_axis=0, concat_axis=0, tiled=True)]
    all_to_all x1 -> x0, waiting for transfers between devices: 2.76 us -> none  [local(): halo = lax.all_to_all(sent, 'cell', split_axis=0, concat_axis=0, tiled=True)]
    ppermute x2 -> x0, waiting for transfers between devices: 2.32 us -> none  [both(): return lax.ppermute(x, ('cell', 'net'), pairs)]
    ppermute x2 -> x0, starting transfers between devices: 2.15 us -> none  [both(): return lax.ppermute(x, ('cell', 'net'), pairs)]
    all_to_all x1, starting transfers between devices: 3.66 us -> 5.63 us  [local(): got = lax.all_to_all(grads, 'cell', split_axis=0, concat_axis=0, tiled=True)]
    ppermute x20, starting transfers between devices: 20.5 us -> 21.7 us  [flip(): return lax.ppermute(x, axis, [(i, i ^ bits) for i in range(size)])]
  transfers between devices with their start and end apart: 24 -> 21, of which waited for: 8 -> 8; matrix products, arithmetic and copies ran while one was open for 0% -> 0% of each run, Pallas kernels for 11% -> 18%
where the time goes in v3:
time: 77.3 us; the launch traced here: 76.9 us
  starting transfers between devices  27.4 us (35%)
  Pallas kernels  25.9 us (34%)
  waiting for transfers between devices  21.7 us (28%)
  between operations  1.72 us (2%)
    ppermute x20, starting transfers between devices, flip(): return lax.ppermute(x, axis, [(i, i ^ bits) for i in range(size)])  21.7 us
    ppermute x20, waiting for transfers between devices, flip(): return lax.ppermute(x, axis, [(i, i ^ bits) for i in range(size)])  21.7 us
    pallas_call x1, Pallas kernels, local(): pl.pallas_call(functools.partial(layer_kernel, fast, len(halo)), in_specs...  7.69 us
    all_to_all x1, starting transfers between devices, local(): got = lax.all_to_all(grads, 'cell', split_axis=0, concat_axis=0, tiled=True)  5.63 us
    pallas_call x1, Pallas kernels, local(): pl.pallas_call(functools.partial(back_kernel, fast), in_specs=[SMEM] + [H...  4.47 us
    pallas_call x1, Pallas kernels, local(): pl.pallas_call(functools.partial(spread_kernel, fast, slots), in_specs=[S...  2.68 us
    pallas_call x1, Pallas kernels, local(): pl.pallas_call(own_pins_kernel, in_specs=[pl.BlockSpec(memory_space=pl.AN...  2.57 us
    pallas_call x1, Pallas kernels, local(): pl.pallas_call(functools.partial(first_kernel, early_tags + twin(early_ta...  2.42 us
  transfers between devices with their start and end apart: 21, of which 8 were waited for; matrix products, arithmetic and copies ran while one was open for 0% of the time, Pallas kernels for 18%

profile of v3, /device:TPU:0, one launch (start us, length us, event | category | flops | bytes accessed | tf_op | source)
XLA Modules:
  0.0 76.9 jit_solution(10898913481111711151)
XLA Ops:
  1.3 0.1 pad_add_fusion.pos_ref
  1.4 2.0 %take_boundary.1 = (s32[1,8,512]{2,1,0:T(8,128)S(1)}, bf16[4,16,512]{2,1,0:T(8,128)(2,1)S(1)}, bf16[4,16,512]{2,1,0:T(8,128)(2,1)S(1)}) custom-call(s32[2]{0:T(128)S(1)} %pad_add_fusion.pos_ref, s32[1,1]{1,0:T(1,128)S(6)} %copy.48.count_ref, s32[1,8,16]{2,1,0:T(8,128)} %idx_ref.1, bf16[512,256]{1,0:T(8,128)(2,1)} %x_hbm.5, bf16[512,256]{1,0:T(8,128)(2,1)} %g_hbm.5, ...), custom_call_target="tpu_custom_call" | custom-call | bytes 7200000 | tf_op jit(solution)/shard_map/take_boundary/pallas_call | solution.py:506
  3.4 2.5 %collective-permute-start.3 = (s32[1,8,512]{2,1,0:T(8,128)S(1)}, s32[1,8,512]{2,1,0:T(8,128)S(1)}, u32[]{:S(2)}, u32[]{:S(2)}) collective-permute-start(s32[1,8,512]{2,1,0:T(8,128)S(1)} %get-tuple-element.68.refs_0_), channel_id=1, source_target_pairs={{0,3},{1,2},{2,1},{3,0},{4,7},{5,6},{6,5},{7,4},{8,11},{9,10},{10,... | collective-permute-start | bytes 49160 | tf_op jit(solution)/shard_map/ppermute | solution.py:476
  5.9 0.6 collective-permute-start.2
  6.5 0.0 collective-permute-start.1
  6.5 1.7 %collective-permute-start = (bf16[4,16,512]{2,1,0:T(8,128)(2,1)S(1)}, bf16[4,16,512]{2,1,0:T(8,128)(2,1)S(1)}, u32[]{:S(2)}, u32[]{:S(2)}) collective-permute-start(bf16[4,16,512]{2,1,0:T(8,128)(2,1)S(1)} %get-tuple-element.62), channel_id=1, source_target_pairs={{0,4},{4,0},{8,12},{12,8},{16,20},{20,16},{24,28},{28,24},{1,5},{5... | collective-permute-start | bytes 196616 | tf_op jit(solution)/shard_map/ppermute | solution.py:476
  8.3 2.7 %collective-permute-done = bf16[4,16,512]{2,1,0:T(8,128)(2,1)S(1)} collective-permute-done((bf16[4,16,512]{2,1,0:T(8,128)(2,1)S(1)}, bf16[4,16,512]{2,1,0:T(8,128)(2,1)S(1)}, u32[]{:S(2)}, u32[]{:S(2)}) %collective-permute-start) | collective-permute-done | bytes 65568 | tf_op jit(solution)/shard_map/ppermute | solution.py:476
  11.0 0.0 collective-permute-done.3.refs_3_
  11.1 0.0 collective-permute-done.2.refs_2_
  11.1 0.0 collective-permute-done.1.refs_1_
  11.1 1.7 %collective-permute-start.4 = (bf16[2,16,512]{2,1,0:T(8,128)(2,1)S(1)}, bf16[2,16,512]{2,1,0:T(8,128)(2,1)S(1)}, u32[]{:S(2)}, u32[]{:S(2)}) collective-permute-start(bf16[2,16,512]{2,1,0:T(8,128)(2,1)S(1)} %get-tuple-element.65), channel_id=1, source_target_pairs={{0,8},{4,12},{8,0},{12,4},{16,24},{20,28},{24,16},{28,20},{1,9},{5... | collective-permute-start | bytes 98312 | tf_op jit(solution)/shard_map/ppermute | solution.py:476
  12.7 2.6 %collective-permute-start.5 = (bf16[2,16,512]{2,1,0:T(8,128)(2,1)S(1)}, bf16[2,16,512]{2,1,0:T(8,128)(2,1)S(1)}, u32[]{:S(2)}, u32[]{:S(2)}) collective-permute-start(bf16[2,16,512]{2,1,0:T(8,128)(2,1)S(1)} %get-tuple-element.66), channel_id=1, source_target_pairs={{0,16},{4,20},{8,24},{12,28},{16,0},{20,4},{24,8},{28,12},{1,17},{... | collective-permute-start | bytes 98312 | tf_op jit(solution)/shard_map/ppermute | solution.py:476
  15.3 0.2 collective-permute-start.6
  15.5 2.7 %spread.1 = (f32[16,512]{1,0:T(8,128)}, bf16[2560,512]{1,0:T(8,128)(2,1)S(1)}, bf16[640,2560]{1,0:T(8,128)(2,1)S(1)}, bf16[2560,128]{1,0:T(8,128)(2,1)S(1)}, bf1...) custom-call(s32[2]{0:T(128)S(1)} %pad_add_fusion.pos_ref, ...), custom_call_target="tpu_custom_call" | custom-call | bytes 16200000 | tf_op jit(solution)/shard_map/spread/pallas_call | solution.py:550
  18.2 2.6 %own_pins.1.refs_12_ = bf16[2560,512]{1,0:T(8,128)(2,1)S(1)} custom-call(bf16[2,16,512]{2,1,0:T(8,128)(2,1)S(1)} %get-tuple-element.64.after_ref.refs_0_, bf16[2560,512]{1,0:T(8,128)(2,1)S(1)} %get-tuple-element.80.at_pin, bf16[512,256]{1,0:T(8,128)(2,1)} %x_hbm.5, bf16[512,256]{1,0:T(8,128)(2,1)} %g_hbm.5), custom_call_target="tpu_custom_call" | custom-call | bytes 9000000 | tf_op jit(solution)/shard_map/own_pins/pallas_call | solution.py:565
  20.8 0.0 collective-permute-done.4.refs_1_
  20.8 0.0 collective-permute-done.5.refs_2_
  20.8 0.2 collective-permute-done.6.refs_3_
  21.0 7.7 %layer.1 = (bf16[8,104,256]{2,1,0:T(8,128)(2,1)}, f32[640,512]{1,0:T(8,128)}, bf16[640,256]{1,0:T(8,128)(2,1)}) custom-call(bf16[2,16,512]{2,1,0:T(8,128)(2,1)S(1)} %get-tuple-element.64.after_ref.refs_0_, bf16[2,16,512]{2,1,0:T(8,128)(2,1)S(1)} %collective-permute-done.4.refs_1_, bf16[2,16,512]{2,1,0:T(8,128)(2,1)S(1)} %collective-permute-done.5.refs_2_, ...), custom_call_target="tpu_custom_call" | custom-call | bytes 27720000 | tf_op jit(solution)/shard_map/layer/pallas_call | solution.py:576
  28.7 5.6 %all-to-all-start = ((bf16[8,104,256]{2,1,0:T(8,128)(2,1)}), bf16[8,104,256]{2,1,0:T(8,128)(2,1)S(1)}, u32[]{:S(2)}, u32[]{:S(2)}) async-start(bf16[8,104,256]{2,1,0:T(8,128)(2,1)} %get-tuple-element.81), calls=%async_computation | async-start | bytes 851968 | tf_op jit(solution)/shard_map/all_to_all | solution.py:601
  34.4 4.5 %back.1 = (f32[160,512]{1,0:T(8,128)S(1)}, f32[160,512]{1,0:T(8,128)S(1)}, bf16[320,512]{1,0:T(8,128)(2,1)S(1)}) custom-call(s32[2]{0:T(128)S(1)} %pad_add_fusion.pos_ref, f32[16,512]{1,0:T(8,128)} %get-tuple-element.82.ids_hbm, f32[640,512]{1,0:T(8,128)} %get-tuple-element.83.sums_hbm, bf16[640,256]{1,0:T(8,128)(2,1)} %get-tuple-element.84.net_grads_hbm, ...), custom_call_target="tpu_custom_call" | custom-call | bytes 16559999 | tf_op jit(solution)/shard_map/back/pallas_call | solution.py:606
  38.9 0.0 copy-start
  38.9 0.1 collective-permute-start.7
  38.9 1.6 %collective-permute-done.7.twin_ref = bf16[320,512]{1,0:T(8,128)(2,1)S(1)} collective-permute-done((bf16[320,512]{1,0:T(8,128)(2,1)S(1)}, bf16[320,512]{1,0:T(8,128)(2,1)S(1)}, u32[]{:S(2)}, u32[]{:S(2)}) %collective-permute-start.7) | collective-permute-done | bytes 327712 | tf_op jit(solution)/shard_map/ppermute | solution.py:476
  40.6 0.1 pairs.1
  40.6 1.6 %collective-permute-start.8 = (bf16[160,512]{1,0:T(8,128)(2,1)S(1)}, bf16[160,512]{1,0:T(8,128)(2,1)S(1)}, u32[]{:S(2)}, u32[]{:S(2)}) collective-permute-start(bf16[160,512]{1,0:T(8,128)(2,1)S(1)} %get-tuple-element.89), channel_id=1, source_target_pairs={{0,2},{1,3},{2,0},{3,1},{4,6},{5,7},{6,4},{7,5},{8,10},{9,11},{10,... | collective-permute-start | bytes 491528 | tf_op jit(solution)/shard_map/ppermute | solution.py:476
  42.2 4.7 %collective-permute-done.8.rest_0_ = bf16[160,512]{1,0:T(8,128)(2,1)S(1)} collective-permute-done((bf16[160,512]{1,0:T(8,128)(2,1)S(1)}, bf16[160,512]{1,0:T(8,128)(2,1)S(1)}, u32[]{:S(2)}, u32[]{:S(2)}) %collective-permute-start.8) | collective-permute-done | bytes 163872 | tf_op jit(solution)/shard_map/ppermute | solution.py:476
  46.9 0.0 all-to-all-done.got_ref
  46.9 0.1 sums.1
  47.0 2.1 %collective-permute-start.9 = (bf16[112,256]{1,0:T(8,128)(2,1)S(1)}, bf16[112,256]{1,0:T(8,128)(2,1)S(1)}, u32[]{:S(2)}, u32[]{:S(2)}) collective-permute-start(bf16[112,256]{1,0:T(8,128)(2,1)S(1)} %get-tuple-element.92), channel_id=1, source_target_pairs={{0,8},{4,12},{8,0},{12,4},{16,24},{20,28},{24,16},{28,20},{1,9},{5... | collective-permute-start | bytes 172040 | tf_op jit(solution)/shard_map/ppermute | solution.py:476
  49.1 2.4 %collective-permute-start.10 = (bf16[112,256]{1,0:T(8,128)(2,1)S(1)}, bf16[112,256]{1,0:T(8,128)(2,1)S(1)}, u32[]{:S(2)}, u32[]{:S(2)}) collective-permute-start(bf16[112,256]{1,0:T(8,128)(2,1)S(1)} %get-tuple-element.93), channel_id=1, source_target_pairs={{0,16},{4,20},{8,24},{12,28},{16,0},{20,4},{24,8},{28,12},{1,17},{... | collective-permute-start | bytes 172040 | tf_op jit(solution)/shard_map/ppermute | solution.py:476
  51.5 0.1 collective-permute-start.11
  51.6 3.9 %collective-permute-done.10 = bf16[112,256]{1,0:T(8,128)(2,1)S(1)} collective-permute-done((bf16[112,256]{1,0:T(8,128)(2,1)S(1)}, bf16[112,256]{1,0:T(8,128)(2,1)S(1)}, u32[]{:S(2)}, u32[]{:S(2)}) %collective-permute-start.10) | collective-permute-done | bytes 57376 | tf_op jit(solution)/shard_map/ppermute | solution.py:476
  55.4 2.0 %collective-permute-done.11 = bf16[112,256]{1,0:T(8,128)(2,1)S(1)} collective-permute-done((bf16[112,256]{1,0:T(8,128)(2,1)S(1)}, bf16[112,256]{1,0:T(8,128)(2,1)S(1)}, u32[]{:S(2)}, u32[]{:S(2)}) %collective-permute-start.11) | collective-permute-done | bytes 57376 | tf_op jit(solution)/shard_map/ppermute | solution.py:476
  57.5 1.6 %collective-permute-start.13 = (bf16[192,256]{1,0:T(8,128)(2,1)S(1)}, bf16[192,256]{1,0:T(8,128)(2,1)S(1)}, u32[]{:S(2)}, u32[]{:S(2)}) collective-permute-start(bf16[192,256]{1,0:T(8,128)(2,1)S(1)} %pad_maximum_fusion.2), channel_id=1, source_target_pairs={{0,2},{1,3},{2,0},{3,1},{4,6},{5,7},{6,4},{7,5},{8,10},{9,11},{10,... | collective-permute-start | bytes 294920 | tf_op jit(solution)/shard_map/ppermute | solution.py:476
  59.1 0.0 collective-permute-done.9
  59.1 1.5 %collective-permute-start.12 = (bf16[256,256]{1,0:T(8,128)(2,1)S(1)}, bf16[256,256]{1,0:T(8,128)(2,1)S(1)}, u32[]{:S(2)}, u32[]{:S(2)}) collective-permute-start(bf16[256,256]{1,0:T(8,128)(2,1)S(1)} %pad_maximum_fusion.1), channel_id=1, source_target_pairs={{0,4},{4,0},{8,12},{12,8},{16,20},{20,16},{24,28},{28,24},{1,5},{5... | collective-permute-start | bytes 393224 | tf_op jit(solution)/shard_map/ppermute | solution.py:476
  60.6 3.5 %collective-permute-done.12 = bf16[256,256]{1,0:T(8,128)(2,1)S(1)} collective-permute-done((bf16[256,256]{1,0:T(8,128)(2,1)S(1)}, bf16[256,256]{1,0:T(8,128)(2,1)S(1)}, u32[]{:S(2)}, u32[]{:S(2)}) %collective-permute-start.12) | collective-permute-done | bytes 131104 | tf_op jit(solution)/shard_map/ppermute | solution.py:476
  64.2 0.6 collective-permute-start.16
  64.8 0.0 collective-permute-start.14
  64.8 0.0 collective-permute-done.13
  64.8 0.6 collective-permute-start.15
  65.4 1.5 %collective-permute-start.17 = (bf16[384,256]{1,0:T(8,128)(2,1)S(1)}, bf16[384,256]{1,0:T(8,128)(2,1)S(1)}, u32[]{:S(2)}, u32[]{:S(2)}) collective-permute-start(bf16[384,256]{1,0:T(8,128)(2,1)S(1)} %pad_maximum_fusion.refs_1_), channel_id=1, source_target_pairs={{0,4},{4,0},{8,12},{12,8},{16,20},{20,16},{24,28},{28,24},{1,5},{5... | collective-permute-start | bytes 589832 | tf_op jit(solution)/shard_map/ppermute | solution.py:476
  66.9 0.0 collective-permute-done.14.refs_2_
  66.9 0.0 collective-permute-done.15.refs_3_
  66.9 0.0 copy-done
  66.9 2.4 %first_pieces.1 = (f32[256,1024]{1,0:T(8,128)}, f32[256,1024]{1,0:T(8,128)}, f32[1024,256]{1,0:T(8,128)}, f32[128,512]{1,0:T(8,128)S(1)}, bf16[128,128]{1,0:T(8,128)(2,1)S(1)}, /*index=5*/bf16[128,128]{1,0:T(8,128)(2,1)S(1)}) custom-call(s32[2]{0:T(128)S(1)} %pad_add_fusion.pos_ref, s32[1,8,16]{2,1,0:T(8,128)S(1)} %copy-done, bf16[512,256]{1,0:T(8,128)(2,1)} %x_hbm.5, ...), custom_call_target="tpu_custom_call" | custom-call | tf_op jit(solution)/shard_map/first_pieces/pallas_call | solution.py:706
  69.3 3.0 %collective-permute-done.17.refs_1_ = bf16[384,256]{1,0:T(8,128)(2,1)S(1)} collective-permute-done((bf16[384,256]{1,0:T(8,128)(2,1)S(1)}, bf16[384,256]{1,0:T(8,128)(2,1)S(1)}, u32[]{:S(2)}, u32[]{:S(2)}) %collective-permute-start.17) | collective-permute-done | bytes 196640 | tf_op jit(solution)/shard_map/ppermute | solution.py:476
  72.3 0.0 collective-permute-done.16.refs_0_
  72.3 0.0 collective-permute-start.18
  72.3 0.5 collective-permute-start.19
  72.8 1.6 %place.1 = (f32[256,1024]{1,0:T(8,128)}, f32[256,1024]{1,0:T(8,128)}, f32[1024,256]{1,0:T(8,128)}) custom-call(s32[2]{0:T(128)S(1)} %pad_add_fusion.pos_ref, bf16[464,256]{1,0:T(8,128)(2,1)S(1)} %collective-permute-done.16.refs_0_, bf16[384,256]{1,0:T(8,128)(2,1)S(1)} %collective-permute-done.17.refs_1_, ...), custom_call_target="tpu_custom_call", output_to_operand_aliasing={{0}: (3, {}), {1}: (4, {}), {2}: (5, {})} | custom-call | tf_op jit(solution)/shard_map/place/pallas_call | solution.py:717
  74.4 0.0 collective-permute-done.18.refs_0_
  74.5 0.0 collective-permute-done.19.refs_1_
  74.5 2.3 %finish.1 = (f32[256,1024]{1,0:T(8,128)}, f32[256,1024]{1,0:T(8,128)}, f32[1024,256]{1,0:T(8,128)}, bf16[128,256]{1,0:T(8,128)(2,1)}, bf16[128,256]{1,0:T(8,128)(2,1)}, /*index=5*/f32[1,1024]{1,0:T(1,128)}) custom-call(s32[2]{0:T(128)S(1)} %pad_add_fusion.pos_ref, ...), custom_call_target="tpu_custom_call", output_to_operand_aliasing={{0}: (10, {}), {1}: (11, {}), {2}: (12, {})} | custom-call | tf_op jit(solution)/shard_map/finish/pallas_call | solution.py:728
  (27 shorter events, 0.1 us)
Async XLA Ops:
  3.4 7.7 %collective-permute-start.3 = (s32[1,8,512]{2,1,0:T(8,128)S(1)}, s32[1,8,512]{2,1,0:T(8,128)S(1)}, u32[]{:S(2)}, u32[]{:S(2)}) collective-permute-start(s32[1,8,512]{2,1,0:T(8,128)S(1)} %get-tuple-element.68.refs_0_), channel_id=1, source_target_pairs={{0,3},{1,2},{2,1},{3,0},{4,7},{5,6},{6,5},{7,4},{8,11},{9,10},{10,... | collective-permute-start | bytes 49160 | tf_op jit(solution)/shard_map/ppermute | solution.py:476
  5.9 5.2 %collective-permute-start.2 = (s32[1,8,512]{2,1,0:T(8,128)S(1)}, s32[1,8,512]{2,1,0:T(8,128)S(1)}, u32[]{:S(2)}, u32[]{:S(2)}) collective-permute-start(s32[1,8,512]{2,1,0:T(8,128)S(1)} %get-tuple-element.68.refs_0_), channel_id=1, source_target_pairs={{0,2},{1,3},{2,0},{3,1},{4,6},{5,7},{6,4},{7,5},{8,10},{9,11},{10,... | collective-permute-start | bytes 49160 | tf_op jit(solution)/shard_map/ppermute | solution.py:476
  6.5 4.6 %collective-permute-start.1 = (s32[1,8,512]{2,1,0:T(8,128)S(1)}, s32[1,8,512]{2,1,0:T(8,128)S(1)}, u32[]{:S(2)}, u32[]{:S(2)}) collective-permute-start(s32[1,8,512]{2,1,0:T(8,128)S(1)} %get-tuple-element.68.refs_0_), channel_id=1, source_target_pairs={{0,1},{1,0},{2,3},{3,2},{4,5},{5,4},{6,7},{7,6},{8,9},{9,8},{10,11... | collective-permute-start | bytes 49160 | tf_op jit(solution)/shard_map/ppermute | solution.py:476
  6.5 4.5 %collective-permute-start = (bf16[4,16,512]{2,1,0:T(8,128)(2,1)S(1)}, bf16[4,16,512]{2,1,0:T(8,128)(2,1)S(1)}, u32[]{:S(2)}, u32[]{:S(2)}) collective-permute-start(bf16[4,16,512]{2,1,0:T(8,128)(2,1)S(1)} %get-tuple-element.62), channel_id=1, source_target_pairs={{0,4},{4,0},{8,12},{12,8},{16,20},{20,16},{24,28},{28,24},{1,5},{5... | collective-permute-start | bytes 196616 | tf_op jit(solution)/shard_map/ppermute | solution.py:476
  11.1 9.7 %collective-permute-start.4 = (bf16[2,16,512]{2,1,0:T(8,128)(2,1)S(1)}, bf16[2,16,512]{2,1,0:T(8,128)(2,1)S(1)}, u32[]{:S(2)}, u32[]{:S(2)}) collective-permute-start(bf16[2,16,512]{2,1,0:T(8,128)(2,1)S(1)} %get-tuple-element.65), channel_id=1, source_target_pairs={{0,8},{4,12},{8,0},{12,4},{16,24},{20,28},{24,16},{28,20},{1,9},{5... | collective-permute-start | bytes 98312 | tf_op jit(solution)/shard_map/ppermute | solution.py:476
  12.7 8.1 %collective-permute-start.5 = (bf16[2,16,512]{2,1,0:T(8,128)(2,1)S(1)}, bf16[2,16,512]{2,1,0:T(8,128)(2,1)S(1)}, u32[]{:S(2)}, u32[]{:S(2)}) collective-permute-start(bf16[2,16,512]{2,1,0:T(8,128)(2,1)S(1)} %get-tuple-element.66), channel_id=1, source_target_pairs={{0,16},{4,20},{8,24},{12,28},{16,0},{20,4},{24,8},{28,12},{1,17},{... | collective-permute-start | bytes 98312 | tf_op jit(solution)/shard_map/ppermute | solution.py:476
  15.3 5.7 %collective-permute-start.6 = (bf16[2,16,512]{2,1,0:T(8,128)(2,1)S(1)}, bf16[2,16,512]{2,1,0:T(8,128)(2,1)S(1)}, u32[]{:S(2)}, u32[]{:S(2)}) collective-permute-start(bf16[2,16,512]{2,1,0:T(8,128)(2,1)S(1)} %get-tuple-element.67), channel_id=1, source_target_pairs={{0,24},{4,28},{8,16},{12,20},{16,8},{20,12},{24,0},{28,4},{1,25},{... | collective-permute-start | bytes 98312 | tf_op jit(solution)/shard_map/ppermute | solution.py:476
  28.7 18.2 %all-to-all-start = ((bf16[8,104,256]{2,1,0:T(8,128)(2,1)}), bf16[8,104,256]{2,1,0:T(8,128)(2,1)S(1)}, u32[]{:S(2)}, u32[]{:S(2)}) async-start(bf16[8,104,256]{2,1,0:T(8,128)(2,1)} %get-tuple-element.81), calls=%async_computation | async-start | bytes 851968 | tf_op jit(solution)/shard_map/all_to_all | solution.py:601
  38.9 28.0 %copy-start = (s32[1,8,16]{2,1,0:T(8,128)S(1)}, s32[1,8,16]{2,1,0:T(8,128)}, u32[]{:S(2)}) copy-start(s32[1,8,16]{2,1,0:T(8,128)} %idx_ref.1) | copy-start | bytes 1540
  38.9 1.7 %collective-permute-start.7 = (bf16[320,512]{1,0:T(8,128)(2,1)S(1)}, bf16[320,512]{1,0:T(8,128)(2,1)S(1)}, u32[]{:S(2)}, u32[]{:S(2)}) collective-permute-start(bf16[320,512]{1,0:T(8,128)(2,1)S(1)} %get-tuple-element.87), channel_id=1, source_target_pairs={{0,1},{1,0},{2,3},{3,2},{4,5},{5,4},{6,7},{7,6},{8,9},{9,8},{10,11... | collective-permute-start | bytes 983048 | tf_op jit(solution)/shard_map/ppermute | solution.py:476
  40.6 6.3 %collective-permute-start.8 = (bf16[160,512]{1,0:T(8,128)(2,1)S(1)}, bf16[160,512]{1,0:T(8,128)(2,1)S(1)}, u32[]{:S(2)}, u32[]{:S(2)}) collective-permute-start(bf16[160,512]{1,0:T(8,128)(2,1)S(1)} %get-tuple-element.89), channel_id=1, source_target_pairs={{0,2},{1,3},{2,0},{3,1},{4,6},{5,7},{6,4},{7,5},{8,10},{9,11},{10,... | collective-permute-start | bytes 491528 | tf_op jit(solution)/shard_map/ppermute | solution.py:476
  47.0 12.0 %collective-permute-start.9 = (bf16[112,256]{1,0:T(8,128)(2,1)S(1)}, bf16[112,256]{1,0:T(8,128)(2,1)S(1)}, u32[]{:S(2)}, u32[]{:S(2)}) collective-permute-start(bf16[112,256]{1,0:T(8,128)(2,1)S(1)} %get-tuple-element.92), channel_id=1, source_target_pairs={{0,8},{4,12},{8,0},{12,4},{16,24},{20,28},{24,16},{28,20},{1,9},{5... | collective-permute-start | bytes 172040 | tf_op jit(solution)/shard_map/ppermute | solution.py:476
  49.1 6.3 %collective-permute-start.10 = (bf16[112,256]{1,0:T(8,128)(2,1)S(1)}, bf16[112,256]{1,0:T(8,128)(2,1)S(1)}, u32[]{:S(2)}, u32[]{:S(2)}) collective-permute-start(bf16[112,256]{1,0:T(8,128)(2,1)S(1)} %get-tuple-element.93), channel_id=1, source_target_pairs={{0,16},{4,20},{8,24},{12,28},{16,0},{20,4},{24,8},{28,12},{1,17},{... | collective-permute-start | bytes 172040 | tf_op jit(solution)/shard_map/ppermute | solution.py:476
  51.5 6.0 %collective-permute-start.11 = (bf16[112,256]{1,0:T(8,128)(2,1)S(1)}, bf16[112,256]{1,0:T(8,128)(2,1)S(1)}, u32[]{:S(2)}, u32[]{:S(2)}) collective-permute-start(bf16[112,256]{1,0:T(8,128)(2,1)S(1)} %get-tuple-element.94), channel_id=1, source_target_pairs={{0,24},{4,28},{8,16},{12,20},{16,8},{20,12},{24,0},{28,4},{1,25},{... | collective-permute-start | bytes 172040 | tf_op jit(solution)/shard_map/ppermute | solution.py:476
  57.5 7.3 %collective-permute-start.13 = (bf16[192,256]{1,0:T(8,128)(2,1)S(1)}, bf16[192,256]{1,0:T(8,128)(2,1)S(1)}, u32[]{:S(2)}, u32[]{:S(2)}) collective-permute-start(bf16[192,256]{1,0:T(8,128)(2,1)S(1)} %pad_maximum_fusion.2), channel_id=1, source_target_pairs={{0,2},{1,3},{2,0},{3,1},{4,6},{5,7},{6,4},{7,5},{8,10},{9,11},{10,... | collective-permute-start | bytes 294920 | tf_op jit(solution)/shard_map/ppermute | solution.py:476
  59.1 5.0 %collective-permute-start.12 = (bf16[256,256]{1,0:T(8,128)(2,1)S(1)}, bf16[256,256]{1,0:T(8,128)(2,1)S(1)}, u32[]{:S(2)}, u32[]{:S(2)}) collective-permute-start(bf16[256,256]{1,0:T(8,128)(2,1)S(1)} %pad_maximum_fusion.1), channel_id=1, source_target_pairs={{0,4},{4,0},{8,12},{12,8},{16,20},{20,16},{24,28},{28,24},{1,5},{5... | collective-permute-start | bytes 393224 | tf_op jit(solution)/shard_map/ppermute | solution.py:476
  64.2 8.1 %collective-permute-start.16 = (bf16[464,256]{1,0:T(8,128)(2,1)S(1)}, bf16[464,256]{1,0:T(8,128)(2,1)S(1)}, u32[]{:S(2)}, u32[]{:S(2)}) collective-permute-start(bf16[464,256]{1,0:T(8,128)(2,1)S(1)} %get-tuple-element.141.refs_0_), channel_id=1, source_target_pairs={{0,2},{1,3},{2,0},{3,1},{4,6},{5,7},{6,4},{7,5},{8,10},{9,11},{10,... | collective-permute-start | bytes 712712 | tf_op jit(solution)/shard_map/ppermute | solution.py:476
  64.8 2.1 %collective-permute-start.14 = (bf16[464,256]{1,0:T(8,128)(2,1)S(1)}, bf16[464,256]{1,0:T(8,128)(2,1)S(1)}, u32[]{:S(2)}, u32[]{:S(2)}) collective-permute-start(bf16[464,256]{1,0:T(8,128)(2,1)S(1)} %get-tuple-element.141.refs_0_), channel_id=1, source_target_pairs={{0,1},{1,0},{2,3},{3,2},{4,5},{5,4},{6,7},{7,6},{8,9},{9,8},{10,11... | collective-permute-start | bytes 712712 | tf_op jit(solution)/shard_map/ppermute | solution.py:476
  64.8 2.0 %collective-permute-start.15 = (bf16[384,256]{1,0:T(8,128)(2,1)S(1)}, bf16[384,256]{1,0:T(8,128)(2,1)S(1)}, u32[]{:S(2)}, u32[]{:S(2)}) collective-permute-start(bf16[384,256]{1,0:T(8,128)(2,1)S(1)} %pad_maximum_fusion.refs_1_), channel_id=1, source_target_pairs={{0,1},{1,0},{2,3},{3,2},{4,5},{5,4},{6,7},{7,6},{8,9},{9,8},{10,11... | collective-permute-start | bytes 589832 | tf_op jit(solution)/shard_map/ppermute | solution.py:476
  65.4 6.9 %collective-permute-start.17 = (bf16[384,256]{1,0:T(8,128)(2,1)S(1)}, bf16[384,256]{1,0:T(8,128)(2,1)S(1)}, u32[]{:S(2)}, u32[]{:S(2)}) collective-permute-start(bf16[384,256]{1,0:T(8,128)(2,1)S(1)} %pad_maximum_fusion.refs_1_), channel_id=1, source_target_pairs={{0,4},{4,0},{8,12},{12,8},{16,20},{20,16},{24,28},{28,24},{1,5},{5... | collective-permute-start | bytes 589832 | tf_op jit(solution)/shard_map/ppermute | solution.py:476
  72.3 2.1 %collective-permute-start.18 = (bf16[464,256]{1,0:T(8,128)(2,1)S(1)}, bf16[464,256]{1,0:T(8,128)(2,1)S(1)}, u32[]{:S(2)}, u32[]{:S(2)}) collective-permute-start(bf16[464,256]{1,0:T(8,128)(2,1)S(1)} %collective-permute-done.16.refs_0_), channel_id=1, source_target_pairs={{0,1},{1,0},{2,3},{3,2},{4,5},{5,4},{6,7},{7,6},{8,9},{9,8},{10,11... | collective-permute-start | bytes 712712 | tf_op jit(solution)/shard_map/ppermute | solution.py:476
  72.3 2.2 %collective-permute-start.19 = (bf16[384,256]{1,0:T(8,128)(2,1)S(1)}, bf16[384,256]{1,0:T(8,128)(2,1)S(1)}, u32[]{:S(2)}, u32[]{:S(2)}) collective-permute-start(bf16[384,256]{1,0:T(8,128)(2,1)S(1)} %collective-permute-done.17.refs_1_), channel_id=1, source_target_pairs={{0,1},{1,0},{2,3},{3,2},{4,5},{5,4},{6,7},{7,6},{8,9},{9,8},{10,11... | collective-permute-start | bytes 589832 | tf_op jit(solution)/shard_map/ppermute | solution.py:476

commit v4 on v3

--- a/solution.py
+++ b/solution.py
@@ -48,7 +48,7 @@
     return copies
 
 
-def gather_kernel(fast, pos_ref, count_ref, idx_hbm, x_hbm, g_hbm, net_hbm, ref_hbm, ints_ref, *rest):
+def gather_kernel(fast, count_ref, idx_hbm, x_hbm, g_hbm, net_hbm, ref_hbm, ints_ref, *rest):
     *outs, idx_ref, x_ref, g_ref, net_ref, ref_ref, sems = rest
     copies = start_copies(
         [(idx_hbm, idx_ref), (x_hbm, x_ref), (g_hbm, g_ref), (net_hbm, net_ref), (ref_hbm, ref_ref)], sems
@@ -62,13 +62,14 @@
     part_count, slots = idx_ref.shape[1:]
     cells, feat = x_ref.shape
     if fast:
-        order = [pos_ref[0] ^ bits for bits in (0, 2, 4, 6, 1, 3, 5, 7)]
+        cell = lax.axis_index("cell")
+        order = [cell ^ bits for bits in range(part_count)]
         idx = jnp.concatenate([idx_ref[0, pl.ds(part, 1), :] for part in order], axis=0)
         onehot = slot_onehot(idx, cells)
         for at, values in ((0, x_ref), (feat, g_ref)):
             rows = dot_tn(onehot, values[...]).astype(BF16)
-            for half, out_ref in enumerate(outs):
-                out_ref[:, :, at : at + feat] = rows[64 * half : 64 * (half + 1)].reshape(4, slots, feat)
+            for k, out_ref in enumerate(outs):
+                out_ref[:, :, at : at + feat] = rows[32 * k : 32 * (k + 1)].reshape(2, slots, feat)
         return
     (out_ref,) = outs
     group = 128 // slots
@@ -195,11 +196,12 @@
     blocks = net_grads.shape[0] // NETS_BLK
     pins = pin_count // blocks
     copies = start_copies([(x_hbm, table.at[:cells, :feat]), (g_hbm, table.at[:cells, feat:])], sems)
-    at = cells
-    for ref in halo_refs:
-        for part in range(ref.shape[0]):
-            table[at : at + ref.shape[1], :] = ref[part]
-            at += ref.shape[1]
+    if fast:
+        *near, cross = halo_refs
+        blocks_of = [block for k, ref in enumerate(near) for block in (ref[0], cross[k])]
+        table[cells:, :] = jnp.concatenate(blocks_of, axis=0)
+    else:
+        table[cells:, :] = halo_refs[0][...].reshape(table_len - cells, 2 * feat)
     for b in range(blocks):
         of = slice(b * pins, (b + 1) * pins)
         nets_of = slice(b * NETS_BLK, (b + 1) * NETS_BLK)
@@ -500,12 +502,12 @@
         return jax.ShapeDtypeStruct(dims, dtype)
 
     if fast:
-        sent_shape = [shape(BF16, 4, slots, 2 * feat)] * 2
+        sent_shape = [shape(BF16, 2, slots, 2 * feat)] * 4
     else:
         sent_shape = [shape(BF16, part_count, slots, 2 * feat)]
     ints, *sent = pl.pallas_call(
         functools.partial(gather_kernel, fast),
-        in_specs=[SMEM] + whole(1) + [HBM] * 5,
+        in_specs=whole(1) + [HBM] * 5,
         out_specs=whole(1 + len(sent_shape)),
         out_shape=[shape(jnp.int32, 1, 8, pins)] + sent_shape,
         scratch_shapes=[
@@ -519,14 +521,12 @@
         name="take_boundary",
         cost_estimate=about(2.0),
         **PARAMS,
-    )(pos, block_count, *in_hbm(send_idx, cell_feat, out_grad, pin_net, pin_ref))
-    if fast:
-        keep, cross = sent
-        all_ints = [ints] + [flip(ints, "net", bits) for bits in range(1, group_size)]
-        cross = flip(cross, "cell", 1)
-        near = [jnp.stack([keep[k], cross[k]]) for k in range(4)]
-        near, all_ints = lax.optimization_barrier((near, all_ints))
-        halo = [near[0]] + [flip(near[k], "cell", 2 * k) for k in (1, 2, 3)]
+    )(block_count, *in_hbm(send_idx, cell_feat, out_grad, pin_net, pin_ref))
+    if fast:
+        all_ints = jnp.concatenate([ints, flip(ints, "net", 1)])
+        all_ints = [all_ints, flip(all_ints, "net", 2)]
+        near = [sent[0]] + [flip(sent[k], "cell", 2 * k) for k in (1, 2, 3)]
+        cross = jnp.stack([a[1] for a in near])
     else:
         halo = [lax.all_to_all(sent[0], "cell", split_axis=0, concat_axis=0, tiled=True)]
         all_ints = [lax.all_gather(ints, "net", tiled=True)]
@@ -562,6 +562,9 @@
         cost_estimate=about(4.5),
         **PARAMS,
     )(pos, *all_ints, *in_hbm(w_in, w_net, bias.reshape(1, hidden_dim), w_out))
+    if fast:
+        cross, at_pin = lax.optimization_barrier((cross, at_pin))
+        halo = near + [flip(cross, "cell", 1)]
     taken = pl.pallas_call(
         own_pins_kernel,
         in_specs=[pl.BlockSpec(memory_space=pl.ANY)] + whole(1) + [HBM] * 2,
@@ -571,7 +574,7 @@
         name="own_pins",
         cost_estimate=about(2.5),
         **PARAMS,
-    )(halo[0], at_pin, *in_hbm(cell_feat, out_grad))
+    )(cross if fast else halo[0], at_pin, *in_hbm(cell_feat, out_grad))
 
     grads, sums, net_grads = pl.pallas_call(
         functools.partial(layer_kernel, fast, len(halo)),

time: 77.3 us -> 76.3 us (0.987)
  starting transfers between devices: 27.4 us -> 25.9 us
  waiting for transfers between devices: 21.7 us -> 22.7 us
    all_to_all x1, starting transfers between devices: 5.63 us -> 4.36 us  [local(): got = lax.all_to_all(grads, 'cell', split_axis=0, concat_axis=0, tiled=True)]
    ppermute x20 -> x19, waiting for transfers between devices: 21.7 us -> 22.7 us  [flip(): return lax.ppermute(x, axis, [(i, i ^ bits) for i in range(size)])]
    ppermute x20 -> x19, starting transfers between devices: 21.7 us -> 21.5 us  [flip(): return lax.ppermute(x, axis, [(i, i ^ bits) for i in range(size)])]
  transfers between devices with their start and end apart: 21 -> 20, of which waited for: 8 -> 9; matrix products, arithmetic and copies ran while one was open for 0% -> 0% of each run, Pallas kernels for 18% -> 15%
where the time goes in v4:
time: 76.3 us; the launch traced here: 75.9 us
  starting transfers between devices  25.9 us (34%)
  Pallas kernels  25.4 us (33%)
  waiting for transfers between devices  22.7 us (30%)
  between operations  1.68 us (2%)
    ppermute x19, waiting for transfers between devices, flip(): return lax.ppermute(x, axis, [(i, i ^ bits) for i in range(size)])  22.7 us
    ppermute x19, starting transfers between devices, flip(): return lax.ppermute(x, axis, [(i, i ^ bits) for i in range(size)])  21.5 us
    pallas_call x1, Pallas kernels, local(): pl.pallas_call(functools.partial(layer_kernel, fast, len(halo)), in_specs...  7.68 us
    pallas_call x1, Pallas kernels, local(): pl.pallas_call(functools.partial(back_kernel, fast), in_specs=[SMEM] + [H...  4.47 us
    all_to_all x1, starting transfers between devices, local(): got = lax.all_to_all(grads, 'cell', split_axis=0, concat_axis=0, tiled=True)  4.36 us
    pallas_call x1, Pallas kernels, local(): pl.pallas_call(functools.partial(spread_kernel, fast, slots), in_specs=[S...  2.68 us
    pallas_call x1, Pallas kernels, local(): pl.pallas_call(own_pins_kernel, in_specs=[pl.BlockSpec(memory_space=pl.AN...  2.56 us
    pallas_call x1, Pallas kernels, local(): pl.pallas_call(functools.partial(first_kernel, early_tags + twin(early_ta...  2.41 us
  transfers between devices with their start and end apart: 20, of which 9 were waited for; matrix products, arithmetic and copies ran while one was open for 0% of the time, Pallas kernels for 15%

profile of v4, /device:TPU:0, one launch (start us, length us, event | category | flops | bytes accessed | tf_op | source)
XLA Modules:
  0.0 75.9 jit_solution(3807235250166710502)
XLA Ops:
  1.3 1.5 %take_boundary.1 = (s32[1,8,512]{2,1,0:T(8,128)S(1)}, bf16[2,16,512]{2,1,0:T(8,128)(2,1)S(1)}, bf16[2,16,512]{2,1,0:T(8,128)(2,1)S(1)}, bf16[2,16,512]{2,1,0:T(8,128)(2,1)S(1)}, bf16[2,16,512]{2,1,0:T(8,128)(2,1)S(1)}) custom-call(s32[1,1]{1,0:T(1,128)S(6)} %copy.49.count_ref, s32[1,8,16]{2,1,0:T(8,128)} %idx_ref.1, bf16[512,256]{1,0:T(8,128)(2,1)} %x_hbm.5, ...), custom_call_target="tpu_custom_call" | custom-call | bytes 7200000 | tf_op jit(solution)/shard_map/take_boundary/pallas_call | solution.py:508
  2.8 0.5 collective-permute-start.3
  3.3 2.6 %collective-permute-start = (bf16[2,16,512]{2,1,0:T(8,128)(2,1)S(1)}, bf16[2,16,512]{2,1,0:T(8,128)(2,1)S(1)}, u32[]{:S(2)}, u32[]{:S(2)}) collective-permute-start(bf16[2,16,512]{2,1,0:T(8,128)(2,1)S(1)} %get-tuple-element.58), channel_id=1, source_target_pairs={{0,8},{4,12},{8,0},{12,4},{16,24},{20,28},{24,16},{28,20},{1,9},{5... | collective-permute-start | bytes 98312 | tf_op jit(solution)/shard_map/ppermute | solution.py:478
  5.9 2.6 %collective-permute-start.1 = (bf16[2,16,512]{2,1,0:T(8,128)(2,1)S(1)}, bf16[2,16,512]{2,1,0:T(8,128)(2,1)S(1)}, u32[]{:S(2)}, u32[]{:S(2)}) collective-permute-start(bf16[2,16,512]{2,1,0:T(8,128)(2,1)S(1)} %get-tuple-element.59), channel_id=1, source_target_pairs={{0,16},{4,20},{8,24},{12,28},{16,0},{20,4},{24,8},{28,12},{1,17},{... | collective-permute-start | bytes 98312 | tf_op jit(solution)/shard_map/ppermute | solution.py:478
  8.5 0.0 collective-permute-start.2
  8.5 0.1 pad_add_fusion.pos_ref
  8.6 0.0 collective-permute-done.3
  8.6 1.8 %collective-permute-start.4 = (s32[2,8,512]{2,1,0:T(8,128)S(1)}, s32[2,8,512]{2,1,0:T(8,128)S(1)}, u32[]{:S(2)}, u32[]{:S(2)}) collective-permute-start(s32[2,8,512]{2,1,0:T(8,128)S(1)} %constant_dynamic-update-slice_fusion.refs_0_), channel_id=1, source_target_pairs={{0,2},{1,3},{2,0},{3,1},{4,6},{5,7},{6,4},{7,5},{8,10},{9,11},{10,... | collective-permute-start | bytes 98312 | tf_op jit(solution)/shard_map/ppermute | solution.py:478
  10.4 0.0 collective-permute-done.refs_1_
  10.4 0.9 %collective-permute-done.1.refs_2_ = bf16[2,16,512]{2,1,0:T(8,128)(2,1)S(1)} collective-permute-done((bf16[2,16,512]{2,1,0:T(8,128)(2,1)S(1)}, bf16[2,16,512]{2,1,0:T(8,128)(2,1)S(1)}, u32[]{:S(2)}, u32[]{:S(2)}) %collective-permute-start.1) | collective-permute-done | bytes 32800 | tf_op jit(solution)/shard_map/ppermute | solution.py:478
  11.3 2.9 %collective-permute-done.2.refs_3_ = bf16[2,16,512]{2,1,0:T(8,128)(2,1)S(1)} collective-permute-done((bf16[2,16,512]{2,1,0:T(8,128)(2,1)S(1)}, bf16[2,16,512]{2,1,0:T(8,128)(2,1)S(1)}, u32[]{:S(2)}, u32[]{:S(2)}) %collective-permute-start.2) | collective-permute-done | bytes 32800 | tf_op jit(solution)/shard_map/ppermute | solution.py:478
  14.3 0.0 collective-permute-done.4.refs_1_
  14.3 2.7 %spread.1 = (f32[16,512]{1,0:T(8,128)}, bf16[2560,512]{1,0:T(8,128)(2,1)S(1)}, bf16[640,2560]{1,0:T(8,128)(2,1)S(1)}, bf16[2560,128]{1,0:T(8,128)(2,1)S(1)}, bf1...) custom-call(s32[2]{0:T(128)S(1)} %pad_add_fusion.pos_ref, ...), custom_call_target="tpu_custom_call" | custom-call | bytes 16200000 | tf_op jit(solution)/shard_map/spread/pallas_call | solution.py:550
  17.0 1.6 %collective-permute-start.5 = (bf16[4,16,512]{2,1,0:T(8,128)(2,1)S(1)}, bf16[4,16,512]{2,1,0:T(8,128)(2,1)S(1)}, u32[]{:S(2)}, u32[]{:S(2)}) collective-permute-start(bf16[4,16,512]{2,1,0:T(8,128)(2,1)S(1)} %pad_maximum_fusion.3.after_ref), channel_id=1, source_target_pairs={{0,4},{4,0},{8,12},{12,8},{16,20},{20,16},{24,28},{28,24},{1,5},{5... | collective-permute-start | bytes 196616 | tf_op jit(solution)/shard_map/ppermute | solution.py:478
  18.5 2.6 %own_pins.1.refs_13_ = bf16[2560,512]{1,0:T(8,128)(2,1)S(1)} custom-call(bf16[4,16,512]{2,1,0:T(8,128)(2,1)S(1)} %pad_maximum_fusion.3.after_ref, bf16[2560,512]{1,0:T(8,128)(2,1)S(1)} %get-tuple-element.72.at_pin, bf16[512,256]{1,0:T(8,128)(2,1)} %x_hbm.5, bf16[512,256]{1,0:T(8,128)(2,1)} %g_hbm.5), custom_call_target="tpu_custom_call" | custom-call | bytes 9000000 | tf_op jit(solution)/shard_map/own_pins/pallas_call | solution.py:568
  21.1 0.2 collective-permute-done.5.refs_4_
  21.3 7.7 %layer.1 = (bf16[8,104,256]{2,1,0:T(8,128)(2,1)}, f32[640,512]{1,0:T(8,128)}, bf16[640,256]{1,0:T(8,128)(2,1)}) custom-call(bf16[2,16,512]{2,1,0:T(8,128)(2,1)S(1)} %get-tuple-element.57.refs_0_, bf16[2,16,512]{2,1,0:T(8,128)(2,1)S(1)} %collective-permute-done.refs_1_, bf16[2,16,512]{2,1,0:T(8,128)(2,1)S(1)} %collective-permute-done.1.refs_2_, ...), custom_call_target="tpu_custom_call" | custom-call | bytes 27720000 | tf_op jit(solution)/shard_map/layer/pallas_call | solution.py:579
  29.0 4.4 %all-to-all-start = ((bf16[8,104,256]{2,1,0:T(8,128)(2,1)}), bf16[8,104,256]{2,1,0:T(8,128)(2,1)S(1)}, u32[]{:S(2)}, u32[]{:S(2)}) async-start(bf16[8,104,256]{2,1,0:T(8,128)(2,1)} %get-tuple-element.73), calls=%async_computation | async-start | bytes 851968 | tf_op jit(solution)/shard_map/all_to_all | solution.py:604
  33.4 4.5 %back.1 = (f32[160,512]{1,0:T(8,128)S(1)}, f32[160,512]{1,0:T(8,128)S(1)}, bf16[320,512]{1,0:T(8,128)(2,1)S(1)}) custom-call(s32[2]{0:T(128)S(1)} %pad_add_fusion.pos_ref, f32[16,512]{1,0:T(8,128)} %get-tuple-element.74.ids_hbm, f32[640,512]{1,0:T(8,128)} %get-tuple-element.75.sums_hbm, bf16[640,256]{1,0:T(8,128)(2,1)} %get-tuple-element.76.net_grads_hbm, ...), custom_call_target="tpu_custom_call" | custom-call | bytes 16559999 | tf_op jit(solution)/shard_map/back/pallas_call | solution.py:609
  37.8 0.0 copy-start
  37.8 0.1 collective-permute-start.6
  37.9 1.6 %collective-permute-done.6.twin_ref = bf16[320,512]{1,0:T(8,128)(2,1)S(1)} collective-permute-done((bf16[320,512]{1,0:T(8,128)(2,1)S(1)}, bf16[320,512]{1,0:T(8,128)(2,1)S(1)}, u32[]{:S(2)}, u32[]{:S(2)}) %collective-permute-start.6) | collective-permute-done | bytes 327712 | tf_op jit(solution)/shard_map/ppermute | solution.py:478
  39.5 0.1 pairs.1
  39.6 1.6 %collective-permute-start.7 = (bf16[160,512]{1,0:T(8,128)(2,1)S(1)}, bf16[160,512]{1,0:T(8,128)(2,1)S(1)}, u32[]{:S(2)}, u32[]{:S(2)}) collective-permute-start(bf16[160,512]{1,0:T(8,128)(2,1)S(1)} %get-tuple-element.81), channel_id=1, source_target_pairs={{0,2},{1,3},{2,0},{3,1},{4,6},{5,7},{6,4},{7,5},{8,10},{9,11},{10,... | collective-permute-start | bytes 491528 | tf_op jit(solution)/shard_map/ppermute | solution.py:478
  41.2 4.7 %collective-permute-done.7.rest_0_ = bf16[160,512]{1,0:T(8,128)(2,1)S(1)} collective-permute-done((bf16[160,512]{1,0:T(8,128)(2,1)S(1)}, bf16[160,512]{1,0:T(8,128)(2,1)S(1)}, u32[]{:S(2)}, u32[]{:S(2)}) %collective-permute-start.7) | collective-permute-done | bytes 163872 | tf_op jit(solution)/shard_map/ppermute | solution.py:478
  45.9 0.0 all-to-all-done.got_ref
  45.9 0.1 sums.1
  46.0 2.1 %collective-permute-start.8 = (bf16[112,256]{1,0:T(8,128)(2,1)S(1)}, bf16[112,256]{1,0:T(8,128)(2,1)S(1)}, u32[]{:S(2)}, u32[]{:S(2)}) collective-permute-start(bf16[112,256]{1,0:T(8,128)(2,1)S(1)} %get-tuple-element.84), channel_id=1, source_target_pairs={{0,8},{4,12},{8,0},{12,4},{16,24},{20,28},{24,16},{28,20},{1,9},{5... | collective-permute-start | bytes 172040 | tf_op jit(solution)/shard_map/ppermute | solution.py:478
  48.1 2.4 %collective-permute-start.9 = (bf16[112,256]{1,0:T(8,128)(2,1)S(1)}, bf16[112,256]{1,0:T(8,128)(2,1)S(1)}, u32[]{:S(2)}, u32[]{:S(2)}) collective-permute-start(bf16[112,256]{1,0:T(8,128)(2,1)S(1)} %get-tuple-element.85), channel_id=1, source_target_pairs={{0,16},{4,20},{8,24},{12,28},{16,0},{20,4},{24,8},{28,12},{1,17},{... | collective-permute-start | bytes 172040 | tf_op jit(solution)/shard_map/ppermute | solution.py:478
  50.5 0.1 collective-permute-start.10
  50.5 3.9 %collective-permute-done.9 = bf16[112,256]{1,0:T(8,128)(2,1)S(1)} collective-permute-done((bf16[112,256]{1,0:T(8,128)(2,1)S(1)}, bf16[112,256]{1,0:T(8,128)(2,1)S(1)}, u32[]{:S(2)}, u32[]{:S(2)}) %collective-permute-start.9) | collective-permute-done | bytes 57376 | tf_op jit(solution)/shard_map/ppermute | solution.py:478
  54.4 2.0 %collective-permute-done.10 = bf16[112,256]{1,0:T(8,128)(2,1)S(1)} collective-permute-done((bf16[112,256]{1,0:T(8,128)(2,1)S(1)}, bf16[112,256]{1,0:T(8,128)(2,1)S(1)}, u32[]{:S(2)}, u32[]{:S(2)}) %collective-permute-start.10) | collective-permute-done | bytes 57376 | tf_op jit(solution)/shard_map/ppermute | solution.py:478
  56.5 1.6 %collective-permute-start.12 = (bf16[192,256]{1,0:T(8,128)(2,1)S(1)}, bf16[192,256]{1,0:T(8,128)(2,1)S(1)}, u32[]{:S(2)}, u32[]{:S(2)}) collective-permute-start(bf16[192,256]{1,0:T(8,128)(2,1)S(1)} %pad_maximum_fusion.2), channel_id=1, source_target_pairs={{0,2},{1,3},{2,0},{3,1},{4,6},{5,7},{6,4},{7,5},{8,10},{9,11},{10,... | collective-permute-start | bytes 294920 | tf_op jit(solution)/shard_map/ppermute | solution.py:478
  58.0 0.0 collective-permute-done.8
  58.1 1.5 %collective-permute-start.11 = (bf16[256,256]{1,0:T(8,128)(2,1)S(1)}, bf16[256,256]{1,0:T(8,128)(2,1)S(1)}, u32[]{:S(2)}, u32[]{:S(2)}) collective-permute-start(bf16[256,256]{1,0:T(8,128)(2,1)S(1)} %pad_maximum_fusion.1), channel_id=1, source_target_pairs={{0,4},{4,0},{8,12},{12,8},{16,20},{20,16},{24,28},{28,24},{1,5},{5... | collective-permute-start | bytes 393224 | tf_op jit(solution)/shard_map/ppermute | solution.py:478
  59.6 3.5 %collective-permute-done.11 = bf16[256,256]{1,0:T(8,128)(2,1)S(1)} collective-permute-done((bf16[256,256]{1,0:T(8,128)(2,1)S(1)}, bf16[256,256]{1,0:T(8,128)(2,1)S(1)}, u32[]{:S(2)}, u32[]{:S(2)}) %collective-permute-start.11) | collective-permute-done | bytes 131104 | tf_op jit(solution)/shard_map/ppermute | solution.py:478
  63.2 0.6 collective-permute-start.15
  63.8 0.0 collective-permute-start.13
  63.8 0.0 collective-permute-done.12
  63.8 0.6 collective-permute-start.14
  64.4 1.5 %collective-permute-start.16 = (bf16[384,256]{1,0:T(8,128)(2,1)S(1)}, bf16[384,256]{1,0:T(8,128)(2,1)S(1)}, u32[]{:S(2)}, u32[]{:S(2)}) collective-permute-start(bf16[384,256]{1,0:T(8,128)(2,1)S(1)} %pad_maximum_fusion.refs_1_), channel_id=1, source_target_pairs={{0,4},{4,0},{8,12},{12,8},{16,20},{20,16},{24,28},{28,24},{1,5},{5... | collective-permute-start | bytes 589832 | tf_op jit(solution)/shard_map/ppermute | solution.py:478
  65.8 0.0 collective-permute-done.13.refs_2_
  65.8 0.0 collective-permute-done.14.refs_3_
  65.9 0.0 copy-done
  65.9 2.4 %first_pieces.1 = (f32[256,1024]{1,0:T(8,128)}, f32[256,1024]{1,0:T(8,128)}, f32[1024,256]{1,0:T(8,128)}, f32[128,512]{1,0:T(8,128)S(1)}, bf16[128,128]{1,0:T(8,128)(2,1)S(1)}, /*index=5*/bf16[128,128]{1,0:T(8,128)(2,1)S(1)}) custom-call(s32[2]{0:T(128)S(1)} %pad_add_fusion.pos_ref, s32[1,8,16]{2,1,0:T(8,128)S(1)} %copy-done, bf16[512,256]{1,0:T(8,128)(2,1)} %x_hbm.5, ...), custom_call_target="tpu_custom_call" | custom-call | tf_op jit(solution)/shard_map/first_pieces/pallas_call | solution.py:709
  68.3 3.0 %collective-permute-done.16.refs_1_ = bf16[384,256]{1,0:T(8,128)(2,1)S(1)} collective-permute-done((bf16[384,256]{1,0:T(8,128)(2,1)S(1)}, bf16[384,256]{1,0:T(8,128)(2,1)S(1)}, u32[]{:S(2)}, u32[]{:S(2)}) %collective-permute-start.16) | collective-permute-done | bytes 196640 | tf_op jit(solution)/shard_map/ppermute | solution.py:478
  71.3 0.0 collective-permute-done.15.refs_0_
  71.3 0.0 collective-permute-start.17
  71.3 0.5 collective-permute-start.18
  71.8 1.6 %place.1 = (f32[256,1024]{1,0:T(8,128)}, f32[256,1024]{1,0:T(8,128)}, f32[1024,256]{1,0:T(8,128)}) custom-call(s32[2]{0:T(128)S(1)} %pad_add_fusion.pos_ref, bf16[464,256]{1,0:T(8,128)(2,1)S(1)} %collective-permute-done.15.refs_0_, bf16[384,256]{1,0:T(8,128)(2,1)S(1)} %collective-permute-done.16.refs_1_, ...), custom_call_target="tpu_custom_call", output_to_operand_aliasing={{0}: (3, {}), {1}: (4, {}), {2}: (5, {})} | custom-call | tf_op jit(solution)/shard_map/place/pallas_call | solution.py:720
  73.4 0.0 collective-permute-done.17.refs_0_
  73.4 0.0 collective-permute-done.18.refs_1_
  73.4 2.3 %finish.1 = (f32[256,1024]{1,0:T(8,128)}, f32[256,1024]{1,0:T(8,128)}, f32[1024,256]{1,0:T(8,128)}, bf16[128,256]{1,0:T(8,128)(2,1)}, bf16[128,256]{1,0:T(8,128)(2,1)}, /*index=5*/f32[1,1024]{1,0:T(1,128)}) custom-call(s32[2]{0:T(128)S(1)} %pad_add_fusion.pos_ref, ...), custom_call_target="tpu_custom_call", output_to_operand_aliasing={{0}: (10, {}), {1}: (11, {}), {2}: (12, {})} | custom-call | tf_op jit(solution)/shard_map/finish/pallas_call | solution.py:731
  (30 shorter events, 0.1 us)
Async XLA Ops:
  2.8 5.8 %collective-permute-start.3 = (s32[1,8,512]{2,1,0:T(8,128)S(1)}, s32[1,8,512]{2,1,0:T(8,128)S(1)}, u32[]{:S(2)}, u32[]{:S(2)}) collective-permute-start(s32[1,8,512]{2,1,0:T(8,128)S(1)} %get-tuple-element.61), channel_id=1, source_target_pairs={{0,1},{1,0},{2,3},{3,2},{4,5},{5,4},{6,7},{7,6},{8,9},{9,8},{10,11... | collective-permute-start | bytes 49160 | tf_op jit(solution)/shard_map/ppermute | solution.py:478
  3.3 7.1 %collective-permute-start = (bf16[2,16,512]{2,1,0:T(8,128)(2,1)S(1)}, bf16[2,16,512]{2,1,0:T(8,128)(2,1)S(1)}, u32[]{:S(2)}, u32[]{:S(2)}) collective-permute-start(bf16[2,16,512]{2,1,0:T(8,128)(2,1)S(1)} %get-tuple-element.58), channel_id=1, source_target_pairs={{0,8},{4,12},{8,0},{12,4},{16,24},{20,28},{24,16},{28,20},{1,9},{5... | collective-permute-start | bytes 98312 | tf_op jit(solution)/shard_map/ppermute | solution.py:478
  5.9 5.4 %collective-permute-start.1 = (bf16[2,16,512]{2,1,0:T(8,128)(2,1)S(1)}, bf16[2,16,512]{2,1,0:T(8,128)(2,1)S(1)}, u32[]{:S(2)}, u32[]{:S(2)}) collective-permute-start(bf16[2,16,512]{2,1,0:T(8,128)(2,1)S(1)} %get-tuple-element.59), channel_id=1, source_target_pairs={{0,16},{4,20},{8,24},{12,28},{16,0},{20,4},{24,8},{28,12},{1,17},{... | collective-permute-start | bytes 98312 | tf_op jit(solution)/shard_map/ppermute | solution.py:478
  8.5 5.7 %collective-permute-start.2 = (bf16[2,16,512]{2,1,0:T(8,128)(2,1)S(1)}, bf16[2,16,512]{2,1,0:T(8,128)(2,1)S(1)}, u32[]{:S(2)}, u32[]{:S(2)}) collective-permute-start(bf16[2,16,512]{2,1,0:T(8,128)(2,1)S(1)} %get-tuple-element.60), channel_id=1, source_target_pairs={{0,24},{4,28},{8,16},{12,20},{16,8},{20,12},{24,0},{28,4},{1,25},{... | collective-permute-start | bytes 98312 | tf_op jit(solution)/shard_map/ppermute | solution.py:478
  8.6 5.6 %collective-permute-start.4 = (s32[2,8,512]{2,1,0:T(8,128)S(1)}, s32[2,8,512]{2,1,0:T(8,128)S(1)}, u32[]{:S(2)}, u32[]{:S(2)}) collective-permute-start(s32[2,8,512]{2,1,0:T(8,128)S(1)} %constant_dynamic-update-slice_fusion.refs_0_), channel_id=1, source_target_pairs={{0,2},{1,3},{2,0},{3,1},{4,6},{5,7},{6,4},{7,5},{8,10},{9,11},{10,... | collective-permute-start | bytes 98312 | tf_op jit(solution)/shard_map/ppermute | solution.py:478
  17.0 4.3 %collective-permute-start.5 = (bf16[4,16,512]{2,1,0:T(8,128)(2,1)S(1)}, bf16[4,16,512]{2,1,0:T(8,128)(2,1)S(1)}, u32[]{:S(2)}, u32[]{:S(2)}) collective-permute-start(bf16[4,16,512]{2,1,0:T(8,128)(2,1)S(1)} %pad_maximum_fusion.3.after_ref), channel_id=1, source_target_pairs={{0,4},{4,0},{8,12},{12,8},{16,20},{20,16},{24,28},{28,24},{1,5},{5... | collective-permute-start | bytes 196616 | tf_op jit(solution)/shard_map/ppermute | solution.py:478
  29.0 16.9 %all-to-all-start = ((bf16[8,104,256]{2,1,0:T(8,128)(2,1)}), bf16[8,104,256]{2,1,0:T(8,128)(2,1)S(1)}, u32[]{:S(2)}, u32[]{:S(2)}) async-start(bf16[8,104,256]{2,1,0:T(8,128)(2,1)} %get-tuple-element.73), calls=%async_computation | async-start | bytes 851968 | tf_op jit(solution)/shard_map/all_to_all | solution.py:604
  37.8 28.0 %copy-start = (s32[1,8,16]{2,1,0:T(8,128)S(1)}, s32[1,8,16]{2,1,0:T(8,128)}, u32[]{:S(2)}) copy-start(s32[1,8,16]{2,1,0:T(8,128)} %idx_ref.1) | copy-start | bytes 1540
  37.8 1.7 %collective-permute-start.6 = (bf16[320,512]{1,0:T(8,128)(2,1)S(1)}, bf16[320,512]{1,0:T(8,128)(2,1)S(1)}, u32[]{:S(2)}, u32[]{:S(2)}) collective-permute-start(bf16[320,512]{1,0:T(8,128)(2,1)S(1)} %get-tuple-element.79), channel_id=1, source_target_pairs={{0,1},{1,0},{2,3},{3,2},{4,5},{5,4},{6,7},{7,6},{8,9},{9,8},{10,11... | collective-permute-start | bytes 983048 | tf_op jit(solution)/shard_map/ppermute | solution.py:478
  39.6 6.3 %collective-permute-start.7 = (bf16[160,512]{1,0:T(8,128)(2,1)S(1)}, bf16[160,512]{1,0:T(8,128)(2,1)S(1)}, u32[]{:S(2)}, u32[]{:S(2)}) collective-permute-start(bf16[160,512]{1,0:T(8,128)(2,1)S(1)} %get-tuple-element.81), channel_id=1, source_target_pairs={{0,2},{1,3},{2,0},{3,1},{4,6},{5,7},{6,4},{7,5},{8,10},{9,11},{10,... | collective-permute-start | bytes 491528 | tf_op jit(solution)/shard_map/ppermute | solution.py:478
  46.0 12.0 %collective-permute-start.8 = (bf16[112,256]{1,0:T(8,128)(2,1)S(1)}, bf16[112,256]{1,0:T(8,128)(2,1)S(1)}, u32[]{:S(2)}, u32[]{:S(2)}) collective-permute-start(bf16[112,256]{1,0:T(8,128)(2,1)S(1)} %get-tuple-element.84), channel_id=1, source_target_pairs={{0,8},{4,12},{8,0},{12,4},{16,24},{20,28},{24,16},{28,20},{1,9},{5... | collective-permute-start | bytes 172040 | tf_op jit(solution)/shard_map/ppermute | solution.py:478
  48.1 6.3 %collective-permute-start.9 = (bf16[112,256]{1,0:T(8,128)(2,1)S(1)}, bf16[112,256]{1,0:T(8,128)(2,1)S(1)}, u32[]{:S(2)}, u32[]{:S(2)}) collective-permute-start(bf16[112,256]{1,0:T(8,128)(2,1)S(1)} %get-tuple-element.85), channel_id=1, source_target_pairs={{0,16},{4,20},{8,24},{12,28},{16,0},{20,4},{24,8},{28,12},{1,17},{... | collective-permute-start | bytes 172040 | tf_op jit(solution)/shard_map/ppermute | solution.py:478
  50.5 6.0 %collective-permute-start.10 = (bf16[112,256]{1,0:T(8,128)(2,1)S(1)}, bf16[112,256]{1,0:T(8,128)(2,1)S(1)}, u32[]{:S(2)}, u32[]{:S(2)}) collective-permute-start(bf16[112,256]{1,0:T(8,128)(2,1)S(1)} %get-tuple-element.86), channel_id=1, source_target_pairs={{0,24},{4,28},{8,16},{12,20},{16,8},{20,12},{24,0},{28,4},{1,25},{... | collective-permute-start | bytes 172040 | tf_op jit(solution)/shard_map/ppermute | solution.py:478
  56.5 7.3 %collective-permute-start.12 = (bf16[192,256]{1,0:T(8,128)(2,1)S(1)}, bf16[192,256]{1,0:T(8,128)(2,1)S(1)}, u32[]{:S(2)}, u32[]{:S(2)}) collective-permute-start(bf16[192,256]{1,0:T(8,128)(2,1)S(1)} %pad_maximum_fusion.2), channel_id=1, source_target_pairs={{0,2},{1,3},{2,0},{3,1},{4,6},{5,7},{6,4},{7,5},{8,10},{9,11},{10,... | collective-permute-start | bytes 294920 | tf_op jit(solution)/shard_map/ppermute | solution.py:478
  58.1 5.0 %collective-permute-start.11 = (bf16[256,256]{1,0:T(8,128)(2,1)S(1)}, bf16[256,256]{1,0:T(8,128)(2,1)S(1)}, u32[]{:S(2)}, u32[]{:S(2)}) collective-permute-start(bf16[256,256]{1,0:T(8,128)(2,1)S(1)} %pad_maximum_fusion.1), channel_id=1, source_target_pairs={{0,4},{4,0},{8,12},{12,8},{16,20},{20,16},{24,28},{28,24},{1,5},{5... | collective-permute-start | bytes 393224 | tf_op jit(solution)/shard_map/ppermute | solution.py:478
  63.2 8.1 %collective-permute-start.15 = (bf16[464,256]{1,0:T(8,128)(2,1)S(1)}, bf16[464,256]{1,0:T(8,128)(2,1)S(1)}, u32[]{:S(2)}, u32[]{:S(2)}) collective-permute-start(bf16[464,256]{1,0:T(8,128)(2,1)S(1)} %get-tuple-element.125.refs_0_), channel_id=1, source_target_pairs={{0,2},{1,3},{2,0},{3,1},{4,6},{5,7},{6,4},{7,5},{8,10},{9,11},{10,... | collective-permute-start | bytes 712712 | tf_op jit(solution)/shard_map/ppermute | solution.py:478
  63.8 2.1 %collective-permute-start.13 = (bf16[464,256]{1,0:T(8,128)(2,1)S(1)}, bf16[464,256]{1,0:T(8,128)(2,1)S(1)}, u32[]{:S(2)}, u32[]{:S(2)}) collective-permute-start(bf16[464,256]{1,0:T(8,128)(2,1)S(1)} %get-tuple-element.125.refs_0_), channel_id=1, source_target_pairs={{0,1},{1,0},{2,3},{3,2},{4,5},{5,4},{6,7},{7,6},{8,9},{9,8},{10,11... | collective-permute-start | bytes 712712 | tf_op jit(solution)/shard_map/ppermute | solution.py:478
  63.8 2.0 %collective-permute-start.14 = (bf16[384,256]{1,0:T(8,128)(2,1)S(1)}, bf16[384,256]{1,0:T(8,128)(2,1)S(1)}, u32[]{:S(2)}, u32[]{:S(2)}) collective-permute-start(bf16[384,256]{1,0:T(8,128)(2,1)S(1)} %pad_maximum_fusion.refs_1_), channel_id=1, source_target_pairs={{0,1},{1,0},{2,3},{3,2},{4,5},{5,4},{6,7},{7,6},{8,9},{9,8},{10,11... | collective-permute-start | bytes 589832 | tf_op jit(solution)/shard_map/ppermute | solution.py:478
  64.4 6.9 %collective-permute-start.16 = (bf16[384,256]{1,0:T(8,128)(2,1)S(1)}, bf16[384,256]{1,0:T(8,128)(2,1)S(1)}, u32[]{:S(2)}, u32[]{:S(2)}) collective-permute-start(bf16[384,256]{1,0:T(8,128)(2,1)S(1)} %pad_maximum_fusion.refs_1_), channel_id=1, source_target_pairs={{0,4},{4,0},{8,12},{12,8},{16,20},{20,16},{24,28},{28,24},{1,5},{5... | collective-permute-start | bytes 589832 | tf_op jit(solution)/shard_map/ppermute | solution.py:478
  71.3 2.1 %collective-permute-start.17 = (bf16[464,256]{1,0:T(8,128)(2,1)S(1)}, bf16[464,256]{1,0:T(8,128)(2,1)S(1)}, u32[]{:S(2)}, u32[]{:S(2)}) collective-permute-start(bf16[464,256]{1,0:T(8,128)(2,1)S(1)} %collective-permute-done.15.refs_0_), channel_id=1, source_target_pairs={{0,1},{1,0},{2,3},{3,2},{4,5},{5,4},{6,7},{7,6},{8,9},{9,8},{10,11... | collective-permute-start | bytes 712712 | tf_op jit(solution)/shard_map/ppermute | solution.py:478
  71.3 2.2 %collective-permute-start.18 = (bf16[384,256]{1,0:T(8,128)(2,1)S(1)}, bf16[384,256]{1,0:T(8,128)(2,1)S(1)}, u32[]{:S(2)}, u32[]{:S(2)}) collective-permute-start(bf16[384,256]{1,0:T(8,128)(2,1)S(1)} %collective-permute-done.16.refs_1_), channel_id=1, source_target_pairs={{0,1},{1,0},{2,3},{3,2},{4,5},{5,4},{6,7},{7,6},{8,9},{9,8},{10,11... | collective-permute-start | bytes 589832 | tf_op jit(solution)/shard_map/ppermute | solution.py:478

commit v5 on v4

--- a/solution.py
+++ b/solution.py
@@ -318,18 +318,21 @@
         send_ref[part, slots:, :] = acc[of, feat:].astype(BF16)
 
 
-def pair_kernel(own_ref, far_ref, twin_ref, own_sum_ref, far_sum_ref):
+def pair_kernel(own_ref, far_ref, twin_ref, rows_ref, edges_ref, far_rows_ref, far_edges_ref):
     length = own_ref.shape[0]
-    own_sum_ref[...] = own_ref[...] + twin_ref[:length, :].astype(F32)
-    far_sum_ref[...] = (far_ref[...] + twin_ref[length:, :].astype(F32)).astype(BF16)
-
-
-def sum_kernel(got_ref, own_ref, *rest):
-    far_ref, *payloads, rows_ref, bias_ref = rest
-    total = own_ref[...] + far_ref[...].astype(F32)
-    share, wide = rows_ref.shape
-    feat = wide // 2
-    rows_ref[...] = total[:share]
+    share = rows_ref.shape[0]
+    own = own_ref[...] + twin_ref[:length, :].astype(F32)
+    far = far_ref[...] + twin_ref[length:, :].astype(F32)
+    rows_ref[...] = own[:share]
+    edges_ref[...] = own[share:]
+    far_rows_ref[...] = far[:share].astype(BF16)
+    far_edges_ref[...] = far[share:].astype(BF16)
+
+
+def sum_kernel(got_ref, edges_ref, far_ref, *rest):
+    *payloads, bias_ref = rest
+    total = edges_ref[...] + far_ref[...].astype(F32)
+    feat = total.shape[1] // 2
     piece = got_ref[0].astype(F32)
     for part in range(1, got_ref.shape[0]):
         piece += got_ref[part].astype(F32)
@@ -338,7 +341,7 @@
     for k, payload in enumerate(payloads):
         edges = []
         for odd in range(2):
-            at = share + 4 * (2 * k + odd)
+            at = 4 * (2 * k + odd)
             edges += [total[at : at + 4, :feat], total[at : at + 4, feat:]]
         payload[...] = jnp.concatenate([piece[:rows]] + edges, axis=0).astype(BF16)
 
@@ -375,7 +378,7 @@
     return jnp.concatenate([edge[:64, :] for edge in edges], axis=0)
 
 
-def first_kernel(tags, pos_ref, idx_ref, x_hbm, g_hbm, rows_ref, *refs):
+def first_kernel(tags, pos_ref, idx_ref, x_hbm, g_hbm, rows_ref, far_ref, *refs):
     ins, refs = refs[: len(tags)], refs[len(tags) :]
     edges, refs = refs[:2], refs[2:]
     grads, (total_ref, pick_y_ref, pick_x_ref, buffer, sems, x_ref, g_ref, row_sems) = refs[:3], refs[3:]
@@ -397,8 +400,9 @@
     halo = edge_rows(edges)
     for copy in copies:
         copy.wait()
-    total_ref[:, :feat] = x_ref[...].astype(F32) + rows_ref[:, :feat] + dot_nn(pick_y[:, :128], halo)
-    total_ref[:, feat:] = g_ref[...].astype(F32) + rows_ref[:, feat:] + dot_nn(pick_x[:, :128], halo)
+    rows = rows_ref[...] + far_ref[...].astype(F32)
+    total_ref[:, :feat] = x_ref[...].astype(F32) + rows[:, :feat] + dot_nn(pick_y[:, :128], halo)
+    total_ref[:, feat:] = g_ref[...].astype(F32) + rows[:, feat:] + dot_nn(pick_x[:, :128], halo)
     for copy in placed:
         copy.wait()
 
@@ -666,25 +670,34 @@
         return (updated, cell_grad, grad_in, grad_net, grad_bias, grad_out)
 
     own, far, twin_share = outs
-    own, far = pl.pallas_call(
+    rows, edges, far_rows, far_edges = pl.pallas_call(
         pair_kernel,
         in_specs=whole(3),
-        out_specs=whole(2),
-        out_shape=[shape(F32, length, 2 * feat), shape(BF16, length, 2 * feat)],
+        out_specs=whole(4),
+        out_shape=[
+            shape(F32, share, 2 * feat),
+            shape(F32, edge, 2 * feat),
+            shape(BF16, share, 2 * feat),
+            shape(BF16, edge, 2 * feat),
+        ],
         name="pairs",
         **PARAMS,
     )(own, far, flip(twin_share, "net", 1))
     rows_of = 3 * part
-    *pays, rows, bias_sum = pl.pallas_call(
+    *pays, bias_sum = pl.pallas_call(
         sum_kernel,
         in_specs=whole(3),
-        out_specs=whole(6),
-        out_shape=[shape(BF16, rows_of + 16, feat)] * 4 + [shape(F32, share, 2 * feat), shape(BF16, 16, feat)],
+        out_specs=whole(5),
+        out_shape=[shape(BF16, rows_of + 16, feat)] * 4 + [shape(BF16, 16, feat)],
         name="sums",
         cost_estimate=about(0.2),
         **PARAMS,
-    )(got, own, flip(far, "net", 2))
+    )(got, edges, flip(far_edges, "net", 2))
+    far_rows, first_pay = lax.optimization_barrier((far_rows, pays[0]))
+    far_rows = flip(far_rows, "net", 2)
+    pays = [first_pay] + pays[1:]
     near = [pays[0]] + [flip(pays[k], "cell", 2 * k) for k in (1, 2, 3)]
+    near, far_rows = lax.optimization_barrier((near, far_rows))
     across = flip(jnp.concatenate(near[:2] + [a[rows_of:] for a in near[2:]]), "cell", 1)
     second = jnp.concatenate([a[:rows_of] for a in near[2:]])
     second = jnp.concatenate([second, flip(second, "net", 2)])
@@ -708,13 +721,13 @@
 
     *grads, total, pick_y, pick_x = pl.pallas_call(
         functools.partial(first_kernel, early_tags + twin(early_tags)),
-        in_specs=[SMEM] + whole(1) + [HBM] * 2 + whole(1 + 4 + 2),
+        in_specs=[SMEM] + whole(1) + [HBM] * 2 + whole(2 + 4 + 2),
         out_specs=[HBM] * 3 + whole(3),
         out_shape=grad_shapes + [shape(F32, share, 2 * feat)] + [shape(BF16, share, 128)] * 2,
         scratch_shapes=scratch([0] * 4) + row_scratch,
         name="first_pieces",
         **PARAMS,
-    )(pos, send_idx, *in_hbm(cell_feat, out_grad), rows, first, second, *early, first[4 * rows_of :], early[0][4 * rows_of :])
+    )(pos, send_idx, *in_hbm(cell_feat, out_grad), rows, far_rows, first, second, *early, first[4 * rows_of :], early[0][4 * rows_of :])
     third, fourth, grads = lax.optimization_barrier((third, fourth, grads))
     late = [flip(third, "net", 1), flip(fourth, "net", 1)]
     grads = pl.pallas_call(

time: 76.3 us -> 75.5 us (0.990)
  waiting for transfers between devices: 22.7 us -> 20.5 us
  starting transfers between devices: 25.9 us -> 27.4 us
    ppermute x19 -> x20, waiting for transfers between devices: 22.7 us -> 20.5 us  [flip(): return lax.ppermute(x, axis, [(i, i ^ bits) for i in range(size)])]
    ppermute x19 -> x20, starting transfers between devices: 21.5 us -> 23 us  [flip(): return lax.ppermute(x, axis, [(i, i ^ bits) for i in range(size)])]
  transfers between devices with their start and end apart: 20 -> 21, of which waited for: 9 -> 10; matrix products, arithmetic and copies ran while one was open for 0% -> 0% of each run, Pallas kernels for 15% -> 15%
where the time goes in v5:
time: 75.5 us; the launch traced here: 75.1 us
  starting transfers between devices  27.4 us (36%)
  Pallas kernels  25.4 us (34%)
  waiting for transfers between devices  20.5 us (27%)
  between operations  1.7 us (2%)
    ppermute x20, starting transfers between devices, flip(): return lax.ppermute(x, axis, [(i, i ^ bits) for i in range(size)])  23 us
    ppermute x20, waiting for transfers between devices, flip(): return lax.ppermute(x, axis, [(i, i ^ bits) for i in range(size)])  20.5 us
    pallas_call x1, Pallas kernels, local(): pl.pallas_call(functools.partial(layer_kernel, fast, len(halo)), in_specs...  7.68 us
    pallas_call x1, Pallas kernels, local(): pl.pallas_call(functools.partial(back_kernel, fast), in_specs=[SMEM] + [H...  4.47 us
    all_to_all x1, starting transfers between devices, local(): got = lax.all_to_all(grads, 'cell', split_axis=0, concat_axis=0, tiled=True)  4.36 us
    pallas_call x1, Pallas kernels, local(): pl.pallas_call(functools.partial(spread_kernel, fast, slots), in_specs=[S...  2.68 us
    pallas_call x1, Pallas kernels, local(): pl.pallas_call(own_pins_kernel, in_specs=[pl.BlockSpec(memory_space=pl.AN...  2.56 us
    pallas_call x1, Pallas kernels, local(): pl.pallas_call(functools.partial(first_kernel, early_tags + twin(early_ta...  2.41 us
  transfers between devices with their start and end apart: 21, of which 10 were waited for; matrix products, arithmetic and copies ran while one was open for 0% of the time, Pallas kernels for 15%

profile of v5, /device:TPU:0, one launch (start us, length us, event | category | flops | bytes accessed | tf_op | source)
XLA Modules:
  0.0 75.1 jit_solution(11124256495324952091)
XLA Ops:
  1.3 1.5 %take_boundary.1 = (s32[1,8,512]{2,1,0:T(8,128)S(1)}, bf16[2,16,512]{2,1,0:T(8,128)(2,1)S(1)}, bf16[2,16,512]{2,1,0:T(8,128)(2,1)S(1)}, bf16[2,16,512]{2,1,0:T(8,128)(2,1)S(1)}, bf16[2,16,512]{2,1,0:T(8,128)(2,1)S(1)}) custom-call(s32[1,1]{1,0:T(1,128)S(6)} %copy.49.count_ref, s32[1,8,16]{2,1,0:T(8,128)} %idx_ref.1, bf16[512,256]{1,0:T(8,128)(2,1)} %x_hbm.5, ...), custom_call_target="tpu_custom_call" | custom-call | bytes 7200000 | tf_op jit(solution)/shard_map/take_boundary/pallas_call | solution.py:512
  2.8 0.5 collective-permute-start
  3.3 2.6 %collective-permute-start.2 = (bf16[2,16,512]{2,1,0:T(8,128)(2,1)S(1)}, bf16[2,16,512]{2,1,0:T(8,128)(2,1)S(1)}, u32[]{:S(2)}, u32[]{:S(2)}) collective-permute-start(bf16[2,16,512]{2,1,0:T(8,128)(2,1)S(1)} %get-tuple-element.68), channel_id=1, source_target_pairs={{0,8},{4,12},{8,0},{12,4},{16,24},{20,28},{24,16},{28,20},{1,9},{5... | collective-permute-start | bytes 98312 | tf_op jit(solution)/shard_map/ppermute | solution.py:482
  5.9 2.6 %collective-permute-start.3 = (bf16[2,16,512]{2,1,0:T(8,128)(2,1)S(1)}, bf16[2,16,512]{2,1,0:T(8,128)(2,1)S(1)}, u32[]{:S(2)}, u32[]{:S(2)}) collective-permute-start(bf16[2,16,512]{2,1,0:T(8,128)(2,1)S(1)} %get-tuple-element.69), channel_id=1, source_target_pairs={{0,16},{4,20},{8,24},{12,28},{16,0},{20,4},{24,8},{28,12},{1,17},{... | collective-permute-start | bytes 98312 | tf_op jit(solution)/shard_map/ppermute | solution.py:482
  8.5 0.0 collective-permute-start.4
  8.5 0.1 pad_add_fusion.pos_ref
  8.6 0.0 collective-permute-done
  8.6 1.8 %collective-permute-start.1 = (s32[2,8,512]{2,1,0:T(8,128)S(1)}, s32[2,8,512]{2,1,0:T(8,128)S(1)}, u32[]{:S(2)}, u32[]{:S(2)}) collective-permute-start(s32[2,8,512]{2,1,0:T(8,128)S(1)} %constant_dynamic-update-slice_fusion.refs_0_), channel_id=1, source_target_pairs={{0,2},{1,3},{2,0},{3,1},{4,6},{5,7},{6,4},{7,5},{8,10},{9,11},{10,... | collective-permute-start | bytes 98312 | tf_op jit(solution)/shard_map/ppermute | solution.py:482
  10.4 0.0 collective-permute-done.2.refs_1_
  10.4 0.9 %collective-permute-done.3.refs_2_ = bf16[2,16,512]{2,1,0:T(8,128)(2,1)S(1)} collective-permute-done((bf16[2,16,512]{2,1,0:T(8,128)(2,1)S(1)}, bf16[2,16,512]{2,1,0:T(8,128)(2,1)S(1)}, u32[]{:S(2)}, u32[]{:S(2)}) %collective-permute-start.3) | collective-permute-done | bytes 32800 | tf_op jit(solution)/shard_map/ppermute | solution.py:482
  11.3 2.9 %collective-permute-done.4.refs_3_ = bf16[2,16,512]{2,1,0:T(8,128)(2,1)S(1)} collective-permute-done((bf16[2,16,512]{2,1,0:T(8,128)(2,1)S(1)}, bf16[2,16,512]{2,1,0:T(8,128)(2,1)S(1)}, u32[]{:S(2)}, u32[]{:S(2)}) %collective-permute-start.4) | collective-permute-done | bytes 32800 | tf_op jit(solution)/shard_map/ppermute | solution.py:482
  14.3 0.0 collective-permute-done.1.refs_1_
  14.3 2.7 %spread.1 = (f32[16,512]{1,0:T(8,128)}, bf16[2560,512]{1,0:T(8,128)(2,1)S(1)}, bf16[640,2560]{1,0:T(8,128)(2,1)S(1)}, bf16[2560,128]{1,0:T(8,128)(2,1)S(1)}, bf1...) custom-call(s32[2]{0:T(128)S(1)} %pad_add_fusion.pos_ref, ...), custom_call_target="tpu_custom_call" | custom-call | bytes 16200000 | tf_op jit(solution)/shard_map/spread/pallas_call | solution.py:554
  17.0 1.6 %collective-permute-start.5 = (bf16[4,16,512]{2,1,0:T(8,128)(2,1)S(1)}, bf16[4,16,512]{2,1,0:T(8,128)(2,1)S(1)}, u32[]{:S(2)}, u32[]{:S(2)}) collective-permute-start(bf16[4,16,512]{2,1,0:T(8,128)(2,1)S(1)} %pad_maximum_fusion.3.after_ref), channel_id=1, source_target_pairs={{0,4},{4,0},{8,12},{12,8},{16,20},{20,16},{24,28},{28,24},{1,5},{5... | collective-permute-start | bytes 196616 | tf_op jit(solution)/shard_map/ppermute | solution.py:482
  18.5 2.6 %own_pins.1.refs_13_ = bf16[2560,512]{1,0:T(8,128)(2,1)S(1)} custom-call(bf16[4,16,512]{2,1,0:T(8,128)(2,1)S(1)} %pad_maximum_fusion.3.after_ref, bf16[2560,512]{1,0:T(8,128)(2,1)S(1)} %get-tuple-element.81.at_pin, bf16[512,256]{1,0:T(8,128)(2,1)} %x_hbm.5, bf16[512,256]{1,0:T(8,128)(2,1)} %g_hbm.5), custom_call_target="tpu_custom_call" | custom-call | bytes 9000000 | tf_op jit(solution)/shard_map/own_pins/pallas_call | solution.py:572
  21.1 0.2 collective-permute-done.5.refs_4_
  21.3 7.7 %layer.1 = (bf16[8,104,256]{2,1,0:T(8,128)(2,1)}, f32[640,512]{1,0:T(8,128)}, bf16[640,256]{1,0:T(8,128)(2,1)}) custom-call(bf16[2,16,512]{2,1,0:T(8,128)(2,1)S(1)} %get-tuple-element.67.refs_0_, bf16[2,16,512]{2,1,0:T(8,128)(2,1)S(1)} %collective-permute-done.2.refs_1_, bf16[2,16,512]{2,1,0:T(8,128)(2,1)S(1)} %collective-permute-done.3.refs_2_, ...), custom_call_target="tpu_custom_call" | custom-call | bytes 27720000 | tf_op jit(solution)/shard_map/layer/pallas_call | solution.py:583
  29.0 4.4 %all-to-all-start = ((bf16[8,104,256]{2,1,0:T(8,128)(2,1)}), bf16[8,104,256]{2,1,0:T(8,128)(2,1)S(1)}, u32[]{:S(2)}, u32[]{:S(2)}) async-start(bf16[8,104,256]{2,1,0:T(8,128)(2,1)} %get-tuple-element.89), calls=%async_computation | async-start | bytes 851968 | tf_op jit(solution)/shard_map/all_to_all | solution.py:608
  33.4 0.0 copy-start
  33.4 4.5 %back.1 = (f32[160,512]{1,0:T(8,128)S(1)}, f32[160,512]{1,0:T(8,128)S(1)}, bf16[320,512]{1,0:T(8,128)(2,1)S(1)}) custom-call(s32[2]{0:T(128)S(1)} %pad_add_fusion.pos_ref, f32[16,512]{1,0:T(8,128)} %get-tuple-element.66.ids_hbm, f32[640,512]{1,0:T(8,128)} %get-tuple-element.82.sums_hbm, bf16[640,256]{1,0:T(8,128)(2,1)} %get-tuple-element.83.net_grads_hbm, ...), custom_call_target="tpu_custom_call" | custom-call | bytes 16559999 | tf_op jit(solution)/shard_map/back/pallas_call | solution.py:613
  37.8 0.1 collective-permute-start.6
  37.9 1.6 %collective-permute-done.6.twin_ref = bf16[320,512]{1,0:T(8,128)(2,1)S(1)} collective-permute-done((bf16[320,512]{1,0:T(8,128)(2,1)S(1)}, bf16[320,512]{1,0:T(8,128)(2,1)S(1)}, u32[]{:S(2)}, u32[]{:S(2)}) %collective-permute-start.6) | collective-permute-done | bytes 327712 | tf_op jit(solution)/shard_map/ppermute | solution.py:482
  39.5 0.1 pairs.1
  39.6 1.6 %collective-permute-start.7 = (bf16[32,512]{1,0:T(8,128)(2,1)S(1)}, bf16[32,512]{1,0:T(8,128)(2,1)S(1)}, u32[]{:S(2)}, u32[]{:S(2)}) collective-permute-start(bf16[32,512]{1,0:T(8,128)(2,1)S(1)} %get-tuple-element.91), channel_id=1, source_target_pairs={{0,2},{1,3},{2,0},{3,1},{4,6},{5,7},{6,4},{7,5},{8,10},{9,11},{10,... | collective-permute-start | bytes 98312 | tf_op jit(solution)/shard_map/ppermute | solution.py:482
  41.2 2.4 %collective-permute-done.7.far_ref = bf16[32,512]{1,0:T(8,128)(2,1)S(1)} collective-permute-done((bf16[32,512]{1,0:T(8,128)(2,1)S(1)}, bf16[32,512]{1,0:T(8,128)(2,1)S(1)}, u32[]{:S(2)}, u32[]{:S(2)}) %collective-permute-start.7) | collective-permute-done | bytes 32800 | tf_op jit(solution)/shard_map/ppermute | solution.py:482
  43.6 0.0 all-to-all-done.got_ref
  43.6 0.1 sums.1
  43.7 1.6 %collective-permute-start.11 = (bf16[128,512]{1,0:T(8,128)(2,1)S(1)}, bf16[128,512]{1,0:T(8,128)(2,1)S(1)}, u32[]{:S(2)}, u32[]{:S(2)}) collective-permute-start(bf16[128,512]{1,0:T(8,128)(2,1)S(1)} %get-tuple-element.97), channel_id=1, source_target_pairs={{0,2},{1,3},{2,0},{3,1},{4,6},{5,7},{6,4},{7,5},{8,10},{9,11},{10,... | collective-permute-start | bytes 393224 | tf_op jit(solution)/shard_map/ppermute | solution.py:482
  45.3 2.0 %collective-permute-start.8 = (bf16[112,256]{1,0:T(8,128)(2,1)S(1)}, bf16[112,256]{1,0:T(8,128)(2,1)S(1)}, u32[]{:S(2)}, u32[]{:S(2)}) collective-permute-start(bf16[112,256]{1,0:T(8,128)(2,1)S(1)} %get-tuple-element.94), channel_id=1, source_target_pairs={{0,8},{4,12},{8,0},{12,4},{16,24},{20,28},{24,16},{28,20},{1,9},{5... | collective-permute-start | bytes 172040 | tf_op jit(solution)/shard_map/ppermute | solution.py:482
  47.3 2.4 %collective-permute-start.9 = (bf16[112,256]{1,0:T(8,128)(2,1)S(1)}, bf16[112,256]{1,0:T(8,128)(2,1)S(1)}, u32[]{:S(2)}, u32[]{:S(2)}) collective-permute-start(bf16[112,256]{1,0:T(8,128)(2,1)S(1)} %get-tuple-element.95), channel_id=1, source_target_pairs={{0,16},{4,20},{8,24},{12,28},{16,0},{20,4},{24,8},{28,12},{1,17},{... | collective-permute-start | bytes 172040 | tf_op jit(solution)/shard_map/ppermute | solution.py:482
  49.6 0.0 collective-permute-start.10
  49.6 0.2 collective-permute-done.8
  49.9 3.7 %collective-permute-done.9 = bf16[112,256]{1,0:T(8,128)(2,1)S(1)} collective-permute-done((bf16[112,256]{1,0:T(8,128)(2,1)S(1)}, bf16[112,256]{1,0:T(8,128)(2,1)S(1)}, u32[]{:S(2)}, u32[]{:S(2)}) %collective-permute-start.9) | collective-permute-done | bytes 57376 | tf_op jit(solution)/shard_map/ppermute | solution.py:482
  53.6 2.0 %collective-permute-done.10 = bf16[112,256]{1,0:T(8,128)(2,1)S(1)} collective-permute-done((bf16[112,256]{1,0:T(8,128)(2,1)S(1)}, bf16[112,256]{1,0:T(8,128)(2,1)S(1)}, u32[]{:S(2)}, u32[]{:S(2)}) %collective-permute-start.10) | collective-permute-done | bytes 57376 | tf_op jit(solution)/shard_map/ppermute | solution.py:482
  55.6 0.0 collective-permute-done.11.far_ref
  55.7 0.6 collective-permute-start.13
  56.2 1.5 %collective-permute-start.12 = (bf16[256,256]{1,0:T(8,128)(2,1)S(1)}, bf16[256,256]{1,0:T(8,128)(2,1)S(1)}, u32[]{:S(2)}, u32[]{:S(2)}) collective-permute-start(bf16[256,256]{1,0:T(8,128)(2,1)S(1)} %pad_maximum_fusion.1), channel_id=1, source_target_pairs={{0,4},{4,0},{8,12},{12,8},{16,20},{20,16},{24,28},{28,24},{1,5},{5... | collective-permute-start | bytes 393224 | tf_op jit(solution)/shard_map/ppermute | solution.py:482
  57.8 3.5 %collective-permute-done.12 = bf16[256,256]{1,0:T(8,128)(2,1)S(1)} collective-permute-done((bf16[256,256]{1,0:T(8,128)(2,1)S(1)}, bf16[256,256]{1,0:T(8,128)(2,1)S(1)}, u32[]{:S(2)}, u32[]{:S(2)}) %collective-permute-start.12) | collective-permute-done | bytes 131104 | tf_op jit(solution)/shard_map/ppermute | solution.py:482
  61.4 1.6 %collective-permute-start.16 = (bf16[464,256]{1,0:T(8,128)(2,1)S(1)}, bf16[464,256]{1,0:T(8,128)(2,1)S(1)}, u32[]{:S(2)}, u32[]{:S(2)}) collective-permute-start(bf16[464,256]{1,0:T(8,128)(2,1)S(1)} %get-tuple-element.141.refs_0_), channel_id=1, source_target_pairs={{0,2},{1,3},{2,0},{3,1},{4,6},{5,7},{6,4},{7,5},{8,10},{9,11},{10,... | collective-permute-start | bytes 712712 | tf_op jit(solution)/shard_map/ppermute | solution.py:482
  63.0 0.0 collective-permute-start.14
  63.0 0.0 collective-permute-done.13
  63.0 0.6 collective-permute-start.15
  63.6 1.5 %collective-permute-start.17 = (bf16[384,256]{1,0:T(8,128)(2,1)S(1)}, bf16[384,256]{1,0:T(8,128)(2,1)S(1)}, u32[]{:S(2)}, u32[]{:S(2)}) collective-permute-start(bf16[384,256]{1,0:T(8,128)(2,1)S(1)} %pad_maximum_fusion.refs_1_), channel_id=1, source_target_pairs={{0,4},{4,0},{8,12},{12,8},{16,20},{20,16},{24,28},{28,24},{1,5},{5... | collective-permute-start | bytes 589832 | tf_op jit(solution)/shard_map/ppermute | solution.py:482
  65.0 0.0 collective-permute-done.14.refs_2_
  65.1 0.0 collective-permute-done.15.refs_3_
  65.1 0.0 copy-done
  65.1 2.4 %first_pieces.1 = (f32[256,1024]{1,0:T(8,128)}, f32[256,1024]{1,0:T(8,128)}, f32[1024,256]{1,0:T(8,128)}, f32[128,512]{1,0:T(8,128)S(1)}, bf16[128,128]{1,0:T(8,128)(2,1)S(1)}, /*index=5*/bf16[128,128]{1,0:T(8,128)(2,1)S(1)}) custom-call(s32[2]{0:T(128)S(1)} %pad_add_fusion.pos_ref, s32[1,8,16]{2,1,0:T(8,128)S(1)} %copy-done, bf16[512,256]{1,0:T(8,128)(2,1)} %x_hbm.5, ...), custom_call_target="tpu_custom_call" | custom-call | tf_op jit(solution)/shard_map/first_pieces/pallas_call | solution.py:722
  67.5 3.0 %collective-permute-done.17.refs_1_ = bf16[384,256]{1,0:T(8,128)(2,1)S(1)} collective-permute-done((bf16[384,256]{1,0:T(8,128)(2,1)S(1)}, bf16[384,256]{1,0:T(8,128)(2,1)S(1)}, u32[]{:S(2)}, u32[]{:S(2)}) %collective-permute-start.17) | collective-permute-done | bytes 196640 | tf_op jit(solution)/shard_map/ppermute | solution.py:482
  70.5 0.0 collective-permute-done.16.refs_0_
  70.5 0.0 collective-permute-start.18
  70.5 0.5 collective-permute-start.19
  71.0 1.6 %place.1 = (f32[256,1024]{1,0:T(8,128)}, f32[256,1024]{1,0:T(8,128)}, f32[1024,256]{1,0:T(8,128)}) custom-call(s32[2]{0:T(128)S(1)} %pad_add_fusion.pos_ref, bf16[464,256]{1,0:T(8,128)(2,1)S(1)} %collective-permute-done.16.refs_0_, bf16[384,256]{1,0:T(8,128)(2,1)S(1)} %collective-permute-done.17.refs_1_, ...), custom_call_target="tpu_custom_call", output_to_operand_aliasing={{0}: (3, {}), {1}: (4, {}), {2}: (5, {})} | custom-call | tf_op jit(solution)/shard_map/place/pallas_call | solution.py:733
  72.6 0.0 collective-permute-done.18.refs_0_
  72.6 0.0 collective-permute-done.19.refs_1_
  72.6 2.3 %finish.1 = (f32[256,1024]{1,0:T(8,128)}, f32[256,1024]{1,0:T(8,128)}, f32[1024,256]{1,0:T(8,128)}, bf16[128,256]{1,0:T(8,128)(2,1)}, bf16[128,256]{1,0:T(8,128)(2,1)}, /*index=5*/f32[1,1024]{1,0:T(1,128)}) custom-call(s32[2]{0:T(128)S(1)} %pad_add_fusion.pos_ref, ...), custom_call_target="tpu_custom_call", output_to_operand_aliasing={{0}: (10, {}), {1}: (11, {}), {2}: (12, {})} | custom-call | tf_op jit(solution)/shard_map/finish/pallas_call | solution.py:744
  (30 shorter events, 0.1 us)
Async XLA Ops:
  2.8 5.8 %collective-permute-start = (s32[1,8,512]{2,1,0:T(8,128)S(1)}, s32[1,8,512]{2,1,0:T(8,128)S(1)}, u32[]{:S(2)}, u32[]{:S(2)}) collective-permute-start(s32[1,8,512]{2,1,0:T(8,128)S(1)} %get-tuple-element.65), channel_id=1, source_target_pairs={{0,1},{1,0},{2,3},{3,2},{4,5},{5,4},{6,7},{7,6},{8,9},{9,8},{10,11... | collective-permute-start | bytes 49160 | tf_op jit(solution)/shard_map/ppermute | solution.py:482
  3.3 7.1 %collective-permute-start.2 = (bf16[2,16,512]{2,1,0:T(8,128)(2,1)S(1)}, bf16[2,16,512]{2,1,0:T(8,128)(2,1)S(1)}, u32[]{:S(2)}, u32[]{:S(2)}) collective-permute-start(bf16[2,16,512]{2,1,0:T(8,128)(2,1)S(1)} %get-tuple-element.68), channel_id=1, source_target_pairs={{0,8},{4,12},{8,0},{12,4},{16,24},{20,28},{24,16},{28,20},{1,9},{5... | collective-permute-start | bytes 98312 | tf_op jit(solution)/shard_map/ppermute | solution.py:482
  5.9 5.4 %collective-permute-start.3 = (bf16[2,16,512]{2,1,0:T(8,128)(2,1)S(1)}, bf16[2,16,512]{2,1,0:T(8,128)(2,1)S(1)}, u32[]{:S(2)}, u32[]{:S(2)}) collective-permute-start(bf16[2,16,512]{2,1,0:T(8,128)(2,1)S(1)} %get-tuple-element.69), channel_id=1, source_target_pairs={{0,16},{4,20},{8,24},{12,28},{16,0},{20,4},{24,8},{28,12},{1,17},{... | collective-permute-start | bytes 98312 | tf_op jit(solution)/shard_map/ppermute | solution.py:482
  8.5 5.7 %collective-permute-start.4 = (bf16[2,16,512]{2,1,0:T(8,128)(2,1)S(1)}, bf16[2,16,512]{2,1,0:T(8,128)(2,1)S(1)}, u32[]{:S(2)}, u32[]{:S(2)}) collective-permute-start(bf16[2,16,512]{2,1,0:T(8,128)(2,1)S(1)} %get-tuple-element.70), channel_id=1, source_target_pairs={{0,24},{4,28},{8,16},{12,20},{16,8},{20,12},{24,0},{28,4},{1,25},{... | collective-permute-start | bytes 98312 | tf_op jit(solution)/shard_map/ppermute | solution.py:482
  8.6 5.6 %collective-permute-start.1 = (s32[2,8,512]{2,1,0:T(8,128)S(1)}, s32[2,8,512]{2,1,0:T(8,128)S(1)}, u32[]{:S(2)}, u32[]{:S(2)}) collective-permute-start(s32[2,8,512]{2,1,0:T(8,128)S(1)} %constant_dynamic-update-slice_fusion.refs_0_), channel_id=1, source_target_pairs={{0,2},{1,3},{2,0},{3,1},{4,6},{5,7},{6,4},{7,5},{8,10},{9,11},{10,... | collective-permute-start | bytes 98312 | tf_op jit(solution)/shard_map/ppermute | solution.py:482
  17.0 4.3 %collective-permute-start.5 = (bf16[4,16,512]{2,1,0:T(8,128)(2,1)S(1)}, bf16[4,16,512]{2,1,0:T(8,128)(2,1)S(1)}, u32[]{:S(2)}, u32[]{:S(2)}) collective-permute-start(bf16[4,16,512]{2,1,0:T(8,128)(2,1)S(1)} %pad_maximum_fusion.3.after_ref), channel_id=1, source_target_pairs={{0,4},{4,0},{8,12},{12,8},{16,20},{20,16},{24,28},{28,24},{1,5},{5... | collective-permute-start | bytes 196616 | tf_op jit(solution)/shard_map/ppermute | solution.py:482
  29.0 14.6 %all-to-all-start = ((bf16[8,104,256]{2,1,0:T(8,128)(2,1)}), bf16[8,104,256]{2,1,0:T(8,128)(2,1)S(1)}, u32[]{:S(2)}, u32[]{:S(2)}) async-start(bf16[8,104,256]{2,1,0:T(8,128)(2,1)} %get-tuple-element.89), calls=%async_computation | async-start | bytes 851968 | tf_op jit(solution)/shard_map/all_to_all | solution.py:608
  33.4 31.7 %copy-start = (s32[1,8,16]{2,1,0:T(8,128)S(1)}, s32[1,8,16]{2,1,0:T(8,128)}, u32[]{:S(2)}) copy-start(s32[1,8,16]{2,1,0:T(8,128)} %idx_ref.1) | copy-start | bytes 1540
  37.8 1.7 %collective-permute-start.6 = (bf16[320,512]{1,0:T(8,128)(2,1)S(1)}, bf16[320,512]{1,0:T(8,128)(2,1)S(1)}, u32[]{:S(2)}, u32[]{:S(2)}) collective-permute-start(bf16[320,512]{1,0:T(8,128)(2,1)S(1)} %get-tuple-element.86), channel_id=1, source_target_pairs={{0,1},{1,0},{2,3},{3,2},{4,5},{5,4},{6,7},{7,6},{8,9},{9,8},{10,11... | collective-permute-start | bytes 983048 | tf_op jit(solution)/shard_map/ppermute | solution.py:482
  39.6 4.0 %collective-permute-start.7 = (bf16[32,512]{1,0:T(8,128)(2,1)S(1)}, bf16[32,512]{1,0:T(8,128)(2,1)S(1)}, u32[]{:S(2)}, u32[]{:S(2)}) collective-permute-start(bf16[32,512]{1,0:T(8,128)(2,1)S(1)} %get-tuple-element.91), channel_id=1, source_target_pairs={{0,2},{1,3},{2,0},{3,1},{4,6},{5,7},{6,4},{7,5},{8,10},{9,11},{10,... | collective-permute-start | bytes 98312 | tf_op jit(solution)/shard_map/ppermute | solution.py:482
  43.7 12.0 %collective-permute-start.11 = (bf16[128,512]{1,0:T(8,128)(2,1)S(1)}, bf16[128,512]{1,0:T(8,128)(2,1)S(1)}, u32[]{:S(2)}, u32[]{:S(2)}) collective-permute-start(bf16[128,512]{1,0:T(8,128)(2,1)S(1)} %get-tuple-element.97), channel_id=1, source_target_pairs={{0,2},{1,3},{2,0},{3,1},{4,6},{5,7},{6,4},{7,5},{8,10},{9,11},{10,... | collective-permute-start | bytes 393224 | tf_op jit(solution)/shard_map/ppermute | solution.py:482
  45.3 4.6 %collective-permute-start.8 = (bf16[112,256]{1,0:T(8,128)(2,1)S(1)}, bf16[112,256]{1,0:T(8,128)(2,1)S(1)}, u32[]{:S(2)}, u32[]{:S(2)}) collective-permute-start(bf16[112,256]{1,0:T(8,128)(2,1)S(1)} %get-tuple-element.94), channel_id=1, source_target_pairs={{0,8},{4,12},{8,0},{12,4},{16,24},{20,28},{24,16},{28,20},{1,9},{5... | collective-permute-start | bytes 172040 | tf_op jit(solution)/shard_map/ppermute | solution.py:482
  47.3 6.3 %collective-permute-start.9 = (bf16[112,256]{1,0:T(8,128)(2,1)S(1)}, bf16[112,256]{1,0:T(8,128)(2,1)S(1)}, u32[]{:S(2)}, u32[]{:S(2)}) collective-permute-start(bf16[112,256]{1,0:T(8,128)(2,1)S(1)} %get-tuple-element.95), channel_id=1, source_target_pairs={{0,16},{4,20},{8,24},{12,28},{16,0},{20,4},{24,8},{28,12},{1,17},{... | collective-permute-start | bytes 172040 | tf_op jit(solution)/shard_map/ppermute | solution.py:482
  49.6 6.0 %collective-permute-start.10 = (bf16[112,256]{1,0:T(8,128)(2,1)S(1)}, bf16[112,256]{1,0:T(8,128)(2,1)S(1)}, u32[]{:S(2)}, u32[]{:S(2)}) collective-permute-start(bf16[112,256]{1,0:T(8,128)(2,1)S(1)} %get-tuple-element.96), channel_id=1, source_target_pairs={{0,24},{4,28},{8,16},{12,20},{16,8},{20,12},{24,0},{28,4},{1,25},{... | collective-permute-start | bytes 172040 | tf_op jit(solution)/shard_map/ppermute | solution.py:482
  55.7 7.3 %collective-permute-start.13 = (bf16[192,256]{1,0:T(8,128)(2,1)S(1)}, bf16[192,256]{1,0:T(8,128)(2,1)S(1)}, u32[]{:S(2)}, u32[]{:S(2)}) collective-permute-start(bf16[192,256]{1,0:T(8,128)(2,1)S(1)} %pad_maximum_fusion.2), channel_id=1, source_target_pairs={{0,2},{1,3},{2,0},{3,1},{4,6},{5,7},{6,4},{7,5},{8,10},{9,11},{10,... | collective-permute-start | bytes 294920 | tf_op jit(solution)/shard_map/ppermute | solution.py:482
  56.2 5.0 %collective-permute-start.12 = (bf16[256,256]{1,0:T(8,128)(2,1)S(1)}, bf16[256,256]{1,0:T(8,128)(2,1)S(1)}, u32[]{:S(2)}, u32[]{:S(2)}) collective-permute-start(bf16[256,256]{1,0:T(8,128)(2,1)S(1)} %pad_maximum_fusion.1), channel_id=1, source_target_pairs={{0,4},{4,0},{8,12},{12,8},{16,20},{20,16},{24,28},{28,24},{1,5},{5... | collective-permute-start | bytes 393224 | tf_op jit(solution)/shard_map/ppermute | solution.py:482
  61.4 9.1 %collective-permute-start.16 = (bf16[464,256]{1,0:T(8,128)(2,1)S(1)}, bf16[464,256]{1,0:T(8,128)(2,1)S(1)}, u32[]{:S(2)}, u32[]{:S(2)}) collective-permute-start(bf16[464,256]{1,0:T(8,128)(2,1)S(1)} %get-tuple-element.141.refs_0_), channel_id=1, source_target_pairs={{0,2},{1,3},{2,0},{3,1},{4,6},{5,7},{6,4},{7,5},{8,10},{9,11},{10,... | collective-permute-start | bytes 712712 | tf_op jit(solution)/shard_map/ppermute | solution.py:482
  63.0 2.1 %collective-permute-start.14 = (bf16[464,256]{1,0:T(8,128)(2,1)S(1)}, bf16[464,256]{1,0:T(8,128)(2,1)S(1)}, u32[]{:S(2)}, u32[]{:S(2)}) collective-permute-start(bf16[464,256]{1,0:T(8,128)(2,1)S(1)} %get-tuple-element.141.refs_0_), channel_id=1, source_target_pairs={{0,1},{1,0},{2,3},{3,2},{4,5},{5,4},{6,7},{7,6},{8,9},{9,8},{10,11... | collective-permute-start | bytes 712712 | tf_op jit(solution)/shard_map/ppermute | solution.py:482
  63.0 2.0 %collective-permute-start.15 = (bf16[384,256]{1,0:T(8,128)(2,1)S(1)}, bf16[384,256]{1,0:T(8,128)(2,1)S(1)}, u32[]{:S(2)}, u32[]{:S(2)}) collective-permute-start(bf16[384,256]{1,0:T(8,128)(2,1)S(1)} %pad_maximum_fusion.refs_1_), channel_id=1, source_target_pairs={{0,1},{1,0},{2,3},{3,2},{4,5},{5,4},{6,7},{7,6},{8,9},{9,8},{10,11... | collective-permute-start | bytes 589832 | tf_op jit(solution)/shard_map/ppermute | solution.py:482
  63.6 6.9 %collective-permute-start.17 = (bf16[384,256]{1,0:T(8,128)(2,1)S(1)}, bf16[384,256]{1,0:T(8,128)(2,1)S(1)}, u32[]{:S(2)}, u32[]{:S(2)}) collective-permute-start(bf16[384,256]{1,0:T(8,128)(2,1)S(1)} %pad_maximum_fusion.refs_1_), channel_id=1, source_target_pairs={{0,4},{4,0},{8,12},{12,8},{16,20},{20,16},{24,28},{28,24},{1,5},{5... | collective-permute-start | bytes 589832 | tf_op jit(solution)/shard_map/ppermute | solution.py:482
  70.5 2.1 %collective-permute-start.18 = (bf16[464,256]{1,0:T(8,128)(2,1)S(1)}, bf16[464,256]{1,0:T(8,128)(2,1)S(1)}, u32[]{:S(2)}, u32[]{:S(2)}) collective-permute-start(bf16[464,256]{1,0:T(8,128)(2,1)S(1)} %collective-permute-done.16.refs_0_), channel_id=1, source_target_pairs={{0,1},{1,0},{2,3},{3,2},{4,5},{5,4},{6,7},{7,6},{8,9},{9,8},{10,11... | collective-permute-start | bytes 712712 | tf_op jit(solution)/shard_map/ppermute | solution.py:482
  70.5 2.2 %collective-permute-start.19 = (bf16[384,256]{1,0:T(8,128)(2,1)S(1)}, bf16[384,256]{1,0:T(8,128)(2,1)S(1)}, u32[]{:S(2)}, u32[]{:S(2)}) collective-permute-start(bf16[384,256]{1,0:T(8,128)(2,1)S(1)} %collective-permute-done.17.refs_1_), channel_id=1, source_target_pairs={{0,1},{1,0},{2,3},{3,2},{4,5},{5,4},{6,7},{7,6},{8,9},{9,8},{10,11... | collective-permute-start | bytes 589832 | tf_op jit(solution)/shard_map/ppermute | solution.py:482
